TPU v7x, 32 devices: a whole 2x2x4 slice. The times are simulated.
32 devices in a mesh: frames: 4 (over y, x), heads: 8 (over z, core).
Axes of the slice: x: 2, y: 2, z: 4, core: 2. Of those that a mesh axis runs over, the one named last changes fastest.
Arguments:
- block_input: bfloat16 [16, 256, 1024], P('frames'), may hold values from -6 to 6
- action_ids: int32 [16], P('frames'), may hold values from 0 to 7
- segment_ids: int32 [16], replicated, may hold values from 0 to 2, as said below
- action_table: bfloat16 [8, 1024], replicated, may hold values from -3 to 3
- norm_gain: float32 [3, 1024], replicated, may hold values from 0.5 to 1.5
- norm_shift: float32 [3, 1024], replicated, may hold values from -2 to 2
- spatial_qkv: bfloat16 [1024, 3, 1024], P(None, None, 'heads'), may hold values from -0.1875 to 0.1875
- spatial_out: bfloat16 [1024, 1024], P('heads'), may hold values from -0.75 to 0.75
- temporal_qkv: bfloat16 [1024, 3, 1024], P(None, None, 'heads'), may hold values from -0.1875 to 0.1875
- temporal_out: bfloat16 [1024, 1024], P('heads'), may hold values from -0.5 to 0.5
- out_bias: float32 [3, 1024], replicated, may hold values from -2 to 2
- up_weight: bfloat16 [1024, 4096], P(None, 'heads'), may hold values from -0.1875 to 0.1875
- up_bias: float32 [4096], P('heads'), may hold values from -2 to 2
- down_weight: bfloat16 [4096, 1024], P('heads'), may hold values from -0.375 to 0.375
- cotangent: bfloat16 [16, 256, 1024], P('frames'), may hold values from -6 to 6
Outputs:
- block_output: bfloat16 [16, 256, 1024], P('frames', 'heads')
- input_grad: float32 [16, 256, 1024], P('frames', 'heads')
- table_grad: float32 [8, 1024], replicated
- gain_grad: float32 [3, 1024], replicated
- shift_grad: float32 [3, 1024], replicated
- spatial_qkv_grad: float32 [1024, 3, 1024], P(None, None, 'heads')
- spatial_out_grad: float32 [1024, 1024], P('heads')
- temporal_qkv_grad: float32 [1024, 3, 1024], P(None, None, 'heads')
- temporal_out_grad: float32 [1024, 1024], P('heads')
- bias_grad: float32 [3, 1024], replicated
- up_grad: float32 [1024, 4096], P(None, 'heads')
- up_bias_grad: float32 [4096], P('heads')
- down_grad: float32 [4096, 1024], P('heads')
Inputs may be any that keep to these rules, and one draw needn't show every extreme that they name: `segment_ids`: clips are runs of consecutive frames whose numbers never fall; one clip starts within the first 4 frames and ends within the last 4 frames.
All inputs are finite; a program needn't handle non-finite values.
Results may differ from a plain program's by a relative error of at most 0.03.
Values may be sent and summed in bfloat16 or wider, within the bound.
A program may use at most 128 MiB of HBM per device.

v0:
```python
import jax
import jax.numpy as jnp
from jax import lax
from jax.sharding import PartitionSpec as P

HD = 64


HIGH = lax.Precision.HIGHEST


def layer_norm(value, gain, shift):
    centered = value - jnp.mean(value, axis=-1, keepdims=True)
    spread = jnp.mean(centered * centered, axis=-1, keepdims=True)
    return centered * lax.rsqrt(spread + 1e-05) * gain + shift


def smooth_act(value):
    return jax.nn.gelu(value, approximate=True)


def combine_heads(partial_value):
    return lax.psum(partial_value.astype(jnp.bfloat16), "heads").astype(jnp.float32)


def take_share(value):
    share = value.shape[1] // lax.axis_size("heads")
    return lax.dynamic_slice_in_dim(value, lax.axis_index("heads") * share, share, 1)


def own_share(value):
    return take_share(value)


def heads_total(table_part, gain_part, shift_part, bias_part):
    return (table_part, gain_part, shift_part, bias_part)


def attend(query, key, value, allowed, scale):
    scores = jnp.einsum("bqhe,bkhe->bhqk", query, key, preferred_element_type=jnp.float32) * scale
    if allowed is not None:
        scores = jnp.where(allowed, scores, -1000000000.0)
    top = jnp.max(scores, axis=-1, keepdims=True)
    total = jnp.sum(jnp.exp(scores - top), axis=-1, keepdims=True)
    log_total = top + jnp.log(total)
    weights = jnp.exp(scores - log_total).astype(jnp.bfloat16)
    mixed = jnp.einsum("bhqk,bkhe->bqhe", weights, value, preferred_element_type=jnp.float32)
    return (mixed.astype(jnp.bfloat16), log_total)


def attend_back(query, key, value, allowed, scale, log_total, mixed_grad):
    scores = jnp.einsum("bqhe,bkhe->bhqk", query, key, preferred_element_type=jnp.float32) * scale
    if allowed is not None:
        scores = jnp.where(allowed, scores, -1000000000.0)
    probs = jnp.exp(scores - log_total)
    weights = probs.astype(jnp.bfloat16)
    value_grad = jnp.einsum(
        "bhqk,bqhe->bkhe", weights, mixed_grad, preferred_element_type=jnp.float32
    )
    weights_grad = jnp.einsum(
        "bqhe,bkhe->bhqk", mixed_grad, value, preferred_element_type=jnp.float32
    )
    inner = jnp.sum(weights_grad * probs, axis=-1, keepdims=True)
    scores_grad = (probs * (weights_grad - inner)).astype(jnp.bfloat16)
    query_grad = (
        jnp.einsum("bhqk,bkhe->bqhe", scores_grad, key, preferred_element_type=jnp.float32) * scale
    )
    key_grad = (
        jnp.einsum("bhqk,bqhe->bkhe", scores_grad, query, preferred_element_type=jnp.float32)
        * scale
    )
    return (
        query_grad.astype(jnp.bfloat16),
        key_grad.astype(jnp.bfloat16),
        value_grad.astype(jnp.bfloat16),
    )


def on_device(
    block_input,
    action_ids,
    segment_ids,
    action_table,
    norm_gain,
    norm_shift,
    spatial_qkv,
    spatial_out,
    temporal_qkv,
    temporal_out,
    out_bias,
    up_weight,
    up_bias,
    down_weight,
    cotangent,
):
    frames_local, patches, width = block_input.shape
    heads_local = spatial_out.shape[0] // HD
    scale = HD ** (-0.5)
    actions = action_table.shape[0]
    total_frames = segment_ids.shape[0]
    picker = (
        action_ids[:, None] == lax.broadcasted_iota(jnp.int32, (frames_local, actions), 1)
    ).astype(jnp.float32)
    added = jnp.dot(picker, action_table.astype(jnp.float32), precision=HIGH)
    whole0 = block_input.astype(jnp.float32) + added[:, None, :]
    normed1 = layer_norm(whole0, norm_gain[0], norm_shift[0]).astype(jnp.bfloat16)
    s_heads = spatial_out.reshape(heads_local, HD, width)
    s_proj = jnp.einsum("fsd,dch->cfsh", normed1, spatial_qkv, preferred_element_type=jnp.float32)
    s_proj = s_proj.astype(jnp.bfloat16).reshape(3, frames_local, patches, heads_local, HD)
    s_mixed, s_lse = attend(s_proj[0], s_proj[1], s_proj[2], None, scale)
    s_part = jnp.einsum("fshe,hed->fsd", s_mixed, s_heads, preferred_element_type=jnp.float32)
    state1 = whole0 + combine_heads(s_part) + out_bias[0]
    pos1 = lax.all_to_all(
        state1.astype(jnp.bfloat16), "frames", split_axis=1, concat_axis=0, tiled=True
    ).astype(state1.dtype)
    normed2 = layer_norm(pos1, norm_gain[1], norm_shift[1]).astype(jnp.bfloat16)
    places = normed2.shape[1]
    t_heads = temporal_out.reshape(heads_local, HD, width)
    t_proj = jnp.einsum("fpd,dch->cpfh", normed2, temporal_qkv, preferred_element_type=jnp.float32)
    t_proj = t_proj.astype(jnp.bfloat16).reshape(3, places, total_frames, heads_local, HD)
    query_ids = lax.broadcasted_iota(jnp.int32, (total_frames, total_frames), 0)
    key_ids = lax.broadcasted_iota(jnp.int32, (total_frames, total_frames), 1)
    allowed = (key_ids <= query_ids) & (segment_ids[:, None] == segment_ids[None, :])
    t_mixed, t_lse = attend(t_proj[0], t_proj[1], t_proj[2], allowed, scale)
    t_part = jnp.einsum("pfhe,hed->fpd", t_mixed, t_heads, preferred_element_type=jnp.float32)
    pos2 = pos1 + combine_heads(t_part) + out_bias[1]
    state2 = lax.all_to_all(
        pos2.astype(jnp.bfloat16), "frames", split_axis=0, concat_axis=1, tiled=True
    ).astype(pos2.dtype)
    normed3 = layer_norm(state2, norm_gain[2], norm_shift[2]).astype(jnp.bfloat16)
    pre = (
        jnp.einsum("fsd,dk->fsk", normed3, up_weight, preferred_element_type=jnp.float32) + up_bias
    )
    hidden = smooth_act(pre).astype(jnp.bfloat16)
    f_part = jnp.einsum("fsk,kd->fsd", hidden, down_weight, preferred_element_type=jnp.float32)
    state3 = state2 + combine_heads(f_part) + out_bias[2]
    grad3 = cotangent.astype(jnp.float32)
    g_down = jnp.einsum("fsk,fsd->kd", hidden, cotangent, preferred_element_type=jnp.float32)
    d_hidden = jnp.einsum("fsd,kd->fsk", cotangent, down_weight, preferred_element_type=jnp.float32)
    d_pre = jax.vjp(smooth_act, pre)[1](d_hidden)[0].astype(jnp.bfloat16)
    g_up_bias = jnp.sum(d_pre.astype(jnp.float32), axis=(0, 1))
    g_up = jnp.einsum("fsd,fsk->dk", normed3, d_pre, preferred_element_type=jnp.float32)
    d_norm3 = combine_heads(
        jnp.einsum("fsk,dk->fsd", d_pre, up_weight, preferred_element_type=jnp.float32)
    )
    back3 = jax.vjp(layer_norm, state2, norm_gain[2], norm_shift[2])[1](d_norm3)
    grad2 = grad3 + back3[0]
    pos_grad2 = lax.all_to_all(
        grad2.astype(jnp.bfloat16), "frames", split_axis=1, concat_axis=0, tiled=True
    ).astype(grad2.dtype)
    t_branch = pos_grad2.astype(jnp.bfloat16)
    g_t_out = jnp.einsum("pfhe,fpd->hed", t_mixed, t_branch, preferred_element_type=jnp.float32)
    d_tmixed = jnp.einsum(
        "fpd,hed->pfhe", t_branch, t_heads, preferred_element_type=jnp.float32
    ).astype(jnp.bfloat16)
    t_qg, t_kg, t_vg = attend_back(t_proj[0], t_proj[1], t_proj[2], allowed, scale, t_lse, d_tmixed)
    d_tproj = jnp.stack([t_qg, t_kg, t_vg]).reshape(3, places, total_frames, heads_local * HD)
    g_t_qkv = jnp.einsum("fpd,cpfh->dch", normed2, d_tproj, preferred_element_type=jnp.float32)
    d_norm2 = combine_heads(
        jnp.einsum("cpfh,dch->fpd", d_tproj, temporal_qkv, preferred_element_type=jnp.float32)
    )
    back2 = jax.vjp(layer_norm, pos1, norm_gain[1], norm_shift[1])[1](d_norm2)
    pos_grad1 = pos_grad2 + back2[0]
    grad1 = lax.all_to_all(
        pos_grad1.astype(jnp.bfloat16), "frames", split_axis=0, concat_axis=1, tiled=True
    ).astype(pos_grad1.dtype)
    s_branch = grad1.astype(jnp.bfloat16)
    g_s_out = jnp.einsum("fshe,fsd->hed", s_mixed, s_branch, preferred_element_type=jnp.float32)
    d_smixed = jnp.einsum(
        "fsd,hed->fshe", s_branch, s_heads, preferred_element_type=jnp.float32
    ).astype(jnp.bfloat16)
    s_qg, s_kg, s_vg = attend_back(s_proj[0], s_proj[1], s_proj[2], None, scale, s_lse, d_smixed)
    d_sproj = jnp.stack([s_qg, s_kg, s_vg]).reshape(3, frames_local, patches, heads_local * HD)
    g_s_qkv = jnp.einsum("fsd,cfsh->dch", normed1, d_sproj, preferred_element_type=jnp.float32)
    d_norm1 = combine_heads(
        jnp.einsum("cfsh,dch->fsd", d_sproj, spatial_qkv, preferred_element_type=jnp.float32)
    )
    back1 = jax.vjp(layer_norm, whole0, norm_gain[0], norm_shift[0])[1](d_norm1)
    grad0 = grad1 + back1[0]
    table_part = jnp.einsum("fa,fd->ad", picker, jnp.sum(grad0, axis=1), precision=HIGH)
    gain_part = jnp.stack([back1[1], back2[1], back3[1]])
    shift_part = jnp.stack([back1[2], back2[2], back3[2]])
    bias_part = jnp.stack(
        [jnp.sum(grad1, axis=(0, 1)), jnp.sum(pos_grad2, axis=(0, 1)), jnp.sum(grad3, axis=(0, 1))]
    )
    table_part, gain_part, shift_part, bias_part = heads_total(
        table_part, gain_part, shift_part, bias_part
    )
    g_s_out = g_s_out.reshape(heads_local * HD, width)
    g_t_out = g_t_out.reshape(heads_local * HD, width)
    summed = (
        lax.psum(table_part.astype(jnp.bfloat16), "frames").astype(jnp.float32),
        lax.psum(gain_part.astype(jnp.bfloat16), "frames").astype(jnp.float32),
        lax.psum(shift_part.astype(jnp.bfloat16), "frames").astype(jnp.float32),
        lax.psum(g_s_qkv.astype(jnp.bfloat16), "frames").astype(jnp.float32),
        lax.psum(g_s_out.astype(jnp.bfloat16), "frames").astype(jnp.float32),
        lax.psum(g_t_qkv.astype(jnp.bfloat16), "frames").astype(jnp.float32),
        lax.psum(g_t_out.astype(jnp.bfloat16), "frames").astype(jnp.float32),
        lax.psum(bias_part.astype(jnp.bfloat16), "frames").astype(jnp.float32),
        lax.psum(g_up.astype(jnp.bfloat16), "frames").astype(jnp.float32),
        lax.psum(g_up_bias.astype(jnp.bfloat16), "frames").astype(jnp.float32),
        lax.psum(g_down.astype(jnp.bfloat16), "frames").astype(jnp.float32),
    )
    return (
        own_share(state3).astype(jnp.bfloat16),
        own_share(grad0),
        summed[0],
        summed[1],
        summed[2],
        summed[3],
        summed[4],
        summed[5],
        summed[6],
        summed[7],
        summed[8],
        summed[9],
        summed[10],
    )


def solution(mesh):
    return jax.shard_map(
        on_device,
        mesh=mesh,
        in_specs=(
            P("frames", None, None),
            P("frames"),
            P(),
            P(),
            P(),
            P(),
            P(None, None, "heads"),
            P("heads", None),
            P(None, None, "heads"),
            P("heads", None),
            P(),
            P(None, "heads"),
            P("heads"),
            P("heads", None),
            P("frames", None, None),
        ),
        out_specs=(
            P("frames", "heads", None),
            P("frames", "heads", None),
            P(),
            P(),
            P(),
            P(None, None, "heads"),
            P("heads", None),
            P(None, None, "heads"),
            P("heads", None),
            P(),
            P(None, "heads"),
            P("heads"),
            P("heads", None),
        ),
        check_vma=False,
    )
```

profile of v0, /device:TPU:0, one launch (start us, length us, event | category | flops | bytes accessed | tf_op | source)
XLA Modules:
  0.0 788.4 jit_solution(17351148440196956018)
XLA Ops:
  23.0 67.2 %all-reduce.10.cloned.1.call-done = bf16[4,256,1024]{2,1,0:T(8,128)(2,1)} async-done(((bf16[4,256,1024]{2,1,0:T(8,128)(2,1)}), bf16[4,256,1024]{2,1,0:T(8,128)(2,1)}) %all-reduce.10.cloned.1.call-update) | async-done | bytes 2097168 | tf_op jit(solution)/shard_map/psum | solution.py:23
  90.2 2.7 add_convert_fusion.5
  92.9 2.9 copy.214
  95.9 4.5 all-to-all-start
  100.6 23.5 %all-to-all-done = bf16[4,256,1024]{2,0,1:T(4,128)(2,1)} async-done(((bf16[4,256,1024]{2,0,1:T(4,128)(2,1)}), bf16[4,256,1024]{2,0,1:T(4,128)(2,1)}, u32[]{:S(2)}, u32[]{:S(2)}) %all-to-all-start) | async-done | bytes 2097184 | tf_op jit(solution)/shard_map/all_to_all | solution.py:113
  124.1 2.8 bitcast_convert_fusion.9
  129.2 2.4 copy.348
  134.0 4.7 copy.216
  138.7 5.5 reshape.240
  144.4 3.0 fusion.96
  163.4 63.1 %all-reduce.12.cloned.1.call-done = bf16[16,64,1024]{2,0,1:T(8,128)(2,1)} async-done(((bf16[16,64,1024]{2,0,1:T(8,128)(2,1)}), bf16[16,64,1024]{2,0,1:T(8,128)(2,1)}) %all-reduce.12.cloned.1.call-update) | async-done | bytes 2097168 | tf_op jit(solution)/shard_map/psum | solution.py:23
  226.4 3.6 add_convert_fusion.3
  231.2 27.8 %all_to_all.54 = bf16[16,64,1024]{2,1,0:T(8,128)(2,1)S(1)} all-to-all(bf16[16,64,1024]{2,1,0:T(8,128)(2,1)S(1)} %copy.226), channel_id=1, replica_groups=mesh['frames'=4,'heads'=8] {'frames'}, dimensions={0} | all-to-all | bytes 4194304 | tf_op jit(solution)/shard_map/all_to_all | solution.py:127
  261.4 3.5 fusion.109
  269.9 7.0 copy.347
  278.2 7.1 multiply_reduce_fusion
  289.6 4.7 copy.228
  297.5 3.1 fusion.117
  301.5 2.6 convolution_convert_fusion
  304.2 62.5 %all-reduce.14.cloned.1.call-done = bf16[4,256,1024]{2,1,0:T(8,128)(2,1)} async-done(((bf16[4,256,1024]{2,1,0:T(8,128)(2,1)}), bf16[4,256,1024]{2,1,0:T(8,128)(2,1)}) %all-reduce.14.cloned.1.call-update) | async-done | bytes 2097168 | tf_op jit(solution)/shard_map/psum | solution.py:23
  366.7 3.8 fusion.8
  371.5 3.1 fusion.9
  378.2 27.8 %all_to_all.55 = bf16[4,256,1024]{2,0,1:T(4,128)(2,1)S(1)} all-to-all(bf16[4,256,1024]{2,0,1:T(4,128)(2,1)S(1)} %copy.234), channel_id=1, replica_groups=mesh['frames'=4,'heads'=8] {'frames'}, dimensions={1} | all-to-all | bytes 4194304 | tf_op jit(solution)/shard_map/all_to_all | solution.py:148
  407.3 2.6 copy.349
  409.8 4.0 all_to_all.45
  413.8 4.1 fusion.54
  434.3 4.0 fusion.33
  442.7 58.2 %all-reduce.16.cloned.1.call-done = bf16[16,64,1024]{2,0,1:T(8,128)(2,1)} async-done(((bf16[16,64,1024]{2,0,1:T(8,128)(2,1)}), bf16[16,64,1024]{2,0,1:T(8,128)(2,1)}) %all-reduce.16.cloned.1.call-update) | async-done | bytes 2097168 | tf_op jit(solution)/shard_map/psum | solution.py:23
  500.9 3.6 fusion.7
  504.8 4.7 fusion.10
  512.2 4.5 add_convert_fusion
  516.7 2.5 copy.253
  519.2 4.5 all-to-all-start.3
  523.8 4.6 convolution_convert_fusion.1
  528.4 2.5 bitcast_convert_fusion.4
  531.1 2.6 bitcast_convert_fusion.5
  533.7 3.2 fusion.62
  536.8 10.6 %all-to-all-done.3 = bf16[16,64,1024]{2,1,0:T(8,128)(2,1)} async-done(((bf16[16,64,1024]{2,1,0:T(8,128)(2,1)}), bf16[16,64,1024]{2,1,0:T(8,128)(2,1)}, u32[]{:S(2)}, u32[]{:S(2)}) %all-to-all-start.3) | async-done | bytes 2097184 | tf_op jit(solution)/shard_map/all_to_all | solution.py:164
  559.6 4.0 bitcast_convert_fusion
  564.0 4.7 bitcast_convert_fusion.6
  569.9 2.4 bitcast_convert_fusion.7
  576.3 2.5 reduce.11
  582.9 75.8 %all-reduce.18.cloned.1.call-done = (bf16[4,256,1024]{2,1,0:T(8,128)(2,1)}, bf16[4,256,1024]{2,1,0:T(8,128)(2,1)}) async-done(((bf16[4,256,1024]{2,1,0:T(8,128)(2,1)}, bf16[4,256,1024]{2,1,0:T(8,128)(2,1)}), (bf16[4,256,1024]{2,1,0:T(8,128)(2,1)}, bf16[4,256,1024]{2,1,0:T(8,128)(2,1)})) %all-reduce.18.cloned.1.call-update) | async-done | bytes 4194320 | tf_op jit(solution)/shard_map/psum | solution.py:23
  660.7 2.9 fusion.6
  663.6 2.8 fusion.11
  666.5 3.7 fusion.110
  670.5 18.1 %all-reduce.1 = (bf16[8,1024]{1,0:T(8,128)(2,1)S(1)}, bf16[3,1024]{1,0:T(4,128)(2,1)S(1)}, bf16[3,1024]{1,0:T(4,128)(2,1)S(1)}, bf16[3,1024]{1,0:T(4,128)(2,1)S(1)}, bf16[512]{0:T(512)(128)(2,1)S(1)}) all-reduce(bf16[8,1024]{1,0:T(8,128)(2,1)S(1)} %convolution_convert_fusion.8, ...), channel_id=1, replica_groups=mesh['frames'=4,'heads'=8] {'frames'}, use_global_device_ids=true, to_apply=%region_25.26 | all-reduce | flops 17920 | bytes 71680 | tf_op jit(solution)/shard_map/psum | solution.py:192
  693.9 76.8 %all-reduce.20.cloned.1.call-done = (bf16[1024,3,128]{2,0,1:T(8,128)(2,1)}, bf16[128,1024]{1,0:T(8,128)(2,1)}, bf16[1024,3,128]{2,0,1:T(8,128)(2,1)}, bf16[128,1...) async-done(((bf16[1024,3,128]{2,0,1:T(8,128)(2,1)}, bf16[128,1024]{1,0:T(8,128)(2,1)}, bf16[1024,3,128]{2,0,1:T(8,128)(2,1)}, ...) | async-done | bytes 4194320 | tf_op jit(solution)/shard_map/psum | solution.py:195
  (307 shorter events, 124.5 us)
Async XLA Ops:
  7.2 289.3 %copy-start = (bf16[512,1024]{1,0:T(8,128)(2,1)S(1)}, bf16[512,1024]{1,0:T(8,128)(2,1)}, u32[]{:S(2)}) copy-start(bf16[512,1024]{1,0:T(8,128)(2,1)} %param.28) | copy-start | bytes 3145732
  7.2 8.5 %copy-start.2 = (bf16[4,256,1024]{2,1,0:T(8,128)(2,1)S(1)}, bf16[4,256,1024]{2,1,0:T(8,128)(2,1)}, u32[]{:S(2)}) copy-start(bf16[4,256,1024]{2,1,0:T(8,128)(2,1)} %param.15) | copy-start | bytes 6291460
  7.2 83.0 %all-reduce.10.cloned.1.call-start = ((), (), s32[]{:S(2)}) async-start(), calls=%async_computation.4 | async-start | bytes 4194304 | tf_op jit(solution)/shard_map/psum | solution.py:23
  7.3 8.4 %copy-start.83 = (bf16[1024,3,128]{2,0,1:T(8,128)(2,1)S(1)}, bf16[1024,3,128]{2,0,1:T(8,128)(2,1)}, u32[]{:S(2)}) copy-start(bf16[1024,3,128]{2,0,1:T(8,128)(2,1)} %param.21) | copy-start | bytes 2359300
  8.8 8.4 %copy-start.53 = (f32[1,1024]{1,0:T(1,128)}, f32[1,1024]{1,0:T(1,128)S(1)}, u32[]{:S(2)}) copy-start(f32[1,1024]{1,0:T(1,128)S(1)} %get-tuple-element.41) | copy-start | bytes 12292
  8.8 135.6 %copy-start.45 = (f32[1,1024]{1,0:T(1,128)}, f32[1,1024]{1,0:T(1,128)S(1)}, u32[]{:S(2)}) copy-start(f32[1,1024]{1,0:T(1,128)S(1)} %get-tuple-element.42) | copy-start | bytes 12292
  10.2 6.9 copy-start.75
  10.2 134.2 %copy-start.70 = (f32[1,1024]{1,0:T(1,128)}, f32[1,1024]{1,0:T(1,128)S(1)}, u32[]{:S(2)}) copy-start(f32[1,1024]{1,0:T(1,128)S(1)} %get-tuple-element.45) | copy-start | bytes 12292
  18.9 74.0 %copy-start.43 = (f32[1,8,256]{2,1,0:T(8,128)}, f32[1,8,256]{2,1,0:T(8,128)S(1)}, u32[]{:S(2)}) copy-start(f32[1,8,256]{2,1,0:T(8,128)S(1)} %log_add_fusion.1) | copy-start | bytes 24580
  92.9 7.7 copy-start.79
  95.9 28.3 %all-to-all-start = ((bf16[4,256,1024]{2,0,1:T(4,128)(2,1)}), bf16[4,256,1024]{2,0,1:T(4,128)(2,1)}, u32[]{:S(2)}, u32[]{:S(2)}) async-start(bf16[4,256,1024]{2,0,1:T(4,128)(2,1)} %copy.214), calls=%async_computation | async-start | bytes 4194304 | tf_op jit(solution)/shard_map/all_to_all | solution.py:113
  100.3 126.1 %all-reduce.12.cloned.1.call-start = ((), (), s32[]{:S(2)}) async-start(), calls=%async_computation.5 | async-start | bytes 4194304 | tf_op jit(solution)/shard_map/psum | solution.py:23
  155.7 5.5 copy-start.42
  163.3 203.4 %all-reduce.14.cloned.1.call-start = ((), (), s32[]{:S(2)}) async-start(), calls=%async_computation.6 | async-start | bytes 4194304 | tf_op jit(solution)/shard_map/psum | solution.py:23
  289.6 4.7 copy-start.68
  289.6 4.8 copy-start.55
  289.6 4.8 copy-start.58
  289.6 4.8 copy-start.77
  289.6 4.8 copy-start.81
  304.1 196.8 %all-reduce.16.cloned.1.call-start = ((), (), s32[]{:S(2)}) async-start(), calls=%async_computation.7 | async-start | bytes 4194304 | tf_op jit(solution)/shard_map/psum | solution.py:23
  366.7 4.7 copy-start.6
  366.7 4.7 copy-start.12
  366.7 4.7 copy-start.56
  366.7 4.7 copy-start.59
  366.7 4.7 copy-start.64
  413.8 4.7 copy-start.21
  434.3 66.6 %copy-start.46 = (f32[1,1024]{1,0:T(1,128)S(1)}, f32[1,1024]{1,0:T(1,128)}, u32[]{:S(2)}) copy-start(f32[1,1024]{1,0:T(1,128)} %copy-done.45) | copy-start | bytes 12292
  438.3 66.3 %copy-start.51 = (f32[4,4,64]{2,1,0:T(4,128)S(1)}, f32[4,4,64]{2,1,0:T(4,128)}, u32[]{:S(2)}) copy-start(f32[4,4,64]{2,1,0:T(4,128)} %copy-done.50) | copy-start | bytes 12292
  516.6 7.1 copy-start.85
  519.2 28.2 %all-to-all-start.3 = ((bf16[16,64,1024]{2,1,0:T(8,128)(2,1)}), bf16[16,64,1024]{2,1,0:T(8,128)(2,1)}, u32[]{:S(2)}, u32[]{:S(2)}) async-start(bf16[16,64,1024]{2,1,0:T(8,128)(2,1)} %copy.253), calls=%async_computation.3 | async-start | bytes 4194304 | tf_op jit(solution)/shard_map/all_to_all | solution.py:164
  523.7 135.1 %all-reduce.18.cloned.1.call-start = ((), (), s32[]{:S(2)}) async-start(), calls=%async_computation.8 | async-start | bytes 8388608 | tf_op jit(solution)/shard_map/psum | solution.py:23
  533.7 15.8 %copy-start.35 = (bf16[128,1024]{1,0:T(8,128)(2,1)S(1)}, bf16[128,1024]{1,0:T(8,128)(2,1)}, u32[]{:S(2)}) copy-start(bf16[128,1024]{1,0:T(8,128)(2,1)} %param.22) | copy-start | bytes 786436
  536.8 13.4 %copy-start.44 = (f32[1,8,256]{2,1,0:T(8,128)S(1)}, f32[1,8,256]{2,1,0:T(8,128)}, u32[]{:S(2)}) copy-start(f32[1,8,256]{2,1,0:T(8,128)} %copy-done.43) | copy-start | bytes 24580
  563.6 6.3 copy-start.49
  563.6 6.3 copy-start.54
  563.6 6.3 copy-start.62
  563.6 6.2 copy-start.76
  563.6 207.1 %all-reduce.20.cloned.1.call-start = ((), (), s32[]{:S(2)}) async-start(), calls=%async_computation.9 | async-start | bytes 8388608 | tf_op jit(solution)/shard_map/psum | solution.py:195
  563.9 4.7 copy-start.10
  563.9 5.9 copy-start.40
  564.0 5.9 copy-start.41
  572.3 8.6 %copy-start.74 = (bf16[1024]{0:T(1024)(128)(2,1)S(1)}, bf16[1024]{0:T(1024)(128)(2,1)}, u32[]{:S(2)}) copy-start(bf16[1024]{0:T(1024)(128)(2,1)} %get-tuple-element.13) | copy-start | bytes 6148
  580.9 82.7 %copy-start.67 = (f32[4,256]{1,0:T(4,128)S(1)}, f32[4,256]{1,0:T(4,128)}, u32[]{:S(2)}) copy-start(f32[4,256]{1,0:T(4,128)} %copy-done.66) | copy-start | bytes 12292
  660.7 5.7 copy-start.11
  666.5 25.2 %copy-start.69 = (f32[1,1024]{1,0:T(1,128)S(1)}, f32[1,1024]{1,0:T(1,128)}, u32[]{:S(2)}) copy-start(f32[1,1024]{1,0:T(1,128)} %get-tuple-element.46) | copy-start | bytes 12292
  770.7 6.2 copy-start.36
  770.7 7.4 copy-start.32
  772.6 7.1 copy-start.31
  (51 other events, 141.4 us)
Sparse Core Ops, SparseCore 0:
  22.5 67.6 all-reduce.9
  163.4 62.9 all-reduce.11
  304.2 62.4 all-reduce.13
  438.4 62.4 all-reduce.15
  563.7 94.9 all-reduce.17
  663.4 107.2 all-reduce.19
where the time goes:
time: 796 us; the launch traced here: 788 us
  waiting for transfers between devices  438 us (55%)
  other arithmetic  96.9 us (12%)
  local copies, waits for them, and re-layouts  93 us (12%)
  blocking collectives  73.7 us (9%)
  matrix products  61.9 us (8%)
  between operations  15.5 us (2%)
  starting transfers between devices  9.56 us (1%)
    psum x5, waiting for transfers between devices, combine_heads(): lax.psum(partial_value.astype(jnp.bfloat16), 'heads').astype(jnp.float32)  327 us
    psum x1, waiting for transfers between devices, on_device(): lax.psum(g_s_qkv.astype(jnp.bfloat16), 'frames').astype(jnp.float32)  76.8 us
    all_to_all x1, blocking collectives, on_device(): lax.all_to_all(pos2.astype(jnp.bfloat16), 'frames', split_axis=0, concat_...  27.8 us
    all_to_all x1, blocking collectives, on_device(): lax.all_to_all(grad2.astype(jnp.bfloat16), 'frames', split_axis=1, concat...  27.8 us
    reduce_sum x9, other arithmetic, layer_norm(): return centered * lax.rsqrt(spread + 1e-05) * gain + shift  26.8 us
    all_to_all x1, waiting for transfers between devices, on_device(): lax.all_to_all(state1.astype(jnp.bfloat16), 'frames', split_axis=1, conca...  23.5 us
    psum x1, blocking collectives, on_device(): lax.psum(table_part.astype(jnp.bfloat16), 'frames').astype(jnp.float32)  18.1 us
  transfers between devices with their start and end apart: 8, of which 8 were waited for; matrix products, arithmetic and copies ran while one was open for 7% of the time, Pallas kernels for 0%

commit v1 on v0

v1 whole, which is shorter than its diff:
```python
import jax
import jax.numpy as jnp
import numpy as np
from jax import lax
from jax.experimental import pallas as pl
from jax.experimental.pallas import tpu as pltpu
from jax.sharding import PartitionSpec as P

HD = 64
SCALE = HD**-0.5
EPS = 1e-05
MASKED = -1000000000.0
F32 = jnp.float32
BF16 = jnp.bfloat16
MESH = pl.DeviceIdType.MESH
VMEM_LIMIT = 56 * 1024 * 1024
GELU_C = float(np.sqrt(2.0 / np.pi))
LAG = 2
LEAD = 3


def mm(a, b):
    return lax.dot_general(a, b, (((1,), (0,)), ((), ())), preferred_element_type=F32)


def mm_nt(a, b):
    return lax.dot_general(a, b, (((1,), (1,)), ((), ())), preferred_element_type=F32)


def mm_tn(a, b):
    return lax.dot_general(a, b, (((0,), (0,)), ((), ())), preferred_element_type=F32)


def norm_stats(value):
    centered = value - jnp.mean(value, axis=-1, keepdims=True)
    inv = lax.rsqrt(jnp.mean(centered * centered, axis=-1, keepdims=True) + EPS)
    return centered * inv, inv


def norm_back(value, grad, gain):
    normed, inv = norm_stats(value)
    e = grad * gain
    first = jnp.mean(e, axis=-1, keepdims=True)
    second = jnp.mean(e * normed, axis=-1, keepdims=True)
    gain_grad = jnp.sum(grad * normed, axis=0, keepdims=True)
    shift_grad = jnp.sum(grad, axis=0, keepdims=True)
    return (e - first - normed * second) * inv, gain_grad, shift_grad


def head_lanes(shape, head):
    lane = lax.broadcasted_iota(jnp.int32, shape, 1)
    return (lane >= head * HD) & (lane < (head + 1) * HD)


def softmax_of(q, k, mask):
    scores = mm_nt(q, k) * SCALE
    if mask is not None:
        scores = jnp.where(mask, scores, MASKED)
    raised = jnp.exp(scores - jnp.max(scores, axis=-1, keepdims=True))
    return raised / jnp.sum(raised, axis=-1, keepdims=True)


def attend(q, k, v, mask):
    heads = q.shape[1] // HD
    mixed = None
    for head in range(heads):
        lanes = head_lanes(q.shape, head)
        probs = softmax_of(jnp.where(lanes, q, jnp.zeros_like(q)), k, mask).astype(BF16)
        out = mm(probs, v)
        mixed = out if mixed is None else jnp.where(lanes, out, mixed)
    return mixed.astype(BF16)


def attend_back(q, k, v, mask, grad):
    heads = q.shape[1] // HD
    dq = dk = dv = None
    for head in range(heads):
        lanes = head_lanes(q.shape, head)
        qh = jnp.where(lanes, q, jnp.zeros_like(q))
        gh = jnp.where(lanes, grad, jnp.zeros_like(grad))
        probs = softmax_of(qh, k, mask)
        dvh = mm_tn(probs.astype(BF16), gh)
        dp = mm_nt(gh, v)
        ds = (probs * (dp - jnp.sum(dp * probs, axis=-1, keepdims=True))).astype(BF16)
        dqh = mm(ds, k) * SCALE
        dkh = mm_tn(ds, qh) * SCALE
        if head == 0:
            dq, dk, dv = dqh, dkh, dvh
        else:
            dq = jnp.where(lanes, dqh, dq)
            dk = dk + dkh
            dv = dv + dvh
    return dq.astype(BF16), dk.astype(BF16), dv.astype(BF16)


class Line:
    def __init__(self, sems, steps):
        self.frames = lax.axis_size("frames")
        self.heads = lax.axis_size("heads")
        self.chips = self.heads // 2
        self.f = lax.axis_index("frames")
        self.h = lax.axis_index("heads")
        self.z = self.h // 2
        self.c = self.h % 2
        self.steps = steps
        self.sems = sems

    def at(self, z):
        return (self.f, jnp.clip(z, 0, self.chips - 1) * 2 + self.c)

    def sibling(self):
        return (self.f, self.z * 2 + 1 - self.c)

    def barrier(self, over_frames, whole_line=False):
        sem = pltpu.get_barrier_semaphore()

        def greet(device):
            pl.semaphore_signal(sem, inc=1, device_id=device, device_id_type=MESH)

        greet(self.sibling())
        count = 1
        if over_frames:
            for k in range(1, self.frames):
                greet(((self.f + k) % self.frames, self.h))
            count += self.frames - 1
        if whole_line:
            for k in range(1, self.chips):
                greet(self.at((self.z + k) % self.chips))
            count += self.chips - 1
        else:

            @pl.when(self.z > 0)
            def _():
                greet(self.at(self.z - 1))

            @pl.when(self.z < self.chips - 1)
            def _():
                greet(self.at(self.z + 1))

            count = count + (self.z > 0).astype(jnp.int32)
            count = count + (self.z < self.chips - 1).astype(jnp.int32)
        pl.semaphore_wait(sem, count)

    def copy(self, src, dst, send, recv, device):
        return pltpu.make_async_remote_copy(
            src_ref=src,
            dst_ref=dst,
            send_sem=send,
            recv_sem=recv,
            device_id=device,
            device_id_type=MESH,
        )


class Gather:
    def __init__(self, line, buf, sems):
        self.line, self.buf = line, buf
        self.got, self.got_sib, self.sent_up, self.sent_down, self.sent_sib = sems

    def up(self, s, zb):
        ln = self.line
        ref = self.buf.at[s, zb, ln.c]
        return ln.copy(ref, ref, self.sent_up.at[s, zb], self.got.at[s, zb], ln.at(ln.z + 1))

    def down(self, s, zb):
        ln = self.line
        ref = self.buf.at[s, zb, ln.c]
        return ln.copy(ref, ref, self.sent_down.at[s, zb], self.got.at[s, zb], ln.at(ln.z - 1))

    def across(self, s, zb):
        ln = self.line
        ref = self.buf.at[s, zb, ln.c]
        return ln.copy(ref, ref, self.sent_sib.at[s, zb], self.got_sib.at[s, zb], ln.sibling())

    def wait_across(self, s, zb):
        ln = self.line
        ref = self.buf.at[s, zb, 1 - ln.c]
        ln.copy(
            ref, ref, self.sent_sib.at[s, zb], self.got_sib.at[s, zb], ln.sibling()
        ).wait_recv()

    def start(self, own):
        ln = self.line
        for s in range(ln.steps):
            self.buf[s, ln.z, ln.c] = own[s]

            @pl.when(ln.z < ln.chips - 1)
            def _():
                self.up(s, ln.z).start()

            @pl.when(ln.z > 0)
            def _():
                self.down(s, ln.z).start()

            self.across(s, ln.z).start()

    def arrive(self, distance, s):
        ln = self.line
        below, above = ln.z - distance, ln.z + distance

        @pl.when((distance > 0) & (below >= 0))
        def _():
            self.up(s, below).wait_recv()

            @pl.when(ln.z < ln.chips - 1)
            def _():
                self.up(s, below).start()

            self.across(s, below).start()

        @pl.when((distance > 0) & (above < ln.chips))
        def _():
            self.down(s, above).wait_recv()

            @pl.when(ln.z > 0)
            def _():
                self.down(s, above).start()

            self.across(s, above).start()

    def drain(self, s, zb):
        ln = self.line

        @pl.when((zb <= ln.z) & (ln.z < ln.chips - 1))
        def _():
            self.up(s, zb).wait_send()

        @pl.when((zb >= ln.z) & (ln.z > 0))
        def _():
            self.down(s, zb).wait_send()

        self.across(s, zb).wait_send()


class ChainSum:
    def __init__(self, line, bufs, sems):
        self.line = line
        self.part, self.sib, self.rise, self.fall, self.out = bufs
        self.sent_sib, self.got_sib, self.got_up, self.got_down, self.sent = sems

    def across(self, s, zb):
        ln = self.line
        return ln.copy(
            self.part.at[s, zb, 1 - ln.c],
            self.sib.at[s, zb],
            self.sent_sib.at[s, zb],
            self.got_sib.at[s, zb],
            ln.sibling(),
        )

    def up(self, s, o):
        ln = self.line
        return ln.copy(
            self.out.at[s, o],
            self.rise.at[s, o],
            self.sent.at[s, o],
            self.got_up.at[s, o],
            ln.at(ln.z + 1),
        )

    def down(self, s, o):
        ln = self.line
        return ln.copy(
            self.out.at[s, o],
            self.fall.at[s, o],
            self.sent.at[s, o],
            self.got_down.at[s, o],
            ln.at(ln.z - 1),
        )

    def mine(self, s, o):
        return self.part[s, o, self.line.c].astype(F32) + self.sib[s, o].astype(F32)

    def hop_up(self, s, o):
        ln = self.line
        self.across(s, o).wait_recv()

        @pl.when(ln.z == 0)
        def _():
            self.out[s, o] = self.mine(s, o).astype(BF16)

        @pl.when(ln.z > 0)
        def _():
            self.up(s, o).wait_recv()
            self.out[s, o] = (self.mine(s, o) + self.rise[s, o].astype(F32)).astype(BF16)

        self.up(s, o).start()

    def hop_down(self, s, o):
        ln = self.line
        self.across(s, o).wait_recv()

        @pl.when(ln.z == ln.chips - 1)
        def _():
            self.out[s, o] = self.mine(s, o).astype(BF16)

        @pl.when(ln.z < ln.chips - 1)
        def _():
            self.down(s, o).wait_recv()
            self.out[s, o] = (self.mine(s, o) + self.fall[s, o].astype(F32)).astype(BF16)

        self.down(s, o).start()

    def hops(self, t, near_first):
        ln = self.line
        last = ln.chips - 1
        for upward in (True, False):
            place = ln.z if upward else last - ln.z
            q = t - place * LAG
            turn = jnp.maximum(q, 0) // ln.steps
            s = jnp.maximum(q, 0) % ln.steps
            far = turn if near_first else last - turn
            far = jnp.clip(far, 0, last)
            ok = (q >= 0) & (turn < ln.chips) & (far > place)
            o = far if upward else last - far

            @pl.when(ok)
            def _():
                if upward:
                    self.hop_up(s, o)
                else:
                    self.hop_down(s, o)

    def finish(self, s, total):
        ln = self.line
        self.across(s, ln.z).wait_recv()
        total[s] = self.mine(s, ln.z)

        @pl.when(ln.z > 0)
        def _():
            self.up(s, ln.z).wait_recv()
            total[s] += self.rise[s, ln.z].astype(F32)

        @pl.when(ln.z < ln.chips - 1)
        def _():
            self.down(s, ln.z).wait_recv()
            total[s] += self.fall[s, ln.z].astype(F32)

    def drain(self, s, zb):
        ln = self.line
        self.across(s, zb).wait_send()

        @pl.when(zb != ln.z)
        def _():
            self.up(s, zb).wait_send()


def drain_all(line, things):
    def body(i, carry):
        for thing in things:
            thing.drain(i // line.chips, i % line.chips)
        return carry

    lax.fori_loop(0, line.steps * line.chips, body, 0)


class Swap:
    def __init__(self, line, bufs, sems):
        self.line = line
        self.src, self.dst = bufs
        self.sent, self.got = sems

    def copy(self, k):
        ln = self.line
        to = (ln.f + k) % ln.frames
        return ln.copy(
            self.src.at[to], self.dst.at[ln.f], self.sent.at[k], self.got.at[k], (to, ln.h)
        )

    def run(self, value):
        ln = self.line
        shape = self.src.shape
        self.src[...] = value.astype(self.src.dtype).reshape(shape)
        for k in range(1, ln.frames):
            self.copy(k).start()
        self.dst[ln.f] = self.src[ln.f]
        for k in range(1, ln.frames):
            self.copy(k).wait()
        return self.dst[...].reshape(shape[0] * shape[1], shape[2]).astype(BF16)


class FrameSum:
    def __init__(self, line, part, full, dim, reverse, recv_bufs, sems):
        self.line, self.part, self.full, self.dim = line, part, full, dim
        self.recv_bufs = recv_bufs
        self.sent, self.got, self.sent_back, self.got_back = sems
        bits = range(line.frames.bit_length() - 1)
        self.bits = list(reversed(bits)) if reverse else list(bits)
        self.spans = []
        start, size = 0, part.shape[dim]
        for bit in self.bits:
            size //= 2
            side = (line.f // (1 << bit)) % 2
            peer = (line.f + (1 - 2 * side) * (1 << bit), line.h)
            keep, give = start + side * size, start + (1 - side) * size
            self.spans.append((keep, give, size, peer))
            start = keep

    def view(self, ref, start, size):
        if self.dim == 0:
            return ref.at[pl.ds(pl.multiple_of(start, size), size)]
        return ref.at[:, pl.ds(pl.multiple_of(start, size), size)]

    def out(self, i):
        _, give, size, peer = self.spans[i]
        src = self.view(self.part, give, size)
        return self.line.copy(src, self.recv_bufs[i], self.sent.at[i], self.got.at[i], peer)

    def back(self, i):
        keep, _, size, peer = self.spans[i]
        ref = self.view(self.full, keep, size)
        return self.line.copy(ref, ref, self.sent_back.at[i], self.got_back.at[i], peer)

    def back_in(self, i):
        _, give, size, peer = self.spans[i]
        ref = self.view(self.full, give, size)
        return self.line.copy(ref, ref, self.sent_back.at[i], self.got_back.at[i], peer)

    def stages(self):
        return 2 * len(self.bits) + 1

    def stage(self, k):
        n = len(self.bits)
        if 1 <= k <= n:
            keep, _, size, _ = self.spans[k - 1]
            self.out(k - 1).wait()
            ref = self.view(self.part, keep, size)
            to = self.view(self.full, keep, size) if k == n else ref
            to[...] = (ref[...].astype(F32) + self.recv_bufs[k - 1][...].astype(F32)).astype(BF16)
        elif k > n:
            i = 2 * n - k
            self.back(i).wait_send()
            self.back_in(i).wait_recv()
        if k < n:
            self.out(k).start()
        elif k < 2 * n:
            self.back(2 * n - 1 - k).start()


def frame_sum_scratch(frames, shape, dim):
    bits = frames.bit_length() - 1
    scratch = []
    for i in range(bits):
        part = list(shape)
        part[dim] = shape[dim] >> (i + 1)
        scratch.append(pltpu.VMEM(tuple(part), BF16))
    return [pltpu.VMEM(shape, BF16)] + scratch + [pltpu.SemaphoreType.DMA((bits,))] * 4


def frame_sums(line, arrays, scratch):
    bits = line.frames.bit_length() - 1
    sums = []
    for full, dim, reverse in arrays:
        part, *mine = scratch[: bits + 5]
        scratch = scratch[bits + 5 :]
        sums.append(FrameSum(line, part, full, dim, reverse, mine[:bits], mine[bits:]))
    return sums


class Everyone:
    def __init__(self, line, bufs, sems):
        self.line = line
        self.src, self.dst_sib, self.dst_line, self.dst_frames = bufs
        self.sent, self.got = sems

    def run(self, value, frames_value):
        ln = self.line
        self.src[0] = value.astype(BF16)
        copy = ln.copy(self.src.at[0], self.dst_sib, self.sent.at[0], self.got.at[0], ln.sibling())
        copy.start()
        copy.wait()
        pair = self.src[0].astype(F32) + self.dst_sib[...].astype(F32)
        self.src[1] = pair.astype(BF16)
        copies = []
        for k in range(1, ln.chips):
            to = (ln.z + k) % ln.chips
            copies.append(
                ln.copy(
                    self.src.at[1],
                    self.dst_line.at[ln.z],
                    self.sent.at[k],
                    self.got.at[k],
                    ln.at(to),
                )
            )
            copies[-1].start()
        self.dst_line[ln.z] = self.src[1]
        for copy in copies:
            copy.wait()
        total = self.dst_line[0].astype(F32)
        for i in range(1, ln.chips):
            total = total + self.dst_line[i].astype(F32)
        self.src[2] = (total + frames_value).astype(BF16)
        copies = []
        for k in range(1, ln.frames):
            to = (ln.f + k) % ln.frames
            slot = ln.chips + k
            copies.append(
                ln.copy(
                    self.src.at[2],
                    self.dst_frames.at[ln.f],
                    self.sent.at[slot],
                    self.got.at[slot],
                    (to, ln.h),
                )
            )
            copies[-1].start()
        self.dst_frames[ln.f] = self.src[2]
        for copy in copies:
            copy.wait()
        total = self.dst_frames[0].astype(F32)
        for i in range(1, ln.frames):
            total = total + self.dst_frames[i].astype(F32)
        return total


def everyone_scratch(chips, frames, rows, width):
    one = (rows, width)
    return [
        pltpu.VMEM((3,) + one, BF16),
        pltpu.VMEM(one, BF16),
        pltpu.VMEM((chips,) + one, BF16),
        pltpu.VMEM((frames,) + one, BF16),
        pltpu.SemaphoreType.DMA((chips + frames,)),
        pltpu.SemaphoreType.DMA((chips + frames,)),
    ]


def gathered_sum(line, gather, sums, own, compute, total, beside, least):
    steps, chips = line.steps, line.chips
    gather.start(own)
    parts = steps * chips

    def body(t, carry):
        distance, s = t // steps, t % steps

        @pl.when(t < parts)
        def _():
            gather.arrive(distance, s)

        def side(upward, inner):
            u = jnp.maximum(t - 1, 0)
            away = u // steps
            zb = jnp.where(upward == 1, line.z + away, line.z - away)
            ok = (t >= 1) & (t <= parts) & (zb >= 0) & (zb < chips)
            ok = ok & ((away > 0) | (upward == 0))

            @pl.when(ok)
            def _():
                where = jnp.clip(zb, 0, chips - 1)
                gather.wait_across(u % steps, where)
                compute(u % steps, where)
                sums.across(u % steps, where).start()

            return inner

        lax.fori_loop(0, 2, side, 0)
        sums.hops(t - LEAD, True)
        beside(t)
        return carry

    lax.fori_loop(0, max(parts + LEAD + (chips - 1) * LAG, least), body, 0)
    for s in range(steps):
        sums.finish(s, total)


def computed_sum(line, sums, compute, total, beside=None):
    steps, chips = line.steps, line.chips

    def body(t, carry):
        @pl.when(t < steps)
        def _():
            compute(t)
            for zb in range(chips):
                sums.across(t, zb).start()

        sums.hops(t - 1, False)
        if beside is not None:
            beside(t)
        return carry

    lax.fori_loop(0, steps * chips + 1 + (chips - 1) * LAG, body, 0)
    for s in range(steps):
        sums.finish(s, total)


def sem_shapes(steps, chips, gather, swap_frames):
    grid = pltpu.SemaphoreType.DMA((steps, chips))
    shapes = [grid] * 5
    if gather:
        shapes += [grid] * 5
    if swap_frames:
        shapes += [pltpu.SemaphoreType.DMA((swap_frames,))] * 2
    return shapes


def sum_bufs(steps, chips, rows, width, streams=1):
    tail = (rows * streams, width)
    one = pltpu.VMEM((steps, chips) + tail, BF16)
    return [pltpu.VMEM((steps, chips, 2) + tail, BF16), one, one, one, one]


def swap_bufs(frames, rows, width):
    kind = BF16 if rows % 16 == 0 else F32
    return [pltpu.VMEM((frames, rows, width), kind)] * 2


def call(kernel, name, collective_id, outs, scratch, args, smem=(), left=()):
    specs = [
        pl.BlockSpec(
            memory_space=pltpu.SMEM if i in smem else pl.ANY if i in left else pltpu.VMEM
        )
        for i in range(len(args))
    ]
    return pl.pallas_call(
        kernel,
        name=name,
        out_shape=[jax.ShapeDtypeStruct(shape, kind) for shape, kind in outs],
        in_specs=specs,
        out_specs=[pl.BlockSpec(memory_space=pltpu.VMEM)] * len(outs),
        scratch_shapes=scratch,
        compiler_params=pltpu.CompilerParams(
            collective_id=collective_id, has_side_effects=True, vmem_limit_bytes=VMEM_LIMIT
        ),
    )(*args)


def spatial_forward(
    ids, x, table, gain, shift, bias, wqkv, wout, to_peers, to_parts,
    normed_out, qkv_out, mixed_out, state_out, next_out,
    part, sib, rise, fall, out, src, dst, total, state0, *sems,
):
    line = Line(sems, x.shape[0])
    sums = ChainSum(line, (part, sib, rise, fall, out), sems[:5])
    swap = Swap(line, (src, dst), sems[5:7])
    line.barrier(True)
    steps, patches, width = x.shape
    rows = patches // line.heads
    entries = table.shape[0]
    table_row = lax.broadcasted_iota(jnp.int32, (entries, width), 0)

    def compute(s):
        picked = jnp.where(table_row == ids[s], table[...].astype(F32), 0.0)
        added = jnp.sum(picked, axis=0, keepdims=True)
        whole = x[s].astype(F32) + added
        own = x[s, pl.ds(pl.multiple_of(line.h * rows, rows), rows)].astype(F32) + added
        state0[s] = own
        normed = (norm_stats(whole)[0] * gain[0:1, :] + shift[0:1, :]).astype(BF16)
        normed_out[s] = normed
        q = mm(normed, wqkv[0]).astype(BF16)
        k = mm(normed, wqkv[1]).astype(BF16)
        v = mm(normed, wqkv[2]).astype(BF16)
        qkv_out[0, s] = q
        qkv_out[1, s] = k
        qkv_out[2, s] = v
        mixed = attend(q, k, v, None)
        mixed_out[s] = mixed
        part[s] = mm(mixed, wout[...]).astype(BF16).reshape(part.shape[1:])

    computed_sum(line, sums, compute, total)
    tokens = steps * rows
    state = state0[...].reshape(tokens, width) + total[...].reshape(tokens, width)
    state = state + bias[0:1, :]
    state_out[...] = state
    normed = (norm_stats(state)[0] * gain[1:2, :] + shift[1:2, :]).astype(BF16)
    got = swap.run(mm(to_peers[...], normed).astype(BF16))
    next_out[...] = mm(to_parts[...], got).astype(BF16).reshape(next_out.shape)
    drain_all(line, (sums,))


def frame_mask(segments, rows):
    frames = segments.shape[0]
    shift = frames.bit_length() - 1

    def ids_along(axis, shape):
        index = lax.broadcasted_iota(jnp.int32, shape, axis)
        frame = index & (frames - 1)
        segment = jnp.zeros(shape, jnp.int32)
        for i in range(frames):
            segment = jnp.where(frame == i, segments[i], segment)
        return lax.shift_right_logical(index, shift), frame, segment

    place_q, frame_q, segment_q = ids_along(0, (rows, 1))
    place_k, frame_k, segment_k = ids_along(1, (1, rows))
    return (place_q == place_k) & (frame_k <= frame_q) & (segment_q == segment_k)


def temporal_forward(
    segments, own, wqkv, wout, gain, shift, bias, state1, from_parts, from_peers,
    normed_out, qkv_out, mixed_out, state_out, next_out,
    part, sib, rise, fall, out, src, dst, total, mask_ref, *sems,
):
    steps, chips, _, rows, width = normed_out.shape
    line = Line(sems, steps)
    sums = ChainSum(line, (part, sib, rise, fall, out), sems[:5])
    gather = Gather(line, normed_out, sems[5:10])
    swap = Swap(line, (src, dst), sems[10:12])
    line.barrier(True)
    mask_ref[...] = frame_mask(segments, 2 * rows).astype(F32)

    def compute(s, zb):
        a = normed_out[s, zb].reshape(2 * rows, width)
        q = mm(a, wqkv[0]).astype(BF16)
        k = mm(a, wqkv[1]).astype(BF16)
        v = mm(a, wqkv[2]).astype(BF16)
        qkv_out[0, s, zb] = q
        qkv_out[1, s, zb] = k
        qkv_out[2, s, zb] = v
        mixed = attend(q, k, v, mask_ref[...] > 0.0)
        mixed_out[s, zb] = mixed
        part[s, zb] = mm(mixed, wout[...]).astype(BF16).reshape(2, rows, width)

    gathered_sum(line, gather, sums, own, compute, total, lambda t: None, 0)
    tokens = steps * rows
    summed = total[...].reshape(tokens, width).astype(BF16)
    got = swap.run(mm(from_parts[...], summed).astype(BF16))
    state = state1[...] + mm(from_peers[...], got) + bias[1:2, :]
    state_out[...] = state
    normed = norm_stats(state)[0] * gain[2:3, :] + shift[2:3, :]
    next_out[...] = normed.astype(BF16).reshape(next_out.shape)
    drain_all(line, (gather, sums))


def mlp(
    own, up, up_bias, down, cotangent, gain, bias, state2, to_peers, to_parts,
    down_grad, up_grad, result_out, grad_out, next_out, small_out, bias_out,
    normed_out, act_out, dpre_out, part, sib, rise, fall, out, src, dst, total, *sems,
):
    steps, chips, _, rows, width = normed_out.shape
    line = Line(sems, steps)
    sums = ChainSum(line, (part, sib, rise, fall, out), sems[:5])
    gather = Gather(line, normed_out, sems[5:10])
    swap = Swap(line, (src, dst), sems[10:12])
    line.barrier(True)
    bias_out[...] = jnp.zeros_like(bias_out)

    def compute(s, zb):
        a = normed_out[s, zb].reshape(2 * rows, width)
        g = cotangent[s, pl.ds(pl.multiple_of(zb * 2 * rows, 2 * rows), 2 * rows)]
        pre = mm(a, up[...]) + up_bias[...]
        t = jnp.tanh(GELU_C * (pre + 0.044715 * (pre * pre * pre)))
        act = (0.5 * pre * (1.0 + t)).astype(BF16)
        act_out[s, zb] = act
        slope = 0.5 * (1.0 + t)
        slope = slope + 0.5 * pre * (1.0 - t * t) * (GELU_C * (1.0 + 0.134145 * (pre * pre)))
        dpre = (mm_nt(g, down[...]) * slope).astype(BF16)
        dpre_out[s, zb] = dpre
        bias_out[...] += jnp.sum(dpre.astype(F32), axis=0, keepdims=True)
        part[s, zb, :, pl.ds(0, rows)] = mm_nt(dpre, up[...]).astype(BF16).reshape(2, rows, width)
        part[s, zb, :, pl.ds(rows, rows)] = mm(act, down[...]).astype(BF16).reshape(2, rows, width)

    hidden = up.shape[1]
    all_tokens = steps * chips * 2 * rows
    n_down, n_up = hidden // 128, width // 256
    first = steps * chips + 1

    def beside(t):
        @pl.when((t >= first) & (t < first + n_down))
        def _():
            cols = pl.ds(pl.multiple_of((t - first) * 128, 128), 128)
            left = act_out[:, :, :, cols].reshape(all_tokens, 128)
            right = cotangent[...].reshape(all_tokens, width)
            down_grad[cols] = mm_tn(left, right).astype(BF16)

        @pl.when((t >= first + n_down) & (t < first + n_down + n_up))
        def _():
            cols = pl.ds(pl.multiple_of((t - first - n_down) * 256, 256), 256)
            left = normed_out[:, :, :, :, cols].reshape(all_tokens, 256)
            right = dpre_out[...].reshape(all_tokens, hidden)
            up_grad[cols] = mm_tn(left, right).astype(BF16)

    gathered_sum(
        line, gather, sums, own, compute, total, beside, first + n_down + n_up
    )
    tokens = steps * rows
    start = pl.multiple_of(line.h * rows, rows)
    state = state2[...]
    grad = cotangent[:, pl.ds(start, rows)].astype(F32).reshape(tokens, width)
    back, gain_grad, shift_grad = norm_back(
        state, total[:, pl.ds(0, rows)].reshape(tokens, width), gain[2:3, :]
    )
    dh = grad + back
    grad_out[...] = dh
    got = swap.run(mm(to_peers[...], dh.astype(BF16)).astype(BF16))
    next_out[...] = mm(to_parts[...], got).astype(BF16).reshape(next_out.shape)
    result = state + total[:, pl.ds(rows, rows)].reshape(tokens, width) + bias[2:3, :]
    result_out[...] = result.astype(BF16).reshape(result_out.shape)
    small_out[...] = jnp.concatenate(
        [
            gain_grad,
            shift_grad,
            jnp.sum(grad, axis=0, keepdims=True),
            jnp.sum(dh, axis=0, keepdims=True),
            jnp.zeros((4, width), F32),
        ],
        axis=0,
    )
    drain_all(line, (gather, sums))


def temporal_backward(
    segments, own, qkv, wqkv, wout, gain, state1, grad2, from_parts, from_peers,
    normed, mixed, down_part, up_part,
    qk_grad, v_grad, out_grad, down_grad, up_grad, grad_out, next_out, small_out,
    grad_gathered, dqkv_out, load_sems,
    part, sib, rise, fall, out, src, dst, total, mask_ref, *sems,
):
    steps, chips, _, rows, width = grad_gathered.shape
    line = Line(sems, steps)
    reduced = frame_sums(line, [(down_grad, 0, False), (up_grad, 0, True)], sems[12:])
    loads = [
        pltpu.make_async_copy(down_part, reduced[0].part, load_sems.at[0]),
        pltpu.make_async_copy(up_part, reduced[1].part, load_sems.at[1]),
    ]
    for load in loads:
        load.start()
    sums = ChainSum(line, (part, sib, rise, fall, out), sems[:5])
    gather = Gather(line, grad_gathered, sems[5:10])
    swap = Swap(line, (src, dst), sems[10:12])
    line.barrier(True)
    mask_ref[...] = frame_mask(segments, 2 * rows).astype(F32)

    def compute(s, zb):
        r = grad_gathered[s, zb].reshape(2 * rows, width)
        dm = mm_nt(r, wout[...]).astype(BF16)
        mask = mask_ref[...] > 0.0
        dq, dk, dv = attend_back(qkv[0, s, zb], qkv[1, s, zb], qkv[2, s, zb], mask, dm)
        dqkv_out[0, s, zb] = dq
        dqkv_out[1, s, zb] = dk
        dqkv_out[2, s, zb] = dv
        da = mm_nt(dq, wqkv[0]) + mm_nt(dk, wqkv[1]) + mm_nt(dv, wqkv[2])
        part[s, zb] = da.astype(BF16).reshape(2, rows, width)

    columns = wout.shape[0]
    all_tokens = steps * chips * 2 * rows
    first = steps * chips + 1
    n_cols = width // 256
    n_stages = reduced[0].stages()

    def beside(t):
        for k in range(n_stages - 1):

            @pl.when(t == (1, 9, 13, 17)[min(k, 3)] + 4 * max(k - 3, 0))
            def _():
                if k == 0:
                    for load in loads:
                        load.wait()
                for one in reduced:
                    one.stage(k)

        @pl.when(t == first)
        def _():
            left = mixed[...].reshape(all_tokens, columns)
            right = grad_gathered[...].reshape(all_tokens, width)
            out_grad[...] = mm_tn(left, right).astype(BF16)

        @pl.when((t > first) & (t <= first + n_cols))
        def _():
            qkv_grads(
                (t - first - 1) * 256, normed, dqkv_out, qk_grad, v_grad, all_tokens, columns
            )

    gathered_sum(line, gather, sums, own, compute, total, beside, first + n_cols + 1)
    tokens = steps * rows
    summed = total[...].reshape(tokens, width).astype(BF16)
    got = swap.run(mm(from_parts[...], summed).astype(BF16))
    back, gain_grad, shift_grad = norm_back(state1[...], mm(from_peers[...], got), gain[1:2, :])
    dh = grad2[...] + back
    grad_out[...] = dh
    next_out[...] = dh.astype(BF16).reshape(next_out.shape)
    small_out[...] = jnp.concatenate(
        [
            gain_grad,
            shift_grad,
            jnp.sum(dh, axis=0, keepdims=True),
            jnp.zeros((5, width), F32),
        ],
        axis=0,
    )
    for one in reduced:
        one.stage(n_stages - 1)
    drain_all(line, (gather, sums))


def qkv_grads(start, normed, dqkv, qk_grad, v_grad, all_tokens, columns):
    width = normed.shape[-1]
    cols = pl.ds(pl.multiple_of(start, 256), 256)
    lead = (slice(None),) * (len(normed.shape) - 1)
    left = normed[lead + (cols,)].reshape(all_tokens, 256)
    for i in range(3):
        grad = mm_tn(left, dqkv[i].reshape(all_tokens, columns)).astype(BF16)
        if i < 2:
            qk_grad[pl.ds(pl.multiple_of(i * width + start, 256), 256)] = grad
        else:
            v_grad[cols] = grad


def spatial_backward(
    ids, own, qkv, wqkv, wout, gain, x, table, grad1,
    normed, mixed, small2, small3, up_bias_part, t_qk_part, t_v_part, t_out_part,
    t_qk_grad, t_v_grad, t_out_grad, qk_grad, v_grad, out_grad, result_out, small_out,
    grad_gathered, dqkv_out, load_sems, every_src, every_sib, every_line, every_frames, every_sent,
    every_got,
    part, sib, rise, fall, out, total, dmixed, *sems,
):
    steps, chips, _, rows, width = grad_gathered.shape
    line = Line(sems, steps)
    reduced = frame_sums(
        line,
        [
            (t_qk_grad, 0, False), (t_v_grad, 0, True), (t_out_grad, 1, True),
            (qk_grad, 0, False), (v_grad, 0, True), (out_grad, 1, True),
        ],
        sems[10:],
    )
    earlier, later = reduced[:3], reduced[3:]
    loads = [
        pltpu.make_async_copy(t_qk_part, earlier[0].part, load_sems.at[0]),
        pltpu.make_async_copy(t_v_part, earlier[1].part, load_sems.at[1]),
        pltpu.make_async_copy(t_out_part, earlier[2].part, load_sems.at[2]),
    ]
    for load in loads:
        load.start()
    n_stages = earlier[0].stages()
    every = Everyone(line, (every_src, every_sib, every_line, every_frames), (every_sent, every_got))
    sums = ChainSum(line, (part, sib, rise, fall, out), sems[:5])
    gather = Gather(line, grad_gathered, sems[5:10])
    line.barrier(True, True)
    entries = table.shape[0]
    table_row = lax.broadcasted_iota(jnp.int32, (entries, width), 0)
    gather.start(own)
    parts = steps * chips

    def body(t, carry):
        @pl.when(t < parts)
        def _():
            gather.arrive(t // steps, t % steps)

        def side(upward, inner):
            u = jnp.maximum(t - 1, 0)
            away, s = u // steps, u % steps
            zb = jnp.where(upward == 1, line.z + away, line.z - away)
            ok = (t >= 1) & (zb >= 0) & (zb < chips) & ((away > 0) | (upward == 0))

            @pl.when(ok)
            def _():
                where = jnp.clip(zb, 0, chips - 1)
                gather.wait_across(s, where)
                r = grad_gathered[s, where].reshape(2 * rows, width)
                start = pl.multiple_of(where * 2 * rows, 2 * rows)
                dmixed[s, pl.ds(start, 2 * rows)] = mm_nt(r, wout[...]).astype(BF16)

            return inner

        lax.fori_loop(0, 2, side, 0)
        for k in range(n_stages):

            @pl.when(t == (1, 6, 9, 12, 16)[min(k, 4)] + 2 * max(k - 4, 0))
            def _():
                if k == 0:
                    for load in loads:
                        load.wait()
                for one in earlier:
                    one.stage(k)

        return carry

    lax.fori_loop(0, max(parts + 1, 17 + 2 * max(n_stages - 5, 0)), body, 0)
    columns = wout.shape[0]
    all_tokens = steps * chips * 2 * rows

    def compute(s):
        dq, dk, dv = attend_back(qkv[0, s], qkv[1, s], qkv[2, s], None, dmixed[s])
        dqkv_out[0, s] = dq
        dqkv_out[1, s] = dk
        dqkv_out[2, s] = dv
        da = mm_nt(dq, wqkv[0]) + mm_nt(dk, wqkv[1]) + mm_nt(dv, wqkv[2])
        part[s] = da.astype(BF16).reshape(part.shape[1:])

    def beside(t):
        @pl.when(t == steps)
        def _():
            left = mixed[...].reshape(all_tokens, columns)
            right = grad_gathered[...].reshape(all_tokens, width)
            later[2].part[...] = mm_tn(left, right).astype(BF16)

        @pl.when((t >= steps) & (t < steps + 2))
        def _():
            for i in range(width // 512):
                start = ((t - steps) * (width // 512) + i) * 256
                qkv_grads(
                    start, normed, dqkv_out, later[0].part, later[1].part, all_tokens, columns
                )

        for k in range(n_stages - 1):

            @pl.when(t == (steps + 1, steps + 5, steps + 7, steps + 9)[min(k, 3)] + 2 * max(k - 3, 0))
            def _():
                for one in later:
                    one.stage(k)

    computed_sum(line, sums, compute, total, beside)
    gain_grad = jnp.zeros((1, width), F32)
    shift_grad = jnp.zeros((1, width), F32)
    table_grad = jnp.zeros((entries, width), F32)
    for s in range(steps):
        picked = jnp.where(table_row == ids[s], table[...].astype(F32), 0.0)
        added = jnp.sum(picked, axis=0, keepdims=True)
        state = x[s, pl.ds(pl.multiple_of(line.h * rows, rows), rows)].astype(F32) + added
        back, one_gain, one_shift = norm_back(state, total[s], gain[0:1, :])
        grad = grad1[pl.ds(s * rows, rows)] + back
        result_out[s] = grad
        gain_grad += one_gain
        shift_grad += one_shift
        here = jnp.sum(grad, axis=0, keepdims=True)
        table_grad += jnp.where(table_row == ids[s], here, 0.0)
    rows_of = [
        gain_grad, small2[0:1], small3[0:1],
        shift_grad, small2[1:2], small3[1:2],
        small2[2:3], small3[3:4], small3[2:3],
        table_grad,
    ]
    filled = 9 + entries
    room = every_src.shape[1]
    value = jnp.concatenate(rows_of + [jnp.zeros((room - filled, width), F32)], axis=0)
    row = lax.broadcasted_iota(jnp.int32, (room, width), 0)
    frames_value = jnp.where(row == filled, up_bias_part[...], 0.0)
    small_out[...] = every.run(value, frames_value)
    for one in later:
        one.stage(n_stages - 1)
    drain_all(line, (gather, sums))


def orders(frames_local, frames, places, t_steps):
    tokens = frames_local * frames * places
    index = np.arange(tokens).reshape(frames_local, frames, places)
    first = index.transpose(1, 0, 2).reshape(-1)
    index = np.arange(tokens).reshape(frames * frames_local, t_steps, places // t_steps)
    second = index.transpose(1, 2, 0).reshape(-1)
    eye = np.eye(tokens, dtype=np.float32)
    to_peers, to_parts = eye[first], eye[second]
    return [jnp.asarray(m, BF16) for m in (to_peers, to_parts, to_parts.T, to_peers.T)]


def on_device(
    block_input,
    action_ids,
    segment_ids,
    action_table,
    norm_gain,
    norm_shift,
    spatial_qkv,
    spatial_out,
    temporal_qkv,
    temporal_out,
    out_bias,
    up_weight,
    up_bias,
    down_weight,
    cotangent,
):
    frames, heads = lax.axis_size("frames"), lax.axis_size("heads")
    chips = heads // 2
    steps, patches, width = block_input.shape
    rows = patches // heads
    tokens = steps * rows
    total_frames = segment_ids.shape[0]
    places = rows // frames
    t_steps = min(4, places)
    t_rows = tokens // t_steps
    columns = spatial_out.shape[0]
    hidden = up_weight.shape[1]
    s_qkv = spatial_qkv.transpose(1, 0, 2)
    t_qkv = temporal_qkv.transpose(1, 0, 2)
    to_peers, to_parts, from_parts, from_peers = orders(steps, frames, places, t_steps)
    swap = swap_bufs(frames, tokens // frames, width)
    owned = ((tokens, width), F32)
    s_blocks = (steps, rows, width)
    t_blocks = (t_steps, t_rows, width)
    t_mask = pltpu.VMEM((2 * t_rows, 2 * t_rows), F32)
    rest = 8, width

    normed1, s_proj, s_mixed, state1, own2 = call(
        spatial_forward,
        "spatial_forward",
        0,
        [
            ((steps, patches, width), BF16),
            ((3, steps, patches, columns), BF16),
            ((steps, patches, columns), BF16),
            owned,
            (t_blocks, BF16),
        ],
        sum_bufs(steps, chips, rows, width)
        + swap
        + [pltpu.VMEM(s_blocks, F32), pltpu.VMEM(s_blocks, F32)]
        + sem_shapes(steps, chips, False, frames),
        (
            action_ids, block_input, action_table, norm_gain, norm_shift, out_bias,
            s_qkv, spatial_out, to_peers, to_parts,
        ),
        smem=(0,),
    )
    t_all = (t_steps, chips, 2, t_rows, width)
    t_cols = (t_steps, chips, 2 * t_rows, columns)
    normed2, t_proj, t_mixed, state2, own3 = call(
        temporal_forward,
        "temporal_forward",
        1,
        [
            (t_all, BF16),
            ((3,) + t_cols, BF16),
            (t_cols, BF16),
            owned,
            (s_blocks, BF16),
        ],
        sum_bufs(t_steps, chips, t_rows, width)
        + swap
        + [pltpu.VMEM(t_blocks, F32), t_mask]
        + sem_shapes(t_steps, chips, True, frames),
        (
            segment_ids, own2, t_qkv, temporal_out, norm_gain, norm_shift, out_bias,
            state1, from_parts, from_peers,
        ),
        smem=(0,),
    )
    s_all = (steps, chips, 2, rows, width)
    f_cols = (steps, chips, 2 * rows, hidden)
    grads_mlp = [((hidden, width), BF16), ((width, hidden), BF16)]
    down_part, up_part, block_output, grad2, own4, small3, up_bias_part = call(
        mlp,
        "mlp",
        2,
        grads_mlp
        + [
            (s_blocks, BF16),
            owned,
            (t_blocks, BF16),
            (rest, F32),
            ((1, hidden), F32),
        ],
        [pltpu.VMEM(s_all, BF16), pltpu.VMEM(f_cols, BF16), pltpu.VMEM(f_cols, BF16)]
        + sum_bufs(steps, chips, rows, width, 2)
        + swap
        + [pltpu.VMEM((steps, 2 * rows, width), F32)]
        + sem_shapes(steps, chips, True, frames),
        (
            own3, up_weight, up_bias.reshape(1, hidden), down_weight, cotangent, norm_gain,
            out_bias, state2, to_peers, to_parts,
        ),
    )
    grads_attention = [
        ((2 * width, columns), BF16),
        ((width, columns), BF16),
        ((columns, width), BF16),
    ]
    dims_attention = (0, 0, 1)
    t_qk_part, t_v_part, t_out_part, g_down, g_up, grad1, own5, small2 = call(
        temporal_backward,
        "temporal_backward",
        3,
        grads_attention + grads_mlp + [owned, (s_blocks, BF16), (rest, F32)],
        [
            pltpu.VMEM(t_all, BF16),
            pltpu.VMEM((3,) + t_cols, BF16),
            pltpu.SemaphoreType.DMA((2,)),
        ]
        + sum_bufs(t_steps, chips, t_rows, width)
        + swap
        + [pltpu.VMEM(t_blocks, F32), t_mask]
        + sem_shapes(t_steps, chips, True, frames)
        + [x for shape, _ in grads_mlp for x in frame_sum_scratch(frames, shape, 0)],
        (
            segment_ids, own4, t_proj, t_qkv, temporal_out, norm_gain, state1, grad2,
            from_parts, from_peers, normed2, t_mixed, down_part, up_part,
        ),
        smem=(0,),
        left=(12, 13),
    )
    room = -(-(10 + action_table.shape[0]) // 16) * 16
    up_bias_row = jnp.pad(up_bias_part, ((0, 0), (0, width - hidden)))
    g_t_qk, g_t_v, g_t_out, g_s_qk, g_s_v, g_s_out, input_grad, small = call(
        spatial_backward,
        "spatial_backward",
        4,
        grads_attention * 2 + [(s_blocks, F32), ((room, width), F32)],
        [
            pltpu.VMEM(s_all, BF16),
            pltpu.VMEM((3, steps, patches, columns), BF16),
            pltpu.SemaphoreType.DMA((3,)),
        ]
        + everyone_scratch(chips, frames, room, width)
        + sum_bufs(steps, chips, rows, width)
        + [pltpu.VMEM(s_blocks, F32), pltpu.VMEM((steps, patches, columns), BF16)]
        + sem_shapes(steps, chips, True, 0)
        + [
            x
            for (shape, _), dim in zip(grads_attention * 2, dims_attention * 2)
            for x in frame_sum_scratch(frames, shape, dim)
        ],
        (
            action_ids, own5, s_proj, s_qkv, spatial_out, norm_gain, block_input, action_table,
            grad1, normed1, s_mixed, small2, small3, up_bias_row, t_qk_part, t_v_part, t_out_part,
        ),
        smem=(0,),
        left=(14, 15, 16),
    )

    def qkv_of(qk, v):
        whole = jnp.concatenate([qk, v], axis=0).reshape(3, width, columns)
        return whole.transpose(1, 0, 2).astype(F32)

    filled = 9 + action_table.shape[0]
    return (
        block_output,
        input_grad,
        small[9:filled],
        small[0:3],
        small[3:6],
        qkv_of(g_s_qk, g_s_v),
        g_s_out.astype(F32),
        qkv_of(g_t_qk, g_t_v),
        g_t_out.astype(F32),
        small[6:9],
        g_up.astype(F32),
        small[filled, :hidden],
        g_down.astype(F32),
    )


def solution(mesh):
    return jax.shard_map(
        on_device,
        mesh=mesh,
        in_specs=(
            P("frames", None, None),
            P("frames"),
            P(),
            P(),
            P(),
            P(),
            P(None, None, "heads"),
            P("heads", None),
            P(None, None, "heads"),
            P("heads", None),
            P(),
            P(None, "heads"),
            P("heads"),
            P("heads", None),
            P("frames", None, None),
        ),
        out_specs=(
            P("frames", "heads", None),
            P("frames", "heads", None),
            P(),
            P(),
            P(),
            P(None, None, "heads"),
            P("heads", None),
            P(None, None, "heads"),
            P("heads", None),
            P(),
            P(None, "heads"),
            P("heads"),
            P("heads", None),
        ),
        check_vma=False,
    )
```

time: 796 us -> 306 us (0.38)
  waiting for transfers between devices: 438 us -> 0 us
  Pallas kernels: 0 us -> 292 us
  local copies, waits for them, and re-layouts: 93 us -> 3.95 us
  other arithmetic: 96.9 us -> 8.82 us
  blocking collectives: 73.7 us -> 0 us
  matrix products: 61.9 us -> 0 us
  between operations: 15.5 us -> 0.72 us
  starting transfers between devices: 9.56 us -> 0 us
    psum x6 -> x0, waiting for transfers between devices: 404 us -> none  [the longest x5 327 us: combine_heads(): lax.psum(partial_value.astype(jnp.bfloat16), 'heads').astype(jnp.float32)]
    pallas_call x0 -> x5, Pallas kernels: none -> 292 us  [call(): pl.pallas_call(kernel, name=name, out_shape=[jax.ShapeDtypeStruct(shape,...]
    dot_general x32 -> x0, matrix products: 61.9 us -> none  [the longest x1 4.71 us: on_device(): jnp.einsum('fpd,cpfh->dch', normed2, d_tproj, preferred_element_type=jnp....]
    reduce_sum x21 -> x0, other arithmetic: 57.4 us -> none  [the longest x9 26.8 us: layer_norm(): return centered * lax.rsqrt(spread + 1e-05) * gain + shift]
    all_to_all x2 -> x0, blocking collectives: 55.6 us -> none  [the longest x1 27.8 us: on_device(): lax.all_to_all(pos2.astype(jnp.bfloat16), 'frames', split_axis=0, concat_...]
    convert_element_type x13 -> x0, local copies, waits for them, and re-layouts: 40.6 us -> none  [the longest x3 12.6 us: on_device(): pos1 = lax.all_to_all(state1.astype(jnp.bfloat16), 'frames', split_axis=1...]
    all_to_all x2 -> x0, waiting for transfers between devices: 34.1 us -> none  [the longest x1 23.5 us: on_device(): lax.all_to_all(state1.astype(jnp.bfloat16), 'frames', split_axis=1, conca...]
    convert_element_type x21 -> x6, other arithmetic: 35.8 us -> 7.35 us  [the longest x2 2.49 us: qkv_of(): return whole.transpose(1, 0, 2).astype(F32)]
  transfers between devices with their start and end apart: 8 -> 0, of which waited for: 8 -> 0; matrix products, arithmetic and copies ran while one was open for 7% -> 0% of each run, Pallas kernels for 0% -> 0%
where the time goes in v1:
time: 306 us; the launch traced here: 305 us
  Pallas kernels  292 us (95%)
  other arithmetic  8.82 us (3%)
  local copies, waits for them, and re-layouts  3.95 us (1%)
    pallas_call x5, Pallas kernels, call(): pl.pallas_call(kernel, name=name, out_shape=[jax.ShapeDtypeStruct(shape,...  292 us

profile of v1, /device:TPU:0, one launch (start us, length us, event | category | flops | bytes accessed | tf_op | source)
XLA Modules:
  0.0 305.4 jit_solution(8406204497037986027)
XLA Ops:
  0.6 33.0 %spatial_forward.1 = (bf16[4,256,1024]{2,1,0:T(8,128)(2,1)}, bf16[3,4,256,128]{3,2,1,0:T(8,128)(2,1)}, bf16[4,256,128]{2,1,0:T(8,128)(2,1)}, f32[128,1024]{1,0:T(8,128)}, bf16[4,32,1024]{2,1,0:T(8,128)(2,1)}) custom-call(s32[4]{0:T(128)} %ids.3, bf16[4,256,1024]{2,1,0:T(8,128)(2,1)} %x.5, bf16[8,1024]{1,0:T(8,128)(2,1)} %table.3, f32[3,1024]{1,0:T(4,128)} %gain.9, ...), custom_call_target="tpu_custom_call" | custom-call | tf_op jit(solution)/shard_map/spatial_forward/pallas_call | solution.py:615
  33.6 51.6 %temporal_forward.1 = (bf16[4,4,2,32,1024]{4,3,2,1,0:T(8,128)(2,1)}, bf16[3,4,4,64,128]{4,3,2,1,0:T(8,128)(2,1)}, bf16[4,4,64,128]{3,2,1,0:T(8,128)(2,1)}, f32[128,1024]{1,0:T(8,128)}, bf16[4,32,1024]{2,1,0:T(8,128)(2,1)}) custom-call(s32[16]{0:T(128)} %segments.3, bf16[4,32,1024]{2,1,0:T(8,128)(2,1)} %get-tuple-element.46.own, ...), custom_call_target="tpu_custom_call" | custom-call | tf_op jit(solution)/shard_map/temporal_forward/pallas_call | solution.py:615
  85.2 69.2 %mlp.1 = (bf16[512,1024]{1,0:T(8,128)(2,1)}, bf16[1024,512]{1,0:T(8,128)(2,1)}, bf16[4,32,1024]{2,1,0:T(8,128)(2,1)}, f32[128,1024]{1,0:T(8,128)}, bf16[4,32,102...) custom-call(bf16[4,32,1024]{2,1,0:T(8,128)(2,1)} %get-tuple-element.48.own, bf16[1024,512]{1,0:T(8,128)(2,1)} %up.1, ...), custom_call_target="tpu_custom_call" | custom-call | tf_op jit(solution)/shard_map/mlp/pallas_call | solution.py:615
  154.5 0.0 copy-start.7
  154.5 63.0 %temporal_backward.1 = (bf16[2048,128]{1,0:T(8,128)(2,1)}, bf16[1024,128]{1,0:T(8,128)(2,1)}, bf16[128,1024]{1,0:T(8,128)(2,1)}, bf16[512,1024]{1,0:T(8,128)(2,1...) custom-call(s32[16]{0:T(128)} %segments.3, ...), custom_call_target="tpu_custom_call" | custom-call | tf_op jit(solution)/shard_map/temporal_backward/pallas_call | solution.py:615
  217.5 0.0 copy-done.7
  217.5 0.6 pad.4.up_bias_part
  218.1 75.1 %spatial_backward.1 = (bf16[2048,128]{1,0:T(8,128)(2,1)}, bf16[1024,128]{1,0:T(8,128)(2,1)}, bf16[128,1024]{1,0:T(8,128)(2,1)}, bf16[2048,128]{1,0:T(8,128)(2,1)...) custom-call(s32[4]{0:T(128)} %ids.3, ...), custom_call_target="tpu_custom_call" | custom-call | tf_op jit(solution)/shard_map/spatial_backward/pallas_call | solution.py:615
  293.2 1.5 pad_maximum_fusion
  294.7 1.2 convert_bitcast_fusion
  295.9 0.0 copy-start.4
  295.9 0.0 copy-start.3
  295.9 0.0 copy-start.6
  295.9 0.0 copy-start.1
  295.9 1.2 convert_bitcast_fusion.1
  297.2 0.0 copy-done.4
  297.2 0.8 convert_element_type.35
  298.0 0.0 copy-done.3
  298.0 0.8 convert_element_type.39
  298.9 0.0 copy-done.6
  298.9 0.6 fusion
  299.5 0.6 slice.15
  300.1 0.6 slice.19
  300.7 0.0 copy-done.1
  300.7 0.0 copy-start
  300.7 1.6 convert_element_type.40
  302.3 0.0 copy-done
  302.3 0.0 copy-start.5
  302.3 0.0 copy-start.2
  302.3 1.6 convert_element_type.41
  303.9 0.0 copy-done.5
  303.9 0.7 copy.34
  304.6 0.0 copy-done.2
  304.6 0.8 copy.35
Async XLA Ops:
  154.5 63.0 %copy-start.7 = (f32[1,512]{1,0:T(1,128)S(1)}, f32[1,512]{1,0:T(1,128)}, u32[]{:S(2)}) copy-start(f32[1,512]{1,0:T(1,128)} %get-tuple-element.65) | copy-start | bytes 6148
  295.9 1.3 copy-start.4
  295.9 2.1 copy-start.3
  295.9 2.9 copy-start.6
  295.9 4.8 %copy-start.1 = (bf16[1024,512]{1,0:T(8,128)(2,1)S(1)}, bf16[1024,512]{1,0:T(8,128)(2,1)}, u32[]{:S(2)}) copy-start(bf16[1024,512]{1,0:T(8,128)(2,1)} %get-tuple-element.77) | copy-start | bytes 3145732
  300.7 1.6 copy-start
  302.3 1.6 copy-start.5
  302.3 2.3 copy-start.2

commit v2 on v1

--- a/solution.py
+++ b/solution.py
@@ -94,7 +94,7 @@
 
 
 class Line:
-    def __init__(self, sems, steps):
+    def __init__(self, steps):
         self.frames = lax.axis_size("frames")
         self.heads = lax.axis_size("heads")
         self.chips = self.heads // 2
@@ -103,7 +103,6 @@
         self.z = self.h // 2
         self.c = self.h % 2
         self.steps = steps
-        self.sems = sems
 
     def at(self, z):
         return (self.f, jnp.clip(z, 0, self.chips - 1) * 2 + self.c)
@@ -179,20 +178,24 @@
             ref, ref, self.sent_sib.at[s, zb], self.got_sib.at[s, zb], ln.sibling()
         ).wait_recv()
 
+    def send(self, s):
+        ln = self.line
+
+        @pl.when(ln.z < ln.chips - 1)
+        def _():
+            self.up(s, ln.z).start()
+
+        @pl.when(ln.z > 0)
+        def _():
+            self.down(s, ln.z).start()
+
+        self.across(s, ln.z).start()
+
     def start(self, own):
         ln = self.line
         for s in range(ln.steps):
             self.buf[s, ln.z, ln.c] = own[s]
-
-            @pl.when(ln.z < ln.chips - 1)
-            def _():
-                self.up(s, ln.z).start()
-
-            @pl.when(ln.z > 0)
-            def _():
-                self.down(s, ln.z).start()
-
-            self.across(s, ln.z).start()
+            self.send(s)
 
     def arrive(self, distance, s):
         ln = self.line
@@ -301,17 +304,19 @@
 
         self.down(s, o).start()
 
-    def hops(self, t, near_first):
+    def hops(self, t, part=None, fits=True):
         ln = self.line
         last = ln.chips - 1
         for upward in (True, False):
             place = ln.z if upward else last - ln.z
             q = t - place * LAG
-            turn = jnp.maximum(q, 0) // ln.steps
-            s = jnp.maximum(q, 0) % ln.steps
-            far = turn if near_first else last - turn
-            far = jnp.clip(far, 0, last)
-            ok = (q >= 0) & (turn < ln.chips) & (far > place)
+            if part is None:
+                turn = jnp.maximum(q, 0) // ln.steps
+                s = jnp.maximum(q, 0) % ln.steps
+            else:
+                turn, s = jnp.maximum(q, 0), part
+            far = jnp.clip(last - turn, 0, last)
+            ok = (q >= 0) & (turn < last) & (far > place) & fits
             o = far if upward else last - far
 
             @pl.when(ok)
@@ -324,17 +329,17 @@
     def finish(self, s, total):
         ln = self.line
         self.across(s, ln.z).wait_recv()
-        total[s] = self.mine(s, ln.z)
+        total[...] = self.mine(s, ln.z)
 
         @pl.when(ln.z > 0)
         def _():
             self.up(s, ln.z).wait_recv()
-            total[s] += self.rise[s, ln.z].astype(F32)
+            total[...] += self.rise[s, ln.z].astype(F32)
 
         @pl.when(ln.z < ln.chips - 1)
         def _():
             self.down(s, ln.z).wait_recv()
-            total[s] += self.fall[s, ln.z].astype(F32)
+            total[...] += self.fall[s, ln.z].astype(F32)
 
     def drain(self, s, zb):
         ln = self.line
@@ -345,13 +350,13 @@
             self.up(s, zb).wait_send()
 
 
-def drain_all(line, things):
+def drain_all(line, things, parts):
     def body(i, carry):
         for thing in things:
             thing.drain(i // line.chips, i % line.chips)
         return carry
 
-    lax.fori_loop(0, line.steps * line.chips, body, 0)
+    lax.fori_loop(0, parts * line.chips, body, 0)
 
 
 class Swap:
@@ -367,15 +372,21 @@
             self.src.at[to], self.dst.at[ln.f], self.sent.at[k], self.got.at[k], (to, ln.h)
         )
 
-    def run(self, value):
-        ln = self.line
-        shape = self.src.shape
-        self.src[...] = value.astype(self.src.dtype).reshape(shape)
+    def start(self):
+        ln = self.line
         for k in range(1, ln.frames):
             self.copy(k).start()
         self.dst[ln.f] = self.src[ln.f]
-        for k in range(1, ln.frames):
+
+    def wait(self):
+        for k in range(1, self.line.frames):
             self.copy(k).wait()
+
+    def run(self, value):
+        shape = self.src.shape
+        self.src[...] = value.astype(self.src.dtype).reshape(shape)
+        self.start()
+        self.wait()
         return self.dst[...].reshape(shape[0] * shape[1], shape[2]).astype(BF16)
 
 
@@ -526,45 +537,65 @@
     ]
 
 
-def gathered_sum(line, gather, sums, own, compute, total, beside, least):
-    steps, chips = line.steps, line.chips
-    gather.start(own)
-    parts = steps * chips
-
-    def body(t, carry):
-        distance, s = t // steps, t % steps
-
-        @pl.when(t < parts)
-        def _():
-            gather.arrive(distance, s)
-
-        def side(upward, inner):
-            u = jnp.maximum(t - 1, 0)
-            away = u // steps
-            zb = jnp.where(upward == 1, line.z + away, line.z - away)
-            ok = (t >= 1) & (t <= parts) & (zb >= 0) & (zb < chips)
-            ok = ok & ((away > 0) | (upward == 0))
-
-            @pl.when(ok)
-            def _():
-                where = jnp.clip(zb, 0, chips - 1)
-                gather.wait_across(u % steps, where)
-                compute(u % steps, where)
-                sums.across(u % steps, where).start()
-
-            return inner
-
-        lax.fori_loop(0, 2, side, 0)
-        sums.hops(t - LEAD, True)
-        beside(t)
+def pipeline(line, gather, sums, items, streams, compute, owner, total, beside):
+    last = line.chips - 1
+    at_compute = 2 * last + 1
+    at_sum = at_compute + 1
+    at_owner = at_sum + last * LAG
+    every = -(-(at_owner + 2) // streams)
+
+    def body(m, carry):
+        for i in range(every):
+            for behind in reversed(range(streams)):
+                q = behind * every + i
+                n = m - behind
+                fits = (n >= 0) & (n < items)
+                n = jnp.clip(n, 0, items - 1)
+                if q == 0:
+
+                    @pl.when(fits)
+                    def _():
+                        gather.send(n)
+
+                if q % 2 == 0 and 1 <= q // 2 <= last:
+
+                    @pl.when(fits)
+                    def _():
+                        gather.arrive(q // 2, n)
+
+                if q == at_compute:
+
+                    @pl.when(fits)
+                    def _():
+                        for zb in range(line.chips):
+                            gather.wait_across(n, zb)
+                        compute(n)
+                        for zb in range(line.chips):
+                            sums.across(n, zb).start()
+
+                if at_sum <= q < at_owner:
+                    sums.hops(q - at_sum, n, fits)
+                if q == at_owner:
+
+                    @pl.when(fits)
+                    def _():
+                        sums.finish(n, total)
+                        owner(n)
+
+            beside(m * every + i, i)
         return carry
 
-    lax.fori_loop(0, max(parts + LEAD + (chips - 1) * LAG, least), body, 0)
-    for s in range(steps):
-        sums.finish(s, total)
-
-
-def computed_sum(line, sums, compute, total, beside=None):
+    lax.fori_loop(0, items + streams - 1, body, 0)
+
+
+def pipeline_steps(chips, items, streams):
+    last = chips - 1
+    at_compute = 2 * last + 1
+    every = -(-(at_compute + 1 + last * LAG + 2) // streams)
+    return every, lambda n: n + at_compute // every + 1, (items + streams - 1) * every
+
+
+def computed_sum(line, sums, compute, totals, beside):
     steps, chips = line.steps, line.chips
 
     def body(t, carry):
@@ -574,35 +605,32 @@
             for zb in range(chips):
                 sums.across(t, zb).start()
 
-        sums.hops(t - 1, False)
-        if beside is not None:
-            beside(t)
+        sums.hops(t - 1)
+        beside(t)
         return carry
 
     lax.fori_loop(0, steps * chips + 1 + (chips - 1) * LAG, body, 0)
     for s in range(steps):
-        sums.finish(s, total)
-
-
-def sem_shapes(steps, chips, gather, swap_frames):
-    grid = pltpu.SemaphoreType.DMA((steps, chips))
-    shapes = [grid] * 5
-    if gather:
-        shapes += [grid] * 5
-    if swap_frames:
-        shapes += [pltpu.SemaphoreType.DMA((swap_frames,))] * 2
-    return shapes
-
-
-def sum_bufs(steps, chips, rows, width, streams=1):
-    tail = (rows * streams, width)
+        sums.finish(s, totals.at[s])
+
+
+def chain_sems(parts, chips):
+    return [pltpu.SemaphoreType.DMA((parts, chips))] * 5
+
+
+def swap_sems(frames):
+    return [pltpu.SemaphoreType.DMA((frames,))] * 2
+
+
+def sum_bufs(steps, chips, rows, width):
+    tail = (rows, width)
     one = pltpu.VMEM((steps, chips) + tail, BF16)
     return [pltpu.VMEM((steps, chips, 2) + tail, BF16), one, one, one, one]
 
 
-def swap_bufs(frames, rows, width):
-    kind = BF16 if rows % 16 == 0 else F32
-    return [pltpu.VMEM((frames, rows, width), kind)] * 2
+def swap_bufs(frames, part):
+    kind = BF16 if part[-2] % 16 == 0 else F32
+    return [pltpu.VMEM((frames,) + part, kind)] * 2
 
 
 def call(kernel, name, collective_id, outs, scratch, args, smem=(), left=()):
@@ -626,18 +654,29 @@
 
 
 def spatial_forward(
-    ids, x, table, gain, shift, bias, wqkv, wout, to_peers, to_parts,
-    normed_out, qkv_out, mixed_out, state_out, next_out,
-    part, sib, rise, fall, out, src, dst, total, state0, *sems,
+    ids, x, table, gain, shift, bias, wqkv, wout, cotangent, to_peers, to_parts,
+    normed_out, qkv_out, mixed_out, state_out, cotangent_out,
+    part, sib, rise, fall, out, src, dst, total, state0, g_src, g_dst, *sems,
 ):
-    line = Line(sems, x.shape[0])
+    steps, patches, width = x.shape
+    line = Line(steps)
     sums = ChainSum(line, (part, sib, rise, fall, out), sems[:5])
     swap = Swap(line, (src, dst), sems[5:7])
+    g_swap = Swap(line, (g_src, g_dst), sems[7:9])
     line.barrier(True)
-    steps, patches, width = x.shape
     rows = patches // line.heads
+    tokens = steps * rows
     entries = table.shape[0]
     table_row = lax.broadcasted_iota(jnp.int32, (entries, width), 0)
+
+    def to_peers_of(i, carry):
+        block = cotangent[:, pl.ds(pl.multiple_of(i * rows, rows), rows)].reshape(tokens, width)
+        moved = mm(to_peers[...], block).astype(BF16).astype(g_src.dtype)
+        g_src[:, i] = moved.reshape(line.frames, tokens // line.frames, width)
+        return carry
+
+    lax.fori_loop(0, line.heads, to_peers_of, 0)
+    g_swap.start()
 
     def compute(s):
         picked = jnp.where(table_row == ids[s], table[...].astype(F32), 0.0)
@@ -657,15 +696,21 @@
         mixed_out[s] = mixed
         part[s] = mm(mixed, wout[...]).astype(BF16).reshape(part.shape[1:])
 
-    computed_sum(line, sums, compute, total)
-    tokens = steps * rows
+    computed_sum(line, sums, compute, total, lambda t: None)
     state = state0[...].reshape(tokens, width) + total[...].reshape(tokens, width)
-    state = state + bias[0:1, :]
-    state_out[...] = state
-    normed = (norm_stats(state)[0] * gain[1:2, :] + shift[1:2, :]).astype(BF16)
-    got = swap.run(mm(to_peers[...], normed).astype(BF16))
-    next_out[...] = mm(to_parts[...], got).astype(BF16).reshape(next_out.shape)
-    drain_all(line, (sums,))
+    state = (state + bias[0:1, :]).astype(BF16)
+    got = swap.run(mm(to_peers[...], state).astype(BF16))
+    state_out[...] = mm(to_parts[...], got).astype(BF16).reshape(state_out.shape)
+    g_swap.wait()
+
+    def to_parts_of(i, carry):
+        block = g_dst[:, i].reshape(tokens, width).astype(BF16)
+        moved = mm(to_parts[...], block).astype(BF16)
+        cotangent_out[:, i] = moved.reshape(state_out.shape)
+        return carry
+
+    lax.fori_loop(0, line.heads, to_parts_of, 0)
+    drain_all(line, (sums,), steps)
 
 
 def frame_mask(segments, rows):
@@ -685,262 +730,258 @@
     return (place_q == place_k) & (frame_k <= frame_q) & (segment_q == segment_k)
 
 
-def temporal_forward(
-    segments, own, wqkv, wout, gain, shift, bias, state1, from_parts, from_peers,
-    normed_out, qkv_out, mixed_out, state_out, next_out,
-    part, sib, rise, fall, out, src, dst, total, mask_ref, *sems,
+def middle(
+    segments, state1, cotangent, wqkv, wout, up, up_bias, down, gain, shift, bias,
+    from_parts, from_peers,
+    down_grad, up_grad, qk_grad, v_grad, out_grad, y_part, result_out, next_out, small_out,
+    bias_out,
+    gathered, qkv, mixed_ref, act_ref, dpre_ref, dqkv, state2, grad2, grad1, mask_ref,
+    part, sib, rise, fall, out, src, dst, total, *sems,
 ):
-    steps, chips, _, rows, width = normed_out.shape
-    line = Line(sems, steps)
+    items, chips, _, rows, width = gathered.shape
+    streams = items // 3
+    line = Line(items)
     sums = ChainSum(line, (part, sib, rise, fall, out), sems[:5])
-    gather = Gather(line, normed_out, sems[5:10])
+    gather = Gather(line, gathered, sems[5:10])
     swap = Swap(line, (src, dst), sems[10:12])
+    reduced = frame_sums(line, [(down_grad, 0, False), (up_grad, 0, True)], sems[12:])
     line.barrier(True)
-    mask_ref[...] = frame_mask(segments, 2 * rows).astype(F32)
-
-    def compute(s, zb):
-        a = normed_out[s, zb].reshape(2 * rows, width)
+    count = 2 * chips * rows
+    columns, hidden = wout.shape[0], up.shape[1]
+    mask_ref[...] = frame_mask(segments, count).astype(F32)
+    bias_out[...] = jnp.zeros_like(bias_out)
+    small_out[...] = jnp.zeros_like(small_out)
+
+    def norm(value, i):
+        return (norm_stats(value)[0] * gain[i : i + 1, :] + shift[i : i + 1, :]).astype(BF16)
+
+    for s in range(streams):
+        gathered[s, line.z, line.c] = norm(state1[s].astype(F32), 1)
+
+    def compute_temporal(s, n):
+        a = gathered[n].reshape(count, width)
         q = mm(a, wqkv[0]).astype(BF16)
         k = mm(a, wqkv[1]).astype(BF16)
         v = mm(a, wqkv[2]).astype(BF16)
-        qkv_out[0, s, zb] = q
-        qkv_out[1, s, zb] = k
-        qkv_out[2, s, zb] = v
+        qkv[0, s] = q
+        qkv[1, s] = k
+        qkv[2, s] = v
         mixed = attend(q, k, v, mask_ref[...] > 0.0)
-        mixed_out[s, zb] = mixed
-        part[s, zb] = mm(mixed, wout[...]).astype(BF16).reshape(2, rows, width)
-
-    gathered_sum(line, gather, sums, own, compute, total, lambda t: None, 0)
-    tokens = steps * rows
-    summed = total[...].reshape(tokens, width).astype(BF16)
-    got = swap.run(mm(from_parts[...], summed).astype(BF16))
-    state = state1[...] + mm(from_peers[...], got) + bias[1:2, :]
-    state_out[...] = state
-    normed = norm_stats(state)[0] * gain[2:3, :] + shift[2:3, :]
-    next_out[...] = normed.astype(BF16).reshape(next_out.shape)
-    drain_all(line, (gather, sums))
-
-
-def mlp(
-    own, up, up_bias, down, cotangent, gain, bias, state2, to_peers, to_parts,
-    down_grad, up_grad, result_out, grad_out, next_out, small_out, bias_out,
-    normed_out, act_out, dpre_out, part, sib, rise, fall, out, src, dst, total, *sems,
-):
-    steps, chips, _, rows, width = normed_out.shape
-    line = Line(sems, steps)
-    sums = ChainSum(line, (part, sib, rise, fall, out), sems[:5])
-    gather = Gather(line, normed_out, sems[5:10])
-    swap = Swap(line, (src, dst), sems[10:12])
-    line.barrier(True)
-    bias_out[...] = jnp.zeros_like(bias_out)
-
-    def compute(s, zb):
-        a = normed_out[s, zb].reshape(2 * rows, width)
-        g = cotangent[s, pl.ds(pl.multiple_of(zb * 2 * rows, 2 * rows), 2 * rows)]
+        mixed_ref[s] = mixed
+        part[n] = mm(mixed, wout[...]).astype(BF16).reshape(chips, 2, rows, width)
+
+    def compute_mlp(s, n):
+        a = gathered[n].reshape(count, width)
+        g = cotangent[s].reshape(count, width)
         pre = mm(a, up[...]) + up_bias[...]
         t = jnp.tanh(GELU_C * (pre + 0.044715 * (pre * pre * pre)))
         act = (0.5 * pre * (1.0 + t)).astype(BF16)
-        act_out[s, zb] = act
+        act_ref[s] = act
         slope = 0.5 * (1.0 + t)
         slope = slope + 0.5 * pre * (1.0 - t * t) * (GELU_C * (1.0 + 0.134145 * (pre * pre)))
         dpre = (mm_nt(g, down[...]) * slope).astype(BF16)
-        dpre_out[s, zb] = dpre
+        dpre_ref[s] = dpre
         bias_out[...] += jnp.sum(dpre.astype(F32), axis=0, keepdims=True)
-        part[s, zb, :, pl.ds(0, rows)] = mm_nt(dpre, up[...]).astype(BF16).reshape(2, rows, width)
-        part[s, zb, :, pl.ds(rows, rows)] = mm(act, down[...]).astype(BF16).reshape(2, rows, width)
-
-    hidden = up.shape[1]
-    all_tokens = steps * chips * 2 * rows
-    n_down, n_up = hidden // 128, width // 256
-    first = steps * chips + 1
-
-    def beside(t):
-        @pl.when((t >= first) & (t < first + n_down))
-        def _():
-            cols = pl.ds(pl.multiple_of((t - first) * 128, 128), 128)
-            left = act_out[:, :, :, cols].reshape(all_tokens, 128)
+        part[n] = mm_nt(dpre, up[...]).astype(BF16).reshape(chips, 2, rows, width)
+        y_part[s] = mm(act, down[...]).astype(BF16).reshape(chips, 2, rows, width)
+
+    def compute_back(s, n):
+        r = gathered[n].reshape(count, width)
+        dm = mm_nt(r, wout[...]).astype(BF16)
+        dq, dk, dv = attend_back(qkv[0, s], qkv[1, s], qkv[2, s], mask_ref[...] > 0.0, dm)
+        dqkv[0, s] = dq
+        dqkv[1, s] = dk
+        dqkv[2, s] = dv
+        da = mm_nt(dq, wqkv[0]) + mm_nt(dk, wqkv[1]) + mm_nt(dv, wqkv[2])
+        part[n] = da.astype(BF16).reshape(chips, 2, rows, width)
+
+    def owner_temporal(s, n):
+        state = state1[s].astype(F32) + total[...] + bias[1:2, :]
+        state2[s] = state
+        result_out[s] = state + bias[2:3, :]
+        gathered[n + streams, line.z, line.c] = norm(state, 2)
+
+    def row_sum(value):
+        return jnp.sum(value, axis=0, keepdims=True)
+
+    def owner_mlp(s, n):
+        grad = cotangent[s, line.h].astype(F32)
+        back, gain_grad, shift_grad = norm_back(state2[s], total[...], gain[2:3, :])
+        dh = grad + back
+        grad2[s] = dh
+        gathered[n + streams, line.z, line.c] = dh.astype(BF16)
+        small_out[0:1] += gain_grad
+        small_out[1:2] += shift_grad
+        small_out[2:3] += row_sum(grad)
+        small_out[3:4] += row_sum(dh)
+
+    def owner_back(s, n):
+        back, gain_grad, shift_grad = norm_back(state1[s].astype(F32), total[...], gain[1:2, :])
+        dh = grad2[s] + back
+        grad1[s] = dh.astype(BF16)
+        small_out[4:5] += gain_grad
+        small_out[5:6] += shift_grad
+        small_out[6:7] += row_sum(dh)
+
+    def by_phase(bodies):
+        def run(n):
+            for i, one in enumerate(bodies):
+
+                @pl.when(n // streams == i)
+                def _():
+                    one(n % streams, n)
+
+        return run
+
+    every, after, all_steps = pipeline_steps(chips, items, streams)
+    mlp_turn, back_turn = after(2 * streams - 1), after(3 * streams - 1)
+    n_stages = reduced[0].stages()
+    begin = mlp_turn * every + every - 1
+    moments = [begin, begin + 10, begin + 16] + [begin + 21 + 4 * i for i in range(n_stages)]
+    moments = [t for t in moments[: n_stages - 1] if t < all_steps]
+    all_tokens = streams * count
+
+    def mlp_grads(which):
+        def down_body(i, carry):
+            cols = pl.ds(pl.multiple_of(i * 128, 128), 128)
+            left = act_ref[:, :, cols].reshape(all_tokens, 128)
             right = cotangent[...].reshape(all_tokens, width)
-            down_grad[cols] = mm_tn(left, right).astype(BF16)
-
-        @pl.when((t >= first + n_down) & (t < first + n_down + n_up))
-        def _():
-            cols = pl.ds(pl.multiple_of((t - first - n_down) * 256, 256), 256)
-            left = normed_out[:, :, :, :, cols].reshape(all_tokens, 256)
-            right = dpre_out[...].reshape(all_tokens, hidden)
-            up_grad[cols] = mm_tn(left, right).astype(BF16)
-
-    gathered_sum(
-        line, gather, sums, own, compute, total, beside, first + n_down + n_up
-    )
-    tokens = steps * rows
-    start = pl.multiple_of(line.h * rows, rows)
-    state = state2[...]
-    grad = cotangent[:, pl.ds(start, rows)].astype(F32).reshape(tokens, width)
-    back, gain_grad, shift_grad = norm_back(
-        state, total[:, pl.ds(0, rows)].reshape(tokens, width), gain[2:3, :]
-    )
-    dh = grad + back
-    grad_out[...] = dh
-    got = swap.run(mm(to_peers[...], dh.astype(BF16)).astype(BF16))
-    next_out[...] = mm(to_parts[...], got).astype(BF16).reshape(next_out.shape)
-    result = state + total[:, pl.ds(rows, rows)].reshape(tokens, width) + bias[2:3, :]
-    result_out[...] = result.astype(BF16).reshape(result_out.shape)
-    small_out[...] = jnp.concatenate(
-        [
-            gain_grad,
-            shift_grad,
-            jnp.sum(grad, axis=0, keepdims=True),
-            jnp.sum(dh, axis=0, keepdims=True),
-            jnp.zeros((4, width), F32),
-        ],
-        axis=0,
-    )
-    drain_all(line, (gather, sums))
-
-
-def temporal_backward(
-    segments, own, qkv, wqkv, wout, gain, state1, grad2, from_parts, from_peers,
-    normed, mixed, down_part, up_part,
-    qk_grad, v_grad, out_grad, down_grad, up_grad, grad_out, next_out, small_out,
-    grad_gathered, dqkv_out, load_sems,
-    part, sib, rise, fall, out, src, dst, total, mask_ref, *sems,
-):
-    steps, chips, _, rows, width = grad_gathered.shape
-    line = Line(sems, steps)
-    reduced = frame_sums(line, [(down_grad, 0, False), (up_grad, 0, True)], sems[12:])
-    loads = [
-        pltpu.make_async_copy(down_part, reduced[0].part, load_sems.at[0]),
-        pltpu.make_async_copy(up_part, reduced[1].part, load_sems.at[1]),
-    ]
-    for load in loads:
-        load.start()
-    sums = ChainSum(line, (part, sib, rise, fall, out), sems[:5])
-    gather = Gather(line, grad_gathered, sems[5:10])
-    swap = Swap(line, (src, dst), sems[10:12])
-    line.barrier(True)
-    mask_ref[...] = frame_mask(segments, 2 * rows).astype(F32)
-
-    def compute(s, zb):
-        r = grad_gathered[s, zb].reshape(2 * rows, width)
-        dm = mm_nt(r, wout[...]).astype(BF16)
-        mask = mask_ref[...] > 0.0
-        dq, dk, dv = attend_back(qkv[0, s, zb], qkv[1, s, zb], qkv[2, s, zb], mask, dm)
-        dqkv_out[0, s, zb] = dq
-        dqkv_out[1, s, zb] = dk
-        dqkv_out[2, s, zb] = dv
-        da = mm_nt(dq, wqkv[0]) + mm_nt(dk, wqkv[1]) + mm_nt(dv, wqkv[2])
-        part[s, zb] = da.astype(BF16).reshape(2, rows, width)
-
-    columns = wout.shape[0]
-    all_tokens = steps * chips * 2 * rows
-    first = steps * chips + 1
-    n_cols = width // 256
-    n_stages = reduced[0].stages()
-
-    def beside(t):
-        for k in range(n_stages - 1):
-
-            @pl.when(t == (1, 9, 13, 17)[min(k, 3)] + 4 * max(k - 3, 0))
-            def _():
-                if k == 0:
-                    for load in loads:
-                        load.wait()
-                for one in reduced:
-                    one.stage(k)
-
-        @pl.when(t == first)
-        def _():
-            left = mixed[...].reshape(all_tokens, columns)
-            right = grad_gathered[...].reshape(all_tokens, width)
+            reduced[0].part[cols] = mm_tn(left, right).astype(BF16)
+            return carry
+
+        def up_body(i, carry):
+            cols = pl.ds(pl.multiple_of(i * 256, 256), 256)
+            left = gathered[streams : 2 * streams, :, :, :, cols].reshape(all_tokens, 256)
+            right = dpre_ref[...].reshape(all_tokens, hidden)
+            reduced[1].part[cols] = mm_tn(left, right).astype(BF16)
+            return carry
+
+        if which == 0:
+            lax.fori_loop(0, hidden // 128, down_body, 0)
+        else:
+            lax.fori_loop(0, width // 256, up_body, 0)
+
+    def attention_grads(which):
+        if which == 0:
+            left = mixed_ref[...].reshape(all_tokens, columns)
+            right = gathered[2 * streams : 3 * streams].reshape(all_tokens, width)
             out_grad[...] = mm_tn(left, right).astype(BF16)
-
-        @pl.when((t > first) & (t <= first + n_cols))
-        def _():
-            qkv_grads(
-                (t - first - 1) * 256, normed, dqkv_out, qk_grad, v_grad, all_tokens, columns
-            )
-
-    gathered_sum(line, gather, sums, own, compute, total, beside, first + n_cols + 1)
-    tokens = steps * rows
-    summed = total[...].reshape(tokens, width).astype(BF16)
-    got = swap.run(mm(from_parts[...], summed).astype(BF16))
-    back, gain_grad, shift_grad = norm_back(state1[...], mm(from_peers[...], got), gain[1:2, :])
-    dh = grad2[...] + back
-    grad_out[...] = dh
-    next_out[...] = dh.astype(BF16).reshape(next_out.shape)
-    small_out[...] = jnp.concatenate(
-        [
-            gain_grad,
-            shift_grad,
-            jnp.sum(dh, axis=0, keepdims=True),
-            jnp.zeros((5, width), F32),
-        ],
-        axis=0,
-    )
-    for one in reduced:
-        one.stage(n_stages - 1)
-    drain_all(line, (gather, sums))
-
-
-def qkv_grads(start, normed, dqkv, qk_grad, v_grad, all_tokens, columns):
-    width = normed.shape[-1]
-    cols = pl.ds(pl.multiple_of(start, 256), 256)
-    lead = (slice(None),) * (len(normed.shape) - 1)
-    left = normed[lead + (cols,)].reshape(all_tokens, 256)
+        else:
+
+            def body(i, carry):
+                start = i * 256
+                cols = pl.ds(pl.multiple_of(start, 256), 256)
+                left = gathered[0:streams, :, :, :, cols].reshape(all_tokens, 256)
+                qkv_grads(start, left, dqkv, qk_grad, v_grad)
+                return carry
+
+            lax.fori_loop(0, width // 256, body, 0)
+
+    def beside(t, i):
+        for turn, grads in ((mlp_turn, mlp_grads), (back_turn, attention_grads)):
+            for which, step in ((0, every // 2), (1, every - 1)):
+                if i == step:
+
+                    @pl.when(t == turn * every + step)
+                    def _():
+                        grads(which)
+
+        for k, moment in enumerate(moments):
+            if moment % every == i:
+
+                @pl.when(t == moment)
+                def _():
+                    for one in reduced:
+                        one.stage(k)
+
+    def compute(n):
+        by_phase((compute_temporal, compute_mlp, compute_back))(n)
+
+    def owner(n):
+        by_phase((owner_temporal, owner_mlp, owner_back))(n)
+
+    pipeline(line, gather, sums, items, streams, compute, owner, total, beside)
+    tokens = streams * rows
+    own = grad1[...].reshape(tokens, width)
+    got = swap.run(mm(from_parts[...], own).astype(BF16))
+    next_out[...] = mm(from_peers[...], got).astype(BF16).reshape(next_out.shape)
+    for k in range(len(moments), n_stages):
+        for one in reduced:
+            one.stage(k)
+    drain_all(line, (gather, sums), items)
+
+
+def qkv_grads(start, left, dqkv, qk_grad, v_grad):
+    all_tokens, width = left.shape[0], v_grad.shape[0]
     for i in range(3):
-        grad = mm_tn(left, dqkv[i].reshape(all_tokens, columns)).astype(BF16)
+        grad = mm_tn(left, dqkv[i].reshape(all_tokens, dqkv.shape[-1])).astype(BF16)
         if i < 2:
             qk_grad[pl.ds(pl.multiple_of(i * width + start, 256), 256)] = grad
         else:
-            v_grad[cols] = grad
+            v_grad[pl.ds(pl.multiple_of(start, 256), 256)] = grad
 
 
 def spatial_backward(
-    ids, own, qkv, wqkv, wout, gain, x, table, grad1,
-    normed, mixed, small2, small3, up_bias_part, t_qk_part, t_v_part, t_out_part,
-    t_qk_grad, t_v_grad, t_out_grad, qk_grad, v_grad, out_grad, result_out, small_out,
+    ids, own, qkv, wqkv, wout, gain, x, table, normed, mixed, small2, up_bias_part, y_base,
+    from_parts, from_peers, y_part, t_qk_part, t_v_part, t_out_part,
+    t_qk_grad, t_v_grad, t_out_grad, qk_grad, v_grad, out_grad, y_out, result_out, small_out,
     grad_gathered, dqkv_out, load_sems, every_src, every_sib, every_line, every_frames, every_sent,
     every_got,
-    part, sib, rise, fall, out, total, dmixed, *sems,
+    part, sib, rise, fall, out, y_part_ref, y_sib, y_rise, y_fall, y_sums, src, dst, y_total, total,
+    dmixed, *sems,
 ):
     steps, chips, _, rows, width = grad_gathered.shape
-    line = Line(sems, steps)
+    line = Line(steps)
+    sums = ChainSum(line, (part, sib, rise, fall, out), sems[:5])
+    gather = Gather(line, grad_gathered, sems[5:10])
+    y_line = Line(y_part_ref.shape[0])
+    y_chain = ChainSum(y_line, (y_part_ref, y_sib, y_rise, y_fall, y_sums), sems[10:15])
+    swap = Swap(line, (src, dst), sems[15:17])
     reduced = frame_sums(
         line,
         [
             (t_qk_grad, 0, False), (t_v_grad, 0, True), (t_out_grad, 1, True),
             (qk_grad, 0, False), (v_grad, 0, True), (out_grad, 1, True),
         ],
-        sems[10:],
+        sems[17:],
     )
     earlier, later = reduced[:3], reduced[3:]
     loads = [
-        pltpu.make_async_copy(t_qk_part, earlier[0].part, load_sems.at[0]),
-        pltpu.make_async_copy(t_v_part, earlier[1].part, load_sems.at[1]),
-        pltpu.make_async_copy(t_out_part, earlier[2].part, load_sems.at[2]),
+        pltpu.make_async_copy(y_part, y_part_ref, load_sems.at[0]),
+        pltpu.make_async_copy(t_qk_part, earlier[0].part, load_sems.at[1]),
+        pltpu.make_async_copy(t_v_part, earlier[1].part, load_sems.at[2]),
+        pltpu.make_async_copy(t_out_part, earlier[2].part, load_sems.at[3]),
     ]
     for load in loads:
         load.start()
     n_stages = earlier[0].stages()
     every = Everyone(line, (every_src, every_sib, every_line, every_frames), (every_sent, every_got))
-    sums = ChainSum(line, (part, sib, rise, fall, out), sems[:5])
-    gather = Gather(line, grad_gathered, sems[5:10])
     line.barrier(True, True)
     entries = table.shape[0]
     table_row = lax.broadcasted_iota(jnp.int32, (entries, width), 0)
     gather.start(own)
+    loads[0].wait()
+
+    def y_across(i, carry):
+        y_chain.across(i // chips, i % chips).start()
+        return carry
+
+    lax.fori_loop(0, y_line.steps * chips, y_across, 0)
     parts = steps * chips
 
     def body(t, carry):
-        @pl.when(t < parts)
-        def _():
-            gather.arrive(t // steps, t % steps)
+        for distance in range(1, chips):
+
+            @pl.when(t // steps == distance)
+            def _():
+                gather.arrive(distance, t % steps)
 
         def side(upward, inner):
             u = jnp.maximum(t - 1, 0)
             away, s = u // steps, u % steps
             zb = jnp.where(upward == 1, line.z + away, line.z - away)
-            ok = (t >= 1) & (zb >= 0) & (zb < chips) & ((away > 0) | (upward == 0))
+            ok = (t >= 1) & (t <= parts) & (zb >= 0) & (zb < chips)
+            ok = ok & ((away > 0) | (upward == 0))
 
             @pl.when(ok)
             def _():
@@ -953,21 +994,23 @@
             return inner
 
         lax.fori_loop(0, 2, side, 0)
+        y_chain.hops(t - 2)
         for k in range(n_stages):
 
             @pl.when(t == (1, 6, 9, 12, 16)[min(k, 4)] + 2 * max(k - 4, 0))
             def _():
                 if k == 0:
-                    for load in loads:
+                    for load in loads[1:]:
                         load.wait()
                 for one in earlier:
                     one.stage(k)
 
         return carry
 
-    lax.fori_loop(0, max(parts + 1, 17 + 2 * max(n_stages - 5, 0)), body, 0)
+    y_bound = 2 + y_line.steps * (chips - 1) + (chips - 2) * LAG
+    lax.fori_loop(0, max(parts + 1, 17 + 2 * max(n_stages - 5, 0), y_bound), body, 0)
     columns = wout.shape[0]
-    all_tokens = steps * chips * 2 * rows
+    all_tokens = parts * 2 * rows
 
     def compute(s):
         dq, dk, dv = attend_back(qkv[0, s], qkv[1, s], qkv[2, s], None, dmixed[s])
@@ -988,18 +1031,25 @@
         def _():
             for i in range(width // 512):
                 start = ((t - steps) * (width // 512) + i) * 256
-                qkv_grads(
-                    start, normed, dqkv_out, later[0].part, later[1].part, all_tokens, columns
-                )
+                cols = pl.ds(pl.multiple_of(start, 256), 256)
+                left = normed[:, :, cols].reshape(all_tokens, 256)
+                qkv_grads(start, left, dqkv_out, later[0].part, later[1].part)
 
         for k in range(n_stages - 1):
-
-            @pl.when(t == (steps + 1, steps + 5, steps + 7, steps + 9)[min(k, 3)] + 2 * max(k - 3, 0))
+            moment = steps + (1, 5, 7, 9)[min(k, 3)] + 2 * max(k - 3, 0)
+
+            @pl.when(t == moment)
             def _():
                 for one in later:
                     one.stage(k)
 
     computed_sum(line, sums, compute, total, beside)
+    for s in range(y_line.steps):
+        y_chain.finish(s, y_total.at[s])
+    tokens = steps * rows
+    result = (y_base[...] + y_total[...]).astype(BF16).reshape(tokens, width)
+    swap.src[...] = mm(from_parts[...], result).astype(swap.src.dtype).reshape(swap.src.shape)
+    swap.start()
     gain_grad = jnp.zeros((1, width), F32)
     shift_grad = jnp.zeros((1, width), F32)
     table_grad = jnp.zeros((entries, width), F32)
@@ -1008,16 +1058,16 @@
         added = jnp.sum(picked, axis=0, keepdims=True)
         state = x[s, pl.ds(pl.multiple_of(line.h * rows, rows), rows)].astype(F32) + added
         back, one_gain, one_shift = norm_back(state, total[s], gain[0:1, :])
-        grad = grad1[pl.ds(s * rows, rows)] + back
-        result_out[s] = grad
+        grad = own[s].astype(F32) + back
+        result_out[pl.ds(s * rows, rows)] = grad
         gain_grad += one_gain
         shift_grad += one_shift
         here = jnp.sum(grad, axis=0, keepdims=True)
         table_grad += jnp.where(table_row == ids[s], here, 0.0)
     rows_of = [
-        gain_grad, small2[0:1], small3[0:1],
-        shift_grad, small2[1:2], small3[1:2],
-        small2[2:3], small3[3:4], small3[2:3],
+        gain_grad, small2[4:5], small2[0:1],
+        shift_grad, small2[5:6], small2[1:2],
+        small2[6:7], small2[3:4], small2[2:3],
         table_grad,
     ]
     filled = 9 + entries
@@ -1026,9 +1076,76 @@
     row = lax.broadcasted_iota(jnp.int32, (room, width), 0)
     frames_value = jnp.where(row == filled, up_bias_part[...], 0.0)
     small_out[...] = every.run(value, frames_value)
+    swap.wait()
+    got = swap.dst[...].reshape(tokens, width).astype(BF16)
+    y_out[...] = mm(from_peers[...], got).astype(BF16)
     for one in later:
         one.stage(n_stages - 1)
-    drain_all(line, (gather, sums))
+    drain_all(line, (gather, sums), steps)
+    drain_all(y_line, (y_chain,), y_line.steps)
+
+
+def finish(
+    t_qk, t_v, t_out, s_qk, s_v, s_out, up, down, y, grad, small,
+    y_res, grad_res, table_res, gain_res, shift_res, s_qkv_res, s_out_res, t_qkv_res, t_out_res,
+    bias_res, up_res, up_bias_res, down_res,
+):
+    for qk, v, res in ((t_qk, t_v, t_qkv_res), (s_qk, s_v, s_qkv_res)):
+        res[0:2] = qk[...].astype(F32)
+        res[2] = v[...].astype(F32)
+    t_out_res[...] = t_out[...].astype(F32)
+    s_out_res[...] = s_out[...].astype(F32)
+    up_res[...] = up[...].astype(F32)
+    down_res[...] = down[...].astype(F32)
+    y_res[...] = y[...]
+    grad_res[...] = grad[...]
+
+    @pl.when(pl.program_id(0) == 0)
+    def _():
+        entries = table_res.shape[0]
+        gain_res[...] = small[0:3]
+        shift_res[...] = small[3:6]
+        bias_res[...] = small[6:9]
+        table_res[...] = small[9 : 9 + entries]
+        up_bias_res[...] = small[9 + entries : 10 + entries, : up_bias_res.shape[1]]
+
+
+def results(values, entries, hidden):
+    grid = 8
+
+    def blocks(shape, sliced=True):
+        axis = len(shape) - 2
+        block = list(shape)
+        if sliced:
+            block[axis] //= grid
+        place = [0] * len(shape)
+
+        def index(i):
+            at = list(place)
+            if sliced:
+                at[axis] = i
+            return tuple(at)
+
+        return pl.BlockSpec(tuple(block), index)
+
+    t_qk, t_v, t_out, _, _, _, g_up, g_down, y, grad, small = values
+    width = g_up.shape[0]
+    qkv = ((3,) + t_qk.shape[1:], F32, True)
+    out = (t_out.shape, F32, True)
+    few = ((3, width), F32, False)
+    outs = [
+        (y.shape, BF16, True), (grad.shape, F32, True), ((entries, width), F32, False), few, few,
+        qkv, out, qkv, out, few,
+        (g_up.shape, F32, True), ((1, hidden), F32, False), (g_down.shape, F32, True),
+    ]
+    return pl.pallas_call(
+        finish,
+        name="finish",
+        grid=(grid,),
+        out_shape=[jax.ShapeDtypeStruct(shape, kind) for shape, kind, _ in outs],
+        in_specs=[blocks(v.shape, v is not small) for v in values],
+        out_specs=[blocks(shape, sliced) for shape, _, sliced in outs],
+    )(*values)
 
 
 def orders(frames_local, frames, places, t_steps):
@@ -1073,14 +1190,15 @@
     s_qkv = spatial_qkv.transpose(1, 0, 2)
     t_qkv = temporal_qkv.transpose(1, 0, 2)
     to_peers, to_parts, from_parts, from_peers = orders(steps, frames, places, t_steps)
-    swap = swap_bufs(frames, tokens // frames, width)
-    owned = ((tokens, width), F32)
+    swap = swap_bufs(frames, (tokens // frames, width))
     s_blocks = (steps, rows, width)
     t_blocks = (t_steps, t_rows, width)
-    t_mask = pltpu.VMEM((2 * t_rows, 2 * t_rows), F32)
-    rest = 8, width
-
-    normed1, s_proj, s_mixed, state1, own2 = call(
+    s_all = (steps, chips, 2, rows, width)
+    count = heads * t_rows
+    s_scratch = [pltpu.VMEM(s_blocks, F32)]
+    t_scratch = [pltpu.VMEM(t_blocks, F32)]
+
+    normed1, s_proj, s_mixed, state1, g_all = call(
         spatial_forward,
         "spatial_forward",
         0,
@@ -1088,143 +1206,127 @@
             ((steps, patches, width), BF16),
             ((3, steps, patches, columns), BF16),
             ((steps, patches, columns), BF16),
-            owned,
             (t_blocks, BF16),
+            ((t_steps, heads, t_rows, width), BF16),
         ],
         sum_bufs(steps, chips, rows, width)
         + swap
-        + [pltpu.VMEM(s_blocks, F32), pltpu.VMEM(s_blocks, F32)]
-        + sem_shapes(steps, chips, False, frames),
+        + s_scratch * 2
+        + swap_bufs(frames, (heads, tokens // frames, width))
+        + chain_sems(steps, chips)
+        + swap_sems(frames) * 2,
         (
             action_ids, block_input, action_table, norm_gain, norm_shift, out_bias,
-            s_qkv, spatial_out, to_peers, to_parts,
+            s_qkv, spatial_out, cotangent, to_peers, to_parts,
         ),
         smem=(0,),
     )
-    t_all = (t_steps, chips, 2, t_rows, width)
-    t_cols = (t_steps, chips, 2 * t_rows, columns)
-    normed2, t_proj, t_mixed, state2, own3 = call(
-        temporal_forward,
-        "temporal_forward",
-        1,
-        [
-            (t_all, BF16),
-            ((3,) + t_cols, BF16),
-            (t_cols, BF16),
-            owned,
-            (s_blocks, BF16),
-        ],
-        sum_bufs(t_steps, chips, t_rows, width)
-        + swap
-        + [pltpu.VMEM(t_blocks, F32), t_mask]
-        + sem_shapes(t_steps, chips, True, frames),
-        (
-            segment_ids, own2, t_qkv, temporal_out, norm_gain, norm_shift, out_bias,
-            state1, from_parts, from_peers,
-        ),
-        smem=(0,),
-    )
-    s_all = (steps, chips, 2, rows, width)
-    f_cols = (steps, chips, 2 * rows, hidden)
+    items = 3 * t_steps
     grads_mlp = [((hidden, width), BF16), ((width, hidden), BF16)]
-    down_part, up_part, block_output, grad2, own4, small3, up_bias_part = call(
-        mlp,
-        "mlp",
-        2,
-        grads_mlp
-        + [
-            (s_blocks, BF16),
-            owned,
-            (t_blocks, BF16),
-            (rest, F32),
-            ((1, hidden), F32),
-        ],
-        [pltpu.VMEM(s_all, BF16), pltpu.VMEM(f_cols, BF16), pltpu.VMEM(f_cols, BF16)]
-        + sum_bufs(steps, chips, rows, width, 2)
-        + swap
-        + [pltpu.VMEM((steps, 2 * rows, width), F32)]
-        + sem_shapes(steps, chips, True, frames),
-        (
-            own3, up_weight, up_bias.reshape(1, hidden), down_weight, cotangent, norm_gain,
-            out_bias, state2, to_peers, to_parts,
-        ),
-    )
     grads_attention = [
         ((2 * width, columns), BF16),
         ((width, columns), BF16),
         ((columns, width), BF16),
     ]
     dims_attention = (0, 0, 1)
-    t_qk_part, t_v_part, t_out_part, g_down, g_up, grad1, own5, small2 = call(
-        temporal_backward,
-        "temporal_backward",
-        3,
-        grads_attention + grads_mlp + [owned, (s_blocks, BF16), (rest, F32)],
+    t_cols = pltpu.VMEM((t_steps, count, columns), BF16)
+    f_cols = pltpu.VMEM((t_steps, count, hidden), BF16)
+    qkv_cols = pltpu.VMEM((3, t_steps, count, columns), BF16)
+    (
+        g_down, g_up, t_qk_part, t_v_part, t_out_part, y_part, y_base, own, small2, up_bias_part,
+    ) = call(
+        middle,
+        "middle",
+        1,
+        grads_mlp
+        + grads_attention
+        + [
+            ((t_steps, chips, 2, t_rows, width), BF16),
+            (t_blocks, F32),
+            (s_blocks, BF16),
+            ((8, width), F32),
+            ((1, hidden), F32),
+        ],
         [
-            pltpu.VMEM(t_all, BF16),
-            pltpu.VMEM((3,) + t_cols, BF16),
-            pltpu.SemaphoreType.DMA((2,)),
+            pltpu.VMEM((items, chips, 2, t_rows, width), BF16),
+            qkv_cols, t_cols, f_cols, f_cols, qkv_cols,
+            pltpu.VMEM(t_blocks, F32), pltpu.VMEM(t_blocks, F32), pltpu.VMEM(t_blocks, BF16),
+            pltpu.VMEM((count, count), F32),
         ]
-        + sum_bufs(t_steps, chips, t_rows, width)
+        + sum_bufs(items, chips, t_rows, width)
         + swap
-        + [pltpu.VMEM(t_blocks, F32), t_mask]
-        + sem_shapes(t_steps, chips, True, frames)
+        + [pltpu.VMEM((t_rows, width), F32)]
+        + chain_sems(items, chips) * 2
+        + swap_sems(frames)
         + [x for shape, _ in grads_mlp for x in frame_sum_scratch(frames, shape, 0)],
         (
-            segment_ids, own4, t_proj, t_qkv, temporal_out, norm_gain, state1, grad2,
-            from_parts, from_peers, normed2, t_mixed, down_part, up_part,
+            segment_ids, state1, g_all, t_qkv, temporal_out, up_weight, up_bias.reshape(1, hidden),
+            down_weight, norm_gain, norm_shift, out_bias, from_parts, from_peers,
         ),
         smem=(0,),
-        left=(12, 13),
     )
     room = -(-(10 + action_table.shape[0]) // 16) * 16
     up_bias_row = jnp.pad(up_bias_part, ((0, 0), (0, width - hidden)))
-    g_t_qk, g_t_v, g_t_out, g_s_qk, g_s_v, g_s_out, input_grad, small = call(
+    t_qk, t_v, t_out, s_qk, s_v, s_out, y, input_grad, small = call(
         spatial_backward,
         "spatial_backward",
-        4,
-        grads_attention * 2 + [(s_blocks, F32), ((room, width), F32)],
+        2,
+        grads_attention * 2
+        + [((tokens, width), BF16), ((tokens, width), F32), ((room, width), F32)],
         [
             pltpu.VMEM(s_all, BF16),
             pltpu.VMEM((3, steps, patches, columns), BF16),
-            pltpu.SemaphoreType.DMA((3,)),
+            pltpu.SemaphoreType.DMA((4,)),
         ]
         + everyone_scratch(chips, frames, room, width)
         + sum_bufs(steps, chips, rows, width)
-        + [pltpu.VMEM(s_blocks, F32), pltpu.VMEM((steps, patches, columns), BF16)]
-        + sem_shapes(steps, chips, True, 0)
+        + sum_bufs(t_steps, chips, t_rows, width)
+        + swap
+        + t_scratch
+        + s_scratch
+        + [pltpu.VMEM((steps, patches, columns), BF16)]
+        + chain_sems(steps, chips) * 2
+        + chain_sems(t_steps, chips)
+        + swap_sems(frames)
         + [
             x
             for (shape, _), dim in zip(grads_attention * 2, dims_attention * 2)
             for x in frame_sum_scratch(frames, shape, dim)
         ],
         (
-            action_ids, own5, s_proj, s_qkv, spatial_out, norm_gain, block_input, action_table,
-            grad1, normed1, s_mixed, small2, small3, up_bias_row, t_qk_part, t_v_part, t_out_part,
+            action_ids, own, s_proj, s_qkv, spatial_out, norm_gain, block_input, action_table,
+            normed1, s_mixed, small2, up_bias_row, y_base, from_parts, from_peers,
+            y_part, t_qk_part, t_v_part, t_out_part,
         ),
         smem=(0,),
-        left=(14, 15, 16),
+        left=(15, 16, 17, 18),
     )
-
-    def qkv_of(qk, v):
-        whole = jnp.concatenate([qk, v], axis=0).reshape(3, width, columns)
-        return whole.transpose(1, 0, 2).astype(F32)
-
-    filled = 9 + action_table.shape[0]
+    (
+        block_output, input_grad, table_grad, gain_grad, shift_grad, s_qkv_grad, s_out_grad,
+        t_qkv_grad, t_out_grad, bias_grad, up_grad, up_bias_grad, down_grad,
+    ) = results(
+        [
+            t_qk.reshape(2, width, columns), t_v, t_out,
+            s_qk.reshape(2, width, columns), s_v, s_out,
+            g_up, g_down, y, input_grad, small,
+        ],
+        action_table.shape[0],
+        hidden,
+    )
     return (
-        block_output,
-        input_grad,
-        small[9:filled],
-        small[0:3],
-        small[3:6],
-        qkv_of(g_s_qk, g_s_v),
-        g_s_out.astype(F32),
-        qkv_of(g_t_qk, g_t_v),
-        g_t_out.astype(F32),
-        small[6:9],
-        g_up.astype(F32),
-        small[filled, :hidden],
-        g_down.astype(F32),
+        block_output.reshape(s_blocks),
+        input_grad.reshape(s_blocks),
+        table_grad,
+        gain_grad,
+        shift_grad,
+        s_qkv_grad.transpose(1, 0, 2),
+        s_out_grad,
+        t_qkv_grad.transpose(1, 0, 2),
+        t_out_grad,
+        bias_grad,
+        up_grad,
+        up_bias_grad.reshape(hidden),
+        down_grad,
     )
 
 

time: 306 us -> 283 us (0.925)
  Pallas kernels: 292 us -> 281 us
  other arithmetic: 8.82 us -> 0 us
    pallas_call x5 -> x3, Pallas kernels: 292 us -> 272 us  [call(): pl.pallas_call(kernel, name=name, out_shape=[jax.ShapeDtypeStruct(shape,...]
    pallas_call x0 -> x1, Pallas kernels: none -> 8.31 us  [results(): pl.pallas_call(finish, name='finish', grid=(grid,), out_shape=[jax.ShapeD...]
    convert_element_type x6 -> x0, other arithmetic: 7.35 us -> none  [the longest x2 2.49 us: qkv_of(): return whole.transpose(1, 0, 2).astype(F32)]
where the time goes in v2:
time: 283 us
  Pallas kernels  281 us (99%)
    pallas_call x3, Pallas kernels, call(): pl.pallas_call(kernel, name=name, out_shape=[jax.ShapeDtypeStruct(shape,...  272 us
    pallas_call x1, Pallas kernels, results(): pl.pallas_call(finish, name='finish', grid=(grid,), out_shape=[jax.ShapeD...  8.31 us

profile of v2, /device:TPU:0, one launch (start us, length us, event | category | flops | bytes accessed | tf_op | source)
XLA Modules:
  0.0 282.7 jit_solution(6249704449329439917)
XLA Ops:
  0.6 40.3 %spatial_forward.1 = (bf16[4,256,1024]{2,1,0:T(8,128)(2,1)}, bf16[3,4,256,128]{3,2,1,0:T(8,128)(2,1)}, bf16[4,256,128]{2,1,0:T(8,128)(2,1)}, bf16[4,32,1024]{2,1,0:T(8,128)(2,1)}, bf16[4,8,32,1024]{3,2,1,0:T(8,128)(2,1)}) custom-call(s32[4]{0:T(128)} %ids.3, bf16[4,256,1024]{2,1,0:T(8,128)(2,1)} %x.5, bf16[8,1024]{1,0:T(8,128)(2,1)} %table.3, ...), custom_call_target="tpu_custom_call" | custom-call | tf_op jit(solution)/shard_map/spatial_forward/pallas_call | solution.py:643
  40.9 150.7 %middle.1 = (bf16[512,1024]{1,0:T(8,128)(2,1)}, bf16[1024,512]{1,0:T(8,128)(2,1)}, bf16[2048,128]{1,0:T(8,128)(2,1)}, bf16[1024,128]{1,0:T(8,128)(2,1)}, bf16[12...) custom-call(s32[16]{0:T(128)} %segments.1, ...), custom_call_target="tpu_custom_call" | custom-call | tf_op jit(solution)/shard_map/middle/pallas_call | solution.py:643
  191.6 1.2 pad.4.up_bias_part
  192.8 81.4 %spatial_backward.1 = (bf16[2048,128]{1,0:T(8,128)(2,1)}, bf16[1024,128]{1,0:T(8,128)(2,1)}, bf16[128,1024]{1,0:T(8,128)(2,1)}, bf16[2048,128]{1,0:T(8,128)(2,1)...) custom-call(s32[4]{0:T(128)} %ids.3, ...), custom_call_target="tpu_custom_call" | custom-call | tf_op jit(solution)/shard_map/spatial_backward/pallas_call | solution.py:643
  274.2 8.3 %finish.1 = (bf16[128,1024]{1,0:T(8,128)(2,1)}, f32[128,1024]{1,0:T(8,128)}, f32[8,1024]{1,0:T(8,128)}, f32[3,1024]{1,0:T(4,128)}, f32[3,1024]{1,0:T(4,128)}, /*...) custom-call(bf16[2,1024,128]{2,1,0:T(8,128)(2,1)} %bitcast.13, ...), custom_call_target="tpu_custom_call" | custom-call | tf_op jit(solution)/shard_map/finish/pallas_call | solution.py:1141

commit v3 on v2

v3 whole, which is shorter than its diff:
```python
import jax
import jax.numpy as jnp
import numpy as np
from jax import lax
from jax.experimental import pallas as pl
from jax.experimental.pallas import tpu as pltpu
from jax.sharding import PartitionSpec as P

HD = 64
SCALE = HD**-0.5
EPS = 1e-05
MASKED = -1000000000.0
F32 = jnp.float32
BF16 = jnp.bfloat16
MESH = pl.DeviceIdType.MESH
VMEM_LIMIT = 62 * 1024 * 1024
GELU_C = float(np.sqrt(2.0 / np.pi))
LAG = 2
HOP = 3
SLACK = 2


def mm(a, b):
    return lax.dot_general(a, b, (((1,), (0,)), ((), ())), preferred_element_type=F32)


def mm_nt(a, b):
    return lax.dot_general(a, b, (((1,), (1,)), ((), ())), preferred_element_type=F32)


def mm_tn(a, b):
    return lax.dot_general(a, b, (((0,), (0,)), ((), ())), preferred_element_type=F32)


def norm_stats(value):
    centered = value - jnp.mean(value, axis=-1, keepdims=True)
    inv = lax.rsqrt(jnp.mean(centered * centered, axis=-1, keepdims=True) + EPS)
    return centered * inv, inv


def norm_back(value, grad, gain):
    normed, inv = norm_stats(value)
    e = grad * gain
    first = jnp.mean(e, axis=-1, keepdims=True)
    second = jnp.mean(e * normed, axis=-1, keepdims=True)
    gain_grad = jnp.sum(grad * normed, axis=0, keepdims=True)
    shift_grad = jnp.sum(grad, axis=0, keepdims=True)
    return (e - first - normed * second) * inv, gain_grad, shift_grad


def head_lanes(shape, head):
    lane = lax.broadcasted_iota(jnp.int32, shape, 1)
    return (lane >= head * HD) & (lane < (head + 1) * HD)


def softmax_of(q, k, mask):
    scores = mm_nt(q, k) * SCALE
    if mask is not None:
        scores = jnp.where(mask, scores, MASKED)
    raised = jnp.exp(scores - jnp.max(scores, axis=-1, keepdims=True))
    return raised / jnp.sum(raised, axis=-1, keepdims=True)


def attend(q, k, v, mask):
    heads = q.shape[1] // HD
    mixed = None
    for head in range(heads):
        lanes = head_lanes(q.shape, head)
        probs = softmax_of(jnp.where(lanes, q, jnp.zeros_like(q)), k, mask).astype(BF16)
        out = mm(probs, v)
        mixed = out if mixed is None else jnp.where(lanes, out, mixed)
    return mixed.astype(BF16)


def attend_back(q, k, v, mask, grad):
    heads = q.shape[1] // HD
    dq = dk = dv = None
    for head in range(heads):
        lanes = head_lanes(q.shape, head)
        qh = jnp.where(lanes, q, jnp.zeros_like(q))
        gh = jnp.where(lanes, grad, jnp.zeros_like(grad))
        probs = softmax_of(qh, k, mask)
        dvh = mm_tn(probs.astype(BF16), gh)
        dp = mm_nt(gh, v)
        ds = (probs * (dp - jnp.sum(dp * probs, axis=-1, keepdims=True))).astype(BF16)
        dqh = mm(ds, k) * SCALE
        dkh = mm_tn(ds, qh) * SCALE
        if head == 0:
            dq, dk, dv = dqh, dkh, dvh
        else:
            dq = jnp.where(lanes, dqh, dq)
            dk = dk + dkh
            dv = dv + dvh
    return dq.astype(BF16), dk.astype(BF16), dv.astype(BF16)


class Line:
    def __init__(self, steps):
        self.frames = lax.axis_size("frames")
        self.heads = lax.axis_size("heads")
        self.chips = self.heads // 2
        self.f = lax.axis_index("frames")
        self.h = lax.axis_index("heads")
        self.z = self.h // 2
        self.c = self.h % 2
        self.steps = steps

    def at(self, z):
        return (self.f, jnp.clip(z, 0, self.chips - 1) * 2 + self.c)

    def sibling(self):
        return (self.f, self.z * 2 + 1 - self.c)

    def barrier(self, over_frames, whole_line=False):
        sem = pltpu.get_barrier_semaphore()

        def greet(device):
            pl.semaphore_signal(sem, inc=1, device_id=device, device_id_type=MESH)

        greet(self.sibling())
        count = 1
        if over_frames:
            for k in range(1, self.frames):
                greet(((self.f + k) % self.frames, self.h))
            count += self.frames - 1
        if whole_line:
            for k in range(1, self.chips):
                greet(self.at((self.z + k) % self.chips))
            count += self.chips - 1
        else:

            @pl.when(self.z > 0)
            def _():
                greet(self.at(self.z - 1))

            @pl.when(self.z < self.chips - 1)
            def _():
                greet(self.at(self.z + 1))

            count = count + (self.z > 0).astype(jnp.int32)
            count = count + (self.z < self.chips - 1).astype(jnp.int32)
        pl.semaphore_wait(sem, count)

    def copy(self, src, dst, send, recv, device):
        return pltpu.make_async_remote_copy(
            src_ref=src,
            dst_ref=dst,
            send_sem=send,
            recv_sem=recv,
            device_id=device,
            device_id_type=MESH,
        )


class Gather:
    def __init__(self, line, buf, sems):
        self.line, self.buf = line, buf
        self.got, self.got_sib, self.sent_up, self.sent_down, self.sent_sib = sems

    def up(self, s, zb):
        ln = self.line
        ref = self.buf.at[s, zb, ln.c]
        return ln.copy(ref, ref, self.sent_up.at[s, zb], self.got.at[s, zb], ln.at(ln.z + 1))

    def down(self, s, zb):
        ln = self.line
        ref = self.buf.at[s, zb, ln.c]
        return ln.copy(ref, ref, self.sent_down.at[s, zb], self.got.at[s, zb], ln.at(ln.z - 1))

    def across(self, s, zb):
        ln = self.line
        ref = self.buf.at[s, zb, ln.c]
        return ln.copy(ref, ref, self.sent_sib.at[s, zb], self.got_sib.at[s, zb], ln.sibling())

    def wait_across(self, s, zb):
        ln = self.line
        ref = self.buf.at[s, zb, 1 - ln.c]
        ln.copy(
            ref, ref, self.sent_sib.at[s, zb], self.got_sib.at[s, zb], ln.sibling()
        ).wait_recv()

    def send(self, s):
        ln = self.line

        @pl.when(ln.z < ln.chips - 1)
        def _():
            self.up(s, ln.z).start()

        @pl.when(ln.z > 0)
        def _():
            self.down(s, ln.z).start()

        self.across(s, ln.z).start()

    def start(self, own):
        ln = self.line
        for s in range(ln.steps):
            self.buf[s, ln.z, ln.c] = own[s]
            self.send(s)

    def arrive(self, distance, s):
        ln = self.line
        below, above = ln.z - distance, ln.z + distance

        @pl.when((distance > 0) & (below >= 0))
        def _():
            self.up(s, below).wait_recv()

            @pl.when(ln.z < ln.chips - 1)
            def _():
                self.up(s, below).start()

            self.across(s, below).start()

        @pl.when((distance > 0) & (above < ln.chips))
        def _():
            self.down(s, above).wait_recv()

            @pl.when(ln.z > 0)
            def _():
                self.down(s, above).start()

            self.across(s, above).start()

    def drain(self, s, zb):
        ln = self.line

        @pl.when((zb <= ln.z) & (ln.z < ln.chips - 1))
        def _():
            self.up(s, zb).wait_send()

        @pl.when((zb >= ln.z) & (ln.z > 0))
        def _():
            self.down(s, zb).wait_send()

        self.across(s, zb).wait_send()


class ChainSum:
    def __init__(self, line, bufs, sems):
        self.line = line
        self.part, self.sib, self.rise, self.fall, self.out = bufs
        self.sent_sib, self.got_sib, self.got_up, self.got_down, self.sent = sems

    def across(self, s, zb):
        ln = self.line
        return ln.copy(
            self.part.at[s, zb, 1 - ln.c],
            self.sib.at[s, zb],
            self.sent_sib.at[s, zb],
            self.got_sib.at[s, zb],
            ln.sibling(),
        )

    def up(self, s, o):
        ln = self.line
        return ln.copy(
            self.out.at[s, o],
            self.rise.at[s, o],
            self.sent.at[s, o],
            self.got_up.at[s, o],
            ln.at(ln.z + 1),
        )

    def down(self, s, o):
        ln = self.line
        return ln.copy(
            self.out.at[s, o],
            self.fall.at[s, o],
            self.sent.at[s, o],
            self.got_down.at[s, o],
            ln.at(ln.z - 1),
        )

    def mine(self, s, o):
        return self.part[s, o, self.line.c].astype(F32) + self.sib[s, o].astype(F32)

    def hop_up(self, s, o):
        ln = self.line
        self.across(s, o).wait_recv()

        @pl.when(ln.z == 0)
        def _():
            self.out[s, o] = self.mine(s, o).astype(BF16)

        @pl.when(ln.z > 0)
        def _():
            self.up(s, o).wait_recv()
            self.out[s, o] = (self.mine(s, o) + self.rise[s, o].astype(F32)).astype(BF16)

        self.up(s, o).start()

    def hop_down(self, s, o):
        ln = self.line
        self.across(s, o).wait_recv()

        @pl.when(ln.z == ln.chips - 1)
        def _():
            self.out[s, o] = self.mine(s, o).astype(BF16)

        @pl.when(ln.z < ln.chips - 1)
        def _():
            self.down(s, o).wait_recv()
            self.out[s, o] = (self.mine(s, o) + self.fall[s, o].astype(F32)).astype(BF16)

        self.down(s, o).start()

    def hops(self, t, part=None, fits=True):
        ln = self.line
        last = ln.chips - 1
        for upward in (True, False):
            place = ln.z if upward else last - ln.z
            q = t - place * LAG
            if part is None:
                turn = jnp.maximum(q, 0) // ln.steps
                s = jnp.maximum(q, 0) % ln.steps
            else:
                turn, s = jnp.maximum(q, 0), part
            far = jnp.clip(last - turn, 0, last)
            ok = (q >= 0) & (turn < last) & (far > place) & fits
            o = far if upward else last - far

            @pl.when(ok)
            def _():
                if upward:
                    self.hop_up(s, o)
                else:
                    self.hop_down(s, o)

    def finish(self, s, total):
        ln = self.line
        self.across(s, ln.z).wait_recv()
        total[...] = self.mine(s, ln.z)

        @pl.when(ln.z > 0)
        def _():
            self.up(s, ln.z).wait_recv()
            total[...] += self.rise[s, ln.z].astype(F32)

        @pl.when(ln.z < ln.chips - 1)
        def _():
            self.down(s, ln.z).wait_recv()
            total[...] += self.fall[s, ln.z].astype(F32)

    def drain(self, s, zb):
        ln = self.line
        self.across(s, zb).wait_send()

        @pl.when(zb != ln.z)
        def _():
            self.up(s, zb).wait_send()


def drain_all(line, things, parts):
    def body(i, carry):
        for thing in things:
            thing.drain(i // line.chips, i % line.chips)
        return carry

    lax.fori_loop(0, parts * line.chips, body, 0)


class Swap:
    def __init__(self, line, src_at, dst, sems):
        self.line, self.src_at, self.dst = line, src_at, dst
        self.sent, self.got = sems

    def copy(self, part, k):
        ln = self.line
        to = (ln.f + k) % ln.frames
        return ln.copy(
            self.src_at(part, to),
            self.dst.at[part, ln.f],
            self.sent.at[part, k],
            self.got.at[part, k],
            (to, ln.h),
        )

    def start(self, part):
        ln = self.line
        for k in range(1, ln.frames):
            self.copy(part, k).start()
        self.dst[part, ln.f] = self.src_at(part, ln.f)[...]

    def wait(self, part):
        for k in range(1, self.line.frames):
            self.copy(part, k).wait()


class FrameSum:
    def __init__(self, line, part, full, dim, reverse, recv_bufs, sems):
        self.line, self.part, self.full, self.dim = line, part, full, dim
        self.recv_bufs = recv_bufs
        self.sent, self.got, self.sent_back, self.got_back = sems
        bits = range(line.frames.bit_length() - 1)
        self.bits = list(reversed(bits)) if reverse else list(bits)
        self.spans = []
        start, size = 0, part.shape[dim]
        for bit in self.bits:
            size //= 2
            side = (line.f // (1 << bit)) % 2
            peer = (line.f + (1 - 2 * side) * (1 << bit), line.h)
            keep, give = start + side * size, start + (1 - side) * size
            self.spans.append((keep, give, size, peer))
            start = keep

    def view(self, ref, start, size):
        if self.dim == 0:
            return ref.at[pl.ds(pl.multiple_of(start, size), size)]
        return ref.at[:, pl.ds(pl.multiple_of(start, size), size)]

    def out(self, i):
        _, give, size, peer = self.spans[i]
        src = self.view(self.part, give, size)
        return self.line.copy(src, self.recv_bufs[i], self.sent.at[i], self.got.at[i], peer)

    def back(self, i):
        keep, _, size, peer = self.spans[i]
        ref = self.view(self.full, keep, size)
        return self.line.copy(ref, ref, self.sent_back.at[i], self.got_back.at[i], peer)

    def back_in(self, i):
        _, give, size, peer = self.spans[i]
        ref = self.view(self.full, give, size)
        return self.line.copy(ref, ref, self.sent_back.at[i], self.got_back.at[i], peer)

    def stages(self):
        return 2 * len(self.bits) + 1

    def stage(self, k):
        n = len(self.bits)
        if 1 <= k <= n:
            keep, _, size, _ = self.spans[k - 1]
            self.out(k - 1).wait()
            ref = self.view(self.part, keep, size)
            to = self.view(self.full, keep, size) if k == n else ref
            to[...] = (ref[...].astype(F32) + self.recv_bufs[k - 1][...].astype(F32)).astype(BF16)
        elif k > n:
            i = 2 * n - k
            self.back(i).wait_send()
            self.back_in(i).wait_recv()
        if k < n:
            self.out(k).start()
        elif k < 2 * n:
            self.back(2 * n - 1 - k).start()


def frame_sum_scratch(frames, shape, dim):
    bits = frames.bit_length() - 1
    scratch = []
    for i in range(bits):
        part = list(shape)
        part[dim] = shape[dim] >> (i + 1)
        scratch.append(pltpu.VMEM(tuple(part), BF16))
    return [pltpu.VMEM(shape, BF16)] + scratch + [pltpu.SemaphoreType.DMA((bits,))] * 4


def frame_sums(line, arrays, scratch):
    bits = line.frames.bit_length() - 1
    sums = []
    for full, dim, reverse in arrays:
        part, *mine = scratch[: bits + 5]
        scratch = scratch[bits + 5 :]
        sums.append(FrameSum(line, part, full, dim, reverse, mine[:bits], mine[bits:]))
    return sums


class Everyone:
    def __init__(self, line, bufs, sems):
        self.line = line
        self.src, self.dst_sib, self.dst_line, self.dst_frames = bufs
        self.sent, self.got = sems

    def pair_copy(self):
        ln = self.line
        return ln.copy(
            self.src.at[0], self.dst_sib, self.sent.at[0], self.got.at[0], ln.sibling()
        )

    def line_copies(self):
        ln = self.line
        return [
            ln.copy(
                self.src.at[1],
                self.dst_line.at[ln.z],
                self.sent.at[k],
                self.got.at[k],
                ln.at((ln.z + k) % ln.chips),
            )
            for k in range(1, ln.chips)
        ]

    def frame_copies(self):
        ln = self.line
        return [
            ln.copy(
                self.src.at[2],
                self.dst_frames.at[ln.f],
                self.sent.at[ln.chips + k],
                self.got.at[ln.chips + k],
                ((ln.f + k) % ln.frames, ln.h),
            )
            for k in range(1, ln.frames)
        ]

    def over_pair(self, value):
        self.src[0] = value.astype(BF16)
        self.pair_copy().start()

    def over_line(self):
        self.pair_copy().wait()
        pair = self.src[0].astype(F32) + self.dst_sib[...].astype(F32)
        self.src[1] = pair.astype(BF16)
        copies = self.line_copies()
        for copy in copies:
            copy.start()
        self.dst_line[self.line.z] = self.src[1]

    def over_frames(self, frames_value):
        for copy in self.line_copies():
            copy.wait()
        total = self.dst_line[0].astype(F32)
        for i in range(1, self.line.chips):
            total = total + self.dst_line[i].astype(F32)
        self.src[2] = (total + frames_value).astype(BF16)
        for copy in self.frame_copies():
            copy.start()
        self.dst_frames[self.line.f] = self.src[2]

    def result(self):
        for copy in self.frame_copies():
            copy.wait()
        total = self.dst_frames[0].astype(F32)
        for i in range(1, self.line.frames):
            total = total + self.dst_frames[i].astype(F32)
        return total


class Timetable:
    def __init__(self, chips, streams):
        self.chips, self.streams = chips, streams
        self.every = chips
        while not self.place():
            self.every += 1

    def place(self):
        last, every = self.chips - 1, self.every
        self.arrive = [0]
        for _ in range(1, last):
            t = self.arrive[-1] + HOP
            while t % every in [a % every for a in self.arrive]:
                t += 1
            self.arrive.append(t)
        self.arrive.append(self.arrive[-1] + HOP)
        self.compute = self.arrive[-1] + 2
        self.hops = {}
        for p in range(last):
            taken = {a % every for a in self.arrive[: p + 1]}
            for far in range(last, p, -1):
                t = self.compute + 2
                if p:
                    t = max(t, self.hops[p - 1, far] + HOP)
                while t % every in taken:
                    t += 1
                taken.add(t % every)
                self.hops[p, far] = t
        self.owner = max(self.hops[far - 1, far] for far in range(1, self.chips)) + HOP
        self.turns = self.owner // every + 1
        return self.owner + SLACK <= self.streams * every

    def after(self, item):
        return item + self.compute // self.every + 1

    def steps(self, items):
        return (items + self.turns - 1) * self.every


def pipeline(line, times, gather, sums, phases, enter, compute, owner, total, beside):
    last, streams = line.chips - 1, times.streams
    items = phases * streams

    def body(m, carry):
        for i in range(times.every):
            for behind in reversed(range(times.turns)):
                q = behind * times.every + i
                n = m - behind
                fits = (n >= 0) & (n < items)
                gathers = fits & (n >= streams)
                n = jnp.clip(n, 0, items - 1)
                s = n % streams
                held = jnp.maximum(n - streams, 0)
                if q in times.arrive:
                    distance = times.arrive.index(q)

                    @pl.when(gathers)
                    def _():
                        if distance == 0:
                            enter(n)
                            gather.send(held)
                        else:
                            gather.arrive(distance, held)

                if q == times.compute:

                    @pl.when(gathers)
                    def _():
                        for zb in range(line.chips):
                            gather.wait_across(held, zb)
                            sums.drain(s, zb)

                    @pl.when(fits)
                    def _():
                        compute(n)
                        for zb in range(line.chips):
                            sums.across(s, zb).start()

                for (place, far), at in times.hops.items():
                    if at == q:

                        @pl.when(fits & (line.z == place))
                        def _():
                            sums.hop_up(s, far)

                        @pl.when(fits & (line.z == last - place))
                        def _():
                            sums.hop_down(s, last - far)

                if q == times.owner:

                    @pl.when(fits)
                    def _():
                        sums.finish(s, total)
                        owner(n)

            beside(m, i)
        return carry

    lax.fori_loop(0, items + times.turns - 1, body, 0)


def computed_sum(line, sums, compute, totals, beside):
    steps, chips = line.steps, line.chips

    def body(t, carry):
        @pl.when(t < steps)
        def _():
            compute(t)
            for zb in range(chips):
                sums.across(t, zb).start()

        sums.hops(t - 1)
        beside(t)
        return carry

    lax.fori_loop(0, steps * chips + 1 + (chips - 1) * LAG, body, 0)
    for s in range(steps):
        sums.finish(s, totals.at[s])


def frame_mask(segments, places, rows):
    frames = segments.shape[0]
    bits, place_bits = frames.bit_length() - 1, places.bit_length() - 1

    def ids_along(axis, shape):
        index = lax.broadcasted_iota(jnp.int32, shape, axis)
        frame = lax.shift_right_logical(index, place_bits) & (frames - 1)
        segment = jnp.zeros(shape, jnp.int32)
        for i in range(frames):
            segment = jnp.where(frame == i, segments[i], segment)
        block = lax.shift_right_logical(index, place_bits + bits)
        return block * places + (index & (places - 1)), frame, segment

    place_q, frame_q, segment_q = ids_along(0, (rows, 1))
    place_k, frame_k, segment_k = ids_along(1, (1, rows))
    return (place_q == place_k) & (frame_k <= frame_q) & (segment_q == segment_k)


def qkv_grads(start, left, dqkv, qk_grad, v_grad):
    all_tokens, width = left.shape[0], v_grad.shape[0]
    for i in range(3):
        grad = mm_tn(left, dqkv[i].reshape(all_tokens, dqkv.shape[-1])).astype(BF16)
        if i < 2:
            qk_grad[pl.ds(pl.multiple_of(i * width + start, 256), 256)] = grad
        else:
            v_grad[pl.ds(pl.multiple_of(start, 256), 256)] = grad


def row_sum(value):
    return jnp.sum(value, axis=0, keepdims=True)


def moved_exactly(order, value):
    out = None
    for _ in range(3):
        term = value.astype(BF16)
        value = value - term.astype(F32)
        out = mm(order, term) if out is None else out + mm(order, term)
    return out


class Refs:
    def __init__(self, names, refs):
        for name, ref in zip(names, refs, strict=True):
            setattr(self, name, ref)


def block(names, *refs):
    r = Refs(names, refs)
    steps, patches, width = r.x.shape
    streams, heads, rows, _ = r.g_all.shape
    line, t_line = Line(steps), Line(streams)
    chips, frames = line.chips, line.frames
    s_rows = patches // heads
    tokens = steps * s_rows
    columns, hidden = r.s_wout.shape[0], r.up.shape[1]
    entries = r.table.shape[0]
    count = heads * rows
    all_tokens = heads * tokens
    times = Timetable(chips, streams)
    sums = ChainSum(t_line, (r.part, r.sib, r.rise, r.fall, r.out), r.sum_sems)
    gather = Gather(t_line, r.gathered, r.gather_sems)
    last_part = getattr(r, "last_part", r.part)
    last_out = getattr(r, "last_out", r.out)
    last_sums = ChainSum(
        line, (last_part, r.last_sib, r.last_rise, r.last_fall, last_out), r.last_sems
    )
    shared = not hasattr(r, "g_src")

    def g_src_at(part, to):
        return r.gathered.at[3 * streams + to] if shared else r.g_src.at[part, to]

    g_swap = Swap(line, g_src_at, r.g_dst, r.g_sems)
    state_swap = Swap(line, lambda s, to: r.state_src.at[s, to], r.state_dst, r.state_sems)
    grad_swap = Swap(line, lambda s, to: r.grad_src.at[s, to], r.grad_dst, r.grad_sems)
    y_swap = Swap(line, lambda s, to: r.y_src.at[s, to], r.y_dst, r.y_sems)
    every = Everyone(line, (r.every_src, r.every_sib, r.every_line, r.every_frames), r.every_sems)
    reduced = frame_sums(
        line,
        [
            (r.down_grad, 0, False), (r.up_grad, 0, True),
            (r.t_qk, 0, False), (r.t_v, 0, True), (r.t_out, 1, True),
            (r.s_qk, 0, False), (r.s_v, 0, True), (r.s_out, 1, True),
        ],
        r.reduce,
    )
    mlp_sums, t_sums, s_sums = reduced[:2], reduced[2:5], reduced[5:]
    line.barrier(True, True)

    def g_out(i, carry):
        rows_of = pl.ds(pl.multiple_of(i * s_rows, s_rows), s_rows)
        moved = mm(r.to_peers[...], r.cotangent[:, rows_of].reshape(tokens, width))
        moved = moved.astype(BF16).astype(r.g_dst.dtype).reshape(frames, tokens // frames, width)
        if shared:
            r.gathered[3 * streams : 4 * streams, i // 2, i % 2] = moved
        else:
            r.g_src[0, :, i // 2, i % 2] = moved
        return carry

    lax.fori_loop(0, heads, g_out, 0)
    g_swap.start(0)

    def g_in(i):
        moved = r.g_dst[0, :, i // 2, i % 2].reshape(tokens, width).astype(BF16)
        r.g_all[:, i] = mm(r.to_parts[...], moved).astype(BF16).reshape(streams, rows, width)

    table_row = lax.broadcasted_iota(jnp.int32, (entries, width), 0)

    def added(s):
        return row_sum(jnp.where(table_row == r.ids[s], r.table[...].astype(F32), 0.0))

    def norm(value, i):
        scaled = norm_stats(value)[0] * r.gain[i : i + 1, :]
        return (scaled + r.shift[i : i + 1, :]).astype(BF16)

    def attention(s, carry):
        normed = norm(r.x[s].astype(F32) + added(s), 0)
        r.normed0[s] = normed
        q = mm(normed, r.s_wqkv[0]).astype(BF16)
        k = mm(normed, r.s_wqkv[1]).astype(BF16)
        v = mm(normed, r.s_wqkv[2]).astype(BF16)
        r.s_proj[0, s] = q
        r.s_proj[1, s] = k
        r.s_proj[2, s] = v
        r.s_cols[s] = attend(q, k, v, None)
        return carry

    lax.fori_loop(0, steps, attention, 0)

    def to_streams(i, carry):
        rows_of = pl.ds(pl.multiple_of(i * s_rows, s_rows), s_rows)
        moved = mm(r.to_streams[...], r.s_cols[:, rows_of].reshape(tokens, columns)).astype(BF16)
        r.s_mixed[:, i] = moved.reshape(streams, rows, columns)
        return carry

    lax.fori_loop(0, heads, to_streams, 0)
    own_rows = pl.ds(pl.multiple_of(line.h * s_rows, s_rows), s_rows)
    own = mm(r.to_streams[...], r.x[:, own_rows].reshape(tokens, width))
    row = lax.broadcasted_iota(jnp.int32, (tokens, 1), 0)
    frame = lax.shift_right_logical(row, (rows // (frames * steps)).bit_length() - 1) & (steps - 1)
    entry = jnp.zeros_like(row)
    for s in range(steps):
        entry = jnp.where(frame == s, r.ids[s], entry)
    picker = (entry == lax.broadcasted_iota(jnp.int32, (tokens, entries), 1)).astype(BF16)
    own = own + mm(picker, r.table[...])
    r.state0[...] = own.reshape(streams, rows, width)
    r.mask[...] = frame_mask(r.segments, rows // (frames * steps), count).astype(F32)
    r.up_bias_grad[...] = jnp.zeros_like(r.up_bias_grad)
    r.small[...] = jnp.zeros_like(r.small)

    def held(n):
        return n - streams

    def enter_temporal(s, n):
        state_swap.wait(s)
        state = r.state_dst[s].reshape(rows, width)
        r.state1[s] = state
        r.gathered[held(n), line.z, line.c] = norm(state, 1)

    def enter_spatial(s, n):
        grad_swap.wait(s)
        grad = r.grad_dst[s].reshape(rows, width)
        r.grad1[s] = grad
        r.gathered[held(n), line.z, line.c] = grad.astype(BF16)

    def compute_spatial(s, n):
        left = r.s_mixed[s].reshape(count, columns)
        r.part[s] = mm(left, r.s_wout[...]).astype(BF16).reshape(chips, 2, rows, width)

    def compute_temporal(s, n):
        a = r.gathered[held(n)].reshape(count, width)
        q = mm(a, r.t_wqkv[0]).astype(BF16)
        k = mm(a, r.t_wqkv[1]).astype(BF16)
        v = mm(a, r.t_wqkv[2]).astype(BF16)
        r.t_proj[0, s] = q
        r.t_proj[1, s] = k
        r.t_proj[2, s] = v
        mixed = attend(q, k, v, r.mask[...] > 0.0)
        r.t_mixed[s] = mixed
        r.part[s] = mm(mixed, r.t_wout[...]).astype(BF16).reshape(chips, 2, rows, width)

    def compute_mlp(s, n):
        a = r.gathered[held(n)].reshape(count, width)
        g = r.g_all[s].reshape(count, width)
        pre = mm(a, r.up[...]) + r.up_bias[...]
        t = jnp.tanh(GELU_C * (pre + 0.044715 * (pre * pre * pre)))
        act = (0.5 * pre * (1.0 + t)).astype(BF16)
        r.act[s] = act
        slope = 0.5 * (1.0 + t)
        slope = slope + 0.5 * pre * (1.0 - t * t) * (GELU_C * (1.0 + 0.134145 * (pre * pre)))
        dpre = (mm_nt(g, r.down[...]) * slope).astype(BF16)
        r.dpre[s] = dpre
        r.up_bias_grad[:, :hidden] += row_sum(dpre.astype(F32))
        r.part[s] = mm_nt(dpre, r.up[...]).astype(BF16).reshape(chips, 2, rows, width)

    def compute_back(s, n):
        grad = r.gathered[held(n)].reshape(count, width)
        dm = mm_nt(grad, r.t_wout[...]).astype(BF16)
        mask = r.mask[...] > 0.0
        dq, dk, dv = attend_back(r.t_proj[0, s], r.t_proj[1, s], r.t_proj[2, s], mask, dm)
        r.t_dproj[0, s] = dq
        r.t_dproj[1, s] = dk
        r.t_dproj[2, s] = dv
        da = mm_nt(dq, r.t_wqkv[0]) + mm_nt(dk, r.t_wqkv[1]) + mm_nt(dv, r.t_wqkv[2])
        r.part[s] = da.astype(BF16).reshape(chips, 2, rows, width)

    def compute_last(s, n):
        grad = r.gathered[held(n)].reshape(count, width)
        moved = mm_nt(grad, r.s_wout[...]).astype(BF16)
        r.s_dmixed[s] = moved.reshape(heads, rows, columns)
        y = mm(r.act[s], r.down[...])
        r.part[s] = y.astype(BF16).reshape(chips, 2, rows, width)

    def owner_spatial(s, n):
        state = r.state0[s] + r.total[...] + r.bias[0:1, :]
        r.state_src[s] = state.reshape(r.state_src.shape[1:])
        state_swap.start(s)

    def owner_temporal(s, n):
        state = r.state1[s] + r.total[...] + r.bias[1:2, :]
        r.state2[s] = state
        r.gathered[n, line.z, line.c] = norm(state, 2)

    def owner_mlp(s, n):
        grad = r.g_all[s, line.h].astype(F32)
        back, gain_grad, shift_grad = norm_back(r.state2[s], r.total[...], r.gain[2:3, :])
        dh = grad + back
        r.grad2[s] = dh
        r.gathered[n, line.z, line.c] = dh.astype(BF16)
        r.small[0:1] += gain_grad
        r.small[1:2] += shift_grad
        r.small[2:3] += row_sum(grad)
        r.small[3:4] += row_sum(dh)

    def owner_back(s, n):
        back, gain_grad, shift_grad = norm_back(r.state1[s], r.total[...], r.gain[1:2, :])
        dh = r.grad2[s] + back
        r.grad_src[s] = dh.reshape(r.grad_src.shape[1:])
        grad_swap.start(s)
        r.small[4:5] += gain_grad
        r.small[5:6] += shift_grad
        r.small[6:7] += row_sum(dh)

    def owner_last(s, n):
        r.y[s] = (r.state2[s] + r.total[...] + r.bias[2:3, :]).astype(BF16)

    def by_phase(bodies):
        def run(n):
            for i, one in enumerate(bodies):
                if one is not None:

                    @pl.when(n // streams == i)
                    def _():
                        one(n % streams, n)

        return run

    def down_chunk(i):
        cols = pl.ds(pl.multiple_of(i * 128, 128), 128)
        left = r.act[:, :, cols].reshape(all_tokens, 128)
        right = r.g_all[...].reshape(all_tokens, width)
        mlp_sums[0].part[cols] = mm_tn(left, right).astype(BF16)

    def up_chunk(i):
        cols = pl.ds(pl.multiple_of(i * 256, 256), 256)
        left = r.gathered[streams : 2 * streams, :, :, :, cols].reshape(all_tokens, 256)
        right = r.dpre[...].reshape(all_tokens, hidden)
        mlp_sums[1].part[cols] = mm_tn(left, right).astype(BF16)

    def t_out_chunk(i):
        left = r.t_mixed[...].reshape(all_tokens, columns)
        right = r.gathered[2 * streams : 3 * streams].reshape(all_tokens, width)
        t_sums[2].part[...] = mm_tn(left, right).astype(BF16)

    def t_qkv_chunk(i):
        start = i * 256
        cols = pl.ds(pl.multiple_of(start, 256), 256)
        left = r.gathered[0:streams, :, :, :, cols].reshape(all_tokens, 256)
        qkv_grads(start, left, r.t_dproj, t_sums[0].part, t_sums[1].part)

    def g_in_chunk(i):
        @pl.when(i == 0)
        def _():
            g_swap.wait(0)

        g_in(i)

    n_down, n_up = hidden // 128, width // 256
    turn_of = times.after
    mlp_turn, back_turn = turn_of(3 * streams - 1), turn_of(4 * streams - 1)
    chunks = (
        (streams + 1, 0, heads, g_in_chunk),
        (mlp_turn, 0, n_down, down_chunk),
        (mlp_turn, n_down, n_up, up_chunk),
        (back_turn, 0, 1, t_out_chunk),
        (back_turn, 1, width // 256, t_qkv_chunk),
    )
    slots = [i for i in range(times.every) if i % 2 == 1][:3]
    per_turn = 2 * len(slots)
    turns = 5 * streams + times.turns - 1
    stages = reduced[0].stages()
    bits = len(reduced[0].bits)

    def moments_of(begin, first):
        t, out = begin, []
        for k in range(stages):
            out.append(t)
            halvings = k if k < bits else max(2 * bits - 1 - k, 0)
            t += 2 + max(first >> halvings, 1)
        return out

    def begin_of(turn, number):
        return (turn + number // per_turn) * times.every + times.every - 1

    moments = (
        (mlp_sums, moments_of(begin_of(mlp_turn, n_down + n_up), 10)),
        (t_sums, moments_of(begin_of(back_turn, 1 + width // 256), 5)),
    )

    def beside(m, i):
        if i in slots:
            for turn, first, number, chunk in chunks:
                which = per_turn * (m - turn) + 2 * slots.index(i) - first
                here = jnp.clip(number - which, 0, 2)

                @pl.when((which > -2) & (which < number))
                def _():
                    def one(j, carry):
                        @pl.when(which + j >= 0)
                        def _():
                            chunk(which + j)

                        return carry

                    lax.fori_loop(0, here, one, 0)

        for sums_of, steps_of in moments:
            for k, moment in enumerate(steps_of):
                if moment % times.every == i and moment // times.every < turns:

                    @pl.when(m == moment // times.every)
                    def _():
                        for one in sums_of:
                            one.stage(k)

    enter = by_phase((None, enter_temporal, None, None, enter_spatial))
    compute = by_phase(
        (compute_spatial, compute_temporal, compute_mlp, compute_back, compute_last)
    )
    owner = by_phase((owner_spatial, owner_temporal, owner_mlp, owner_back, owner_last))
    pipeline(t_line, times, gather, sums, 5, enter, compute, owner, r.total, beside)
    drain_all(t_line, (sums,), streams)

    y = mm(r.from_parts[...], r.y[...].reshape(tokens, width)).astype(BF16)
    r.y_src[0] = y.astype(r.y_src.dtype).reshape(r.y_src.shape[1:])
    y_swap.start(0)

    def from_streams(i, carry):
        rows_of = pl.ds(pl.multiple_of(i * s_rows, s_rows), s_rows)
        moved = mm(r.from_streams[...], r.s_dmixed[:, i].reshape(tokens, columns)).astype(BF16)
        r.s_cols[:, rows_of] = moved.reshape(steps, s_rows, columns)
        return carry

    lax.fori_loop(0, heads, from_streams, 0)
    r.sums0[...] = jnp.zeros_like(r.sums0)

    def compute_spatial_back(s):
        dq, dk, dv = attend_back(r.s_proj[0, s], r.s_proj[1, s], r.s_proj[2, s], None, r.s_cols[s])
        r.s_dproj[0, s] = dq
        r.s_dproj[1, s] = dk
        r.s_dproj[2, s] = dv
        da = mm_nt(dq, r.s_wqkv[0]) + mm_nt(dk, r.s_wqkv[1]) + mm_nt(dv, r.s_wqkv[2])
        last_part[s] = da.astype(BF16).reshape(last_part.shape[1:])

    def small_part(s):
        state = r.x[s].astype(F32) + added(s)
        da = last_part[s].reshape(patches, width).astype(F32)
        back, gain_grad, shift_grad = norm_back(state, da, r.gain[0:1, :])
        r.sums0[0:1] += gain_grad
        r.sums0[1:2] += shift_grad
        r.sums0[8 : 8 + entries] += jnp.where(table_row == r.ids[s], row_sum(back), 0.0)

    room = r.every_src.shape[1]
    filled = 9 + entries

    def small_value(own_grad):
        for s in range(steps):
            here = row_sum(own_grad[s * s_rows : (s + 1) * s_rows])
            r.sums0[8 : 8 + entries] += jnp.where(table_row == r.ids[s], here, 0.0)
        rows_of = [
            r.sums0[0:1], r.small[4:5], r.small[0:1],
            r.sums0[1:2], r.small[5:6], r.small[1:2],
            r.small[6:7], r.small[3:4], r.small[2:3],
            r.sums0[8 : 8 + entries], jnp.zeros((room - filled, width), F32),
        ]
        return jnp.concatenate(rows_of, axis=0)

    s_moments = moments_of(steps + 1, 4)

    def beside_last(t):
        @pl.when(t == steps)
        def _():
            left = r.s_mixed[...].reshape(all_tokens, columns)
            right = r.gathered[3 * streams : 4 * streams].reshape(all_tokens, width)
            s_sums[2].part[...] = mm_tn(left, right).astype(BF16)

        @pl.when((t >= steps) & (t < steps + 2))
        def _():
            for i in range(width // 512):
                start = ((t - steps) * (width // 512) + i) * 256
                cols = pl.ds(pl.multiple_of(start, 256), 256)
                left = r.normed0[:, :, cols].reshape(all_tokens, 256)
                qkv_grads(start, left, r.s_dproj, s_sums[0].part, s_sums[1].part)

        for k in range(stages - 1):

            @pl.when(t == s_moments[k])
            def _():
                for one in s_sums:
                    one.stage(k)

        @pl.when((t >= steps + 2) & (t < 2 * steps + 2))
        def _():
            small_part(t - steps - 2)

        @pl.when(t == 2 * steps + 2)
        def _():
            grad = r.grad1[...].reshape(tokens, width)
            own_grad = moved_exactly(r.from_streams[...], grad)
            r.state0[...] = own_grad.reshape(r.state0.shape)
            every.over_pair(small_value(own_grad))

        @pl.when(t == 2 * steps + 4)
        def _():
            every.over_line()

        @pl.when(t == 2 * steps + 7)
        def _():
            row = lax.broadcasted_iota(jnp.int32, (room, width), 0)
            every.over_frames(jnp.where(row == filled, r.up_bias_grad[...], 0.0))

    computed_sum(line, last_sums, compute_spatial_back, r.last_total, beside_last)
    own_grad = r.state0[...].reshape(tokens, width)
    for s in range(steps):
        state = r.x[s, own_rows].astype(F32) + added(s)
        back, _, _ = norm_back(state, r.last_total[s], r.gain[0:1, :])
        r.grad_res[pl.ds(s * s_rows, s_rows)] = own_grad[s * s_rows : (s + 1) * s_rows] + back
    y_swap.wait(0)
    r.y_res[...] = mm(r.from_peers[...], r.y_dst[0].reshape(tokens, width).astype(BF16)).astype(BF16)
    r.small_res[...] = every.result()
    for sums_of, steps_of in moments:
        for k, moment in enumerate(steps_of):
            if moment // times.every >= turns:
                for one in sums_of:
                    one.stage(k)
    for k, moment in enumerate(s_moments):
        if k == stages - 1:
            for one in s_sums:
                one.stage(k)
    drain_all(line, (last_sums,), steps)
    drain_all(t_line, (gather,), 4 * streams)


def finish(
    t_qk, t_v, t_out, s_qk, s_v, s_out, up, down, y, grad, small,
    y_res, grad_res, table_res, gain_res, shift_res, s_qkv_res, s_out_res, t_qkv_res, t_out_res,
    bias_res, up_res, up_bias_res, down_res,
):
    for qk, v, res in ((t_qk, t_v, t_qkv_res), (s_qk, s_v, s_qkv_res)):
        res[0:2] = qk[...].astype(F32)
        res[2] = v[...].astype(F32)
    t_out_res[...] = t_out[...].astype(F32)
    s_out_res[...] = s_out[...].astype(F32)
    up_res[...] = up[...].astype(F32)
    down_res[...] = down[...].astype(F32)
    y_res[...] = y[...]
    grad_res[...] = grad[...]

    @pl.when(pl.program_id(0) == 0)
    def _():
        entries = table_res.shape[0]
        gain_res[...] = small[0:3]
        shift_res[...] = small[3:6]
        bias_res[...] = small[6:9]
        table_res[...] = small[9 : 9 + entries]
        up_bias_res[...] = small[9 + entries : 10 + entries, : up_bias_res.shape[1]]


def results(values, entries, hidden):
    grid = 8

    def blocks(shape, sliced=True):
        axis = len(shape) - 2
        block = list(shape)
        if sliced:
            block[axis] //= grid
        place = [0] * len(shape)

        def index(i):
            at = list(place)
            if sliced:
                at[axis] = i
            return tuple(at)

        return pl.BlockSpec(tuple(block), index)

    t_qk, t_v, t_out, _, _, _, g_up, g_down, y, grad, small = values
    width = g_up.shape[0]
    qkv = ((3,) + t_qk.shape[1:], F32, True)
    out = (t_out.shape, F32, True)
    few = ((3, width), F32, False)
    outs = [
        (y.shape, BF16, True), (grad.shape, F32, True), ((entries, width), F32, False), few, few,
        qkv, out, qkv, out, few,
        (g_up.shape, F32, True), ((1, hidden), F32, False), (g_down.shape, F32, True),
    ]
    return pl.pallas_call(
        finish,
        name="finish",
        grid=(grid,),
        out_shape=[jax.ShapeDtypeStruct(shape, kind) for shape, kind, _ in outs],
        in_specs=[blocks(v.shape, v is not small) for v in values],
        out_specs=[blocks(shape, sliced) for shape, _, sliced in outs],
    )(*values)


def orders(frames_local, frames, places, streams):
    tokens = frames_local * frames * places
    index = np.arange(tokens).reshape(frames_local, frames, streams, places // streams)
    to_streams = index.transpose(2, 1, 0, 3).reshape(-1)
    to_peers = index.transpose(1, 0, 2, 3).reshape(-1)
    index = np.arange(tokens).reshape(frames * frames_local, streams, places // streams)
    to_parts = index.transpose(1, 0, 2).reshape(-1)
    eye = np.eye(tokens, dtype=np.float32)
    there = [eye[order] for order in (to_streams, to_peers, to_parts)]
    back = [m.T for m in there]
    names = ("to_streams", "to_peers", "to_parts", "from_streams", "from_peers", "from_parts")
    return {name: jnp.asarray(m, BF16) for name, m in zip(names, there + back)}


def on_device(
    block_input,
    action_ids,
    segment_ids,
    action_table,
    norm_gain,
    norm_shift,
    spatial_qkv,
    spatial_out,
    temporal_qkv,
    temporal_out,
    out_bias,
    up_weight,
    up_bias,
    down_weight,
    cotangent,
):
    frames, heads = lax.axis_size("frames"), lax.axis_size("heads")
    chips = heads // 2
    steps, patches, width = block_input.shape
    rows = patches // heads
    tokens = steps * rows
    total_frames = segment_ids.shape[0]
    places = rows // frames
    streams = min(4, places)
    t_rows = tokens // streams
    columns = spatial_out.shape[0]
    hidden = up_weight.shape[1]
    entries = action_table.shape[0]
    count = heads * t_rows
    room = -(-(10 + entries) // 16) * 16
    args = dict(
        ids=action_ids,
        segments=segment_ids,
        x=block_input,
        cotangent=cotangent,
        table=action_table,
        gain=norm_gain,
        shift=norm_shift,
        bias=out_bias,
        s_wqkv=spatial_qkv.transpose(1, 0, 2),
        s_wout=spatial_out,
        t_wqkv=temporal_qkv.transpose(1, 0, 2),
        t_wout=temporal_out,
        up=up_weight,
        up_bias=up_bias.reshape(1, hidden),
        down=down_weight,
        **orders(steps, frames, places, streams),
    )
    qk, v, out = (2 * width, columns), (width, columns), (columns, width)
    down, up = (hidden, width), (width, hidden)
    outs = dict(
        t_qk=(qk, BF16),
        t_v=(v, BF16),
        t_out=(out, BF16),
        s_qk=(qk, BF16),
        s_v=(v, BF16),
        s_out=(out, BF16),
        up_grad=(up, BF16),
        down_grad=(down, BF16),
        y_res=((tokens, width), BF16),
        grad_res=((tokens, width), F32),
        small_res=((room, width), F32),
    )
    s_all = (steps, chips, 2, rows, width)
    t_all = (streams, chips, 2, t_rows, width)
    s_one, t_one = (steps, chips, rows, width), (streams, chips, t_rows, width)
    owned = (streams, t_rows, width)
    swapped = (streams, frames, t_rows // frames, width)
    whole = (1, frames, tokens // frames, width)
    g_part = (1, frames, chips, 2, tokens // frames, width)

    def kind_of(shape):
        return BF16 if shape[-2] % 16 == 0 else F32

    cols = dict(
        s_cols=(steps, patches, columns),
        s_proj=(3, steps, patches, columns),
        s_dproj=(3, steps, patches, columns),
        s_mixed=(streams, heads, t_rows, columns),
        s_dmixed=(streams, heads, t_rows, columns),
        t_proj=(3, streams, count, columns),
        t_dproj=(3, streams, count, columns),
        t_mixed=(streams, count, columns),
        act=(streams, count, hidden),
        dpre=(streams, count, hidden),
        normed0=(steps, patches, width),
        gathered=(4 * streams,) + t_all[1:],
        g_all=(streams, heads, t_rows, width),
        part=t_all,
        sib=t_one,
        rise=t_one,
        fall=t_one,
        out=t_one,
        **({} if s_all == t_all else dict(last_part=s_all, last_out=s_one)),
        last_sib=s_one,
        last_rise=s_one,
        last_fall=s_one,
        y=owned,
    )
    floats = dict(
        state0=owned,
        state1=owned,
        state2=owned,
        grad1=owned,
        grad2=owned,
        total=(t_rows, width),
        last_total=(steps, rows, width),
        mask=(count, count),
        small=(8, width),
        sums0=(8 + entries, width),
        up_bias_grad=(1, width),
        state_src=swapped,
        state_dst=swapped,
        grad_src=swapped,
        grad_dst=swapped,
    )
    scratch = {name: pltpu.VMEM(shape, BF16) for name, shape in cols.items()}
    scratch |= {name: pltpu.VMEM(shape, F32) for name, shape in floats.items()}
    moving = ("g_dst",) if g_part[1:] == t_all else ("g_src", "g_dst")
    scratch |= {name: pltpu.VMEM(g_part, kind_of(g_part)) for name in moving}
    scratch |= {name: pltpu.VMEM(whole, kind_of(whole)) for name in ("y_src", "y_dst")}
    every_shape = (room, width)
    scratch |= dict(
        every_src=pltpu.VMEM((3,) + every_shape, BF16),
        every_sib=pltpu.VMEM(every_shape, BF16),
        every_line=pltpu.VMEM((chips,) + every_shape, BF16),
        every_frames=pltpu.VMEM((frames,) + every_shape, BF16),
        every_sems=[pltpu.SemaphoreType.DMA((chips + frames,))] * 2,
        sum_sems=[pltpu.SemaphoreType.DMA((streams, chips))] * 5,
        last_sems=[pltpu.SemaphoreType.DMA((steps, chips))] * 5,
        gather_sems=[pltpu.SemaphoreType.DMA((4 * streams, chips))] * 5,
        state_sems=[pltpu.SemaphoreType.DMA((streams, frames))] * 2,
        grad_sems=[pltpu.SemaphoreType.DMA((streams, frames))] * 2,
        g_sems=[pltpu.SemaphoreType.DMA((1, frames))] * 2,
        y_sems=[pltpu.SemaphoreType.DMA((1, frames))] * 2,
        reduce=[
            x
            for shape, dim in (
                (down, 0), (up, 0), (qk, 0), (v, 0), (out, 1), (qk, 0), (v, 0), (out, 1)
            )
            for x in frame_sum_scratch(frames, shape, dim)
        ],
    )
    names = tuple(args) + tuple(outs) + tuple(scratch)
    parts = pl.pallas_call(
        lambda *refs: block(names, *refs),
        name="block",
        out_shape=[jax.ShapeDtypeStruct(shape, kind) for shape, kind in outs.values()],
        in_specs=[
            pl.BlockSpec(memory_space=pltpu.SMEM if name in ("ids", "segments") else pltpu.VMEM)
            for name in args
        ],
        out_specs=[pl.BlockSpec(memory_space=pltpu.VMEM)] * len(outs),
        scratch_shapes=list(scratch.values()),
        compiler_params=pltpu.CompilerParams(
            collective_id=0, has_side_effects=True, vmem_limit_bytes=VMEM_LIMIT
        ),
    )(*args.values())
    found = dict(zip(outs, parts))
    for name in ("t_qk", "s_qk"):
        found[name] = found[name].reshape(2, width, columns)
    (
        block_output, input_grad, table_grad, gain_grad, shift_grad, s_qkv_grad, s_out_grad,
        t_qkv_grad, t_out_grad, bias_grad, up_grad, up_bias_grad, down_grad,
    ) = results(list(found.values()), entries, hidden)
    s_blocks = (steps, rows, width)
    return (
        block_output.reshape(s_blocks),
        input_grad.reshape(s_blocks),
        table_grad,
        gain_grad,
        shift_grad,
        s_qkv_grad.transpose(1, 0, 2),
        s_out_grad,
        t_qkv_grad.transpose(1, 0, 2),
        t_out_grad,
        bias_grad,
        up_grad,
        up_bias_grad.reshape(hidden),
        down_grad,
    )


def solution(mesh):
    return jax.shard_map(
        on_device,
        mesh=mesh,
        in_specs=(
            P("frames", None, None),
            P("frames"),
            P(),
            P(),
            P(),
            P(),
            P(None, None, "heads"),
            P("heads", None),
            P(None, None, "heads"),
            P("heads", None),
            P(),
            P(None, "heads"),
            P("heads"),
            P("heads", None),
            P("frames", None, None),
        ),
        out_specs=(
            P("frames", "heads", None),
            P("frames", "heads", None),
            P(),
            P(),
            P(),
            P(None, None, "heads"),
            P("heads", None),
            P(None, None, "heads"),
            P("heads", None),
            P(),
            P(None, "heads"),
            P("heads"),
            P("heads", None),
        ),
        check_vma=False,
    )
```

time: 283 us -> 262 us (0.926)
  Pallas kernels: 281 us -> 261 us
    pallas_call x3 -> x1, Pallas kernels: 272 us -> 252 us  [on_device(): pl.pallas_call(lambda *refs: block(names, *refs), name='block', out_shape...]
where the time goes in v3:
time: 262 us
  Pallas kernels  261 us (100%)
    pallas_call x1, Pallas kernels, on_device(): pl.pallas_call(lambda *refs: block(names, *refs), name='block', out_shape...  252 us
    pallas_call x1, Pallas kernels, results(): pl.pallas_call(finish, name='finish', grid=(grid,), out_shape=[jax.ShapeD...  8.31 us

profile of v3, /device:TPU:0, one launch (start us, length us, event | category | flops | bytes accessed | tf_op | source)
XLA Modules:
  0.0 261.6 jit_solution(14452891317952025115)
XLA Ops:
  0.7 252.5 %block.1 = (bf16[2048,128]{1,0:T(8,128)(2,1)}, bf16[1024,128]{1,0:T(8,128)(2,1)}, bf16[128,1024]{1,0:T(8,128)(2,1)}, bf16[2048,128]{1,0:T(8,128)(2,1)}, bf16[102...) custom-call(s32[4]{0:T(128)} %refs_0_.1, ...), custom_call_target="tpu_custom_call" | custom-call | tf_op jit(solution)/shard_map/block/pallas_call | solution.py:1345
  253.1 8.3 %finish.1 = (bf16[128,1024]{1,0:T(8,128)(2,1)}, f32[128,1024]{1,0:T(8,128)}, f32[8,1024]{1,0:T(8,128)}, f32[3,1024]{1,0:T(4,128)}, f32[3,1024]{1,0:T(4,128)}, /*...) custom-call(bf16[2,1024,128]{2,1,0:T(8,128)(2,1)} %bitcast.12, ...), custom_call_target="tpu_custom_call" | custom-call | tf_op jit(solution)/shard_map/finish/pallas_call | solution.py:1176

commit v4 on v3

--- a/solution.py
+++ b/solution.py
@@ -16,8 +16,11 @@
 VMEM_LIMIT = 62 * 1024 * 1024
 GELU_C = float(np.sqrt(2.0 / np.pi))
 LAG = 2
-HOP = 3
-SLACK = 2
+MLP_WAITS = (13, 8)
+T_WAITS = (9, 6)
+LAST_STAGES = (8, 11, 14)
+LAST_SMALL = (9, 12, 15)
+HOP_US, SIBLING_US, COMPUTE_US, LINK_US, OWNER_US = 3.4, 0.6, 0.6, 1.45, 0.4
 
 
 def mm(a, b):
@@ -466,113 +469,113 @@
 
 
 class Everyone:
-    def __init__(self, line, bufs, sems):
+    def __init__(self, line, refs, sems):
         self.line = line
-        self.src, self.dst_sib, self.dst_line, self.dst_frames = bufs
+        self.src, self.dst_sib, self.dst_line, self.dst_frames, self.full = refs
         self.sent, self.got = sems
+        self.share = self.src.shape[1] // line.chips
+
+    def cols(self, z):
+        return pl.ds(pl.multiple_of(z * self.share, self.share), self.share)
 
     def pair_copy(self):
         ln = self.line
-        return ln.copy(
-            self.src.at[0], self.dst_sib, self.sent.at[0], self.got.at[0], ln.sibling()
-        )
+        return ln.copy(self.src, self.dst_sib, self.sent.at[0], self.got.at[0], ln.sibling())
 
     def line_copies(self):
-        ln = self.line
-        return [
-            ln.copy(
-                self.src.at[1],
-                self.dst_line.at[ln.z],
-                self.sent.at[k],
-                self.got.at[k],
-                ln.at((ln.z + k) % ln.chips),
-            )
-            for k in range(1, ln.chips)
-        ]
+        ln, copies = self.line, []
+        for k in range(1, ln.chips):
+            to = (ln.z + k) % ln.chips
+            src, dst = self.dst_sib.at[:, self.cols(to)], self.dst_line.at[ln.z]
+            copies.append(ln.copy(src, dst, self.sent.at[k], self.got.at[k], ln.at(to)))
+        return copies
 
     def frame_copies(self):
-        ln = self.line
-        return [
-            ln.copy(
-                self.src.at[2],
-                self.dst_frames.at[ln.f],
-                self.sent.at[ln.chips + k],
-                self.got.at[ln.chips + k],
-                ((ln.f + k) % ln.frames, ln.h),
-            )
-            for k in range(1, ln.frames)
-        ]
+        ln, copies = self.line, []
+        for k in range(1, ln.frames):
+            to, i = ((ln.f + k) % ln.frames, ln.h), ln.chips + k
+            src, dst = self.dst_line.at[ln.z], self.dst_frames.at[ln.f]
+            copies.append(ln.copy(src, dst, self.sent.at[i], self.got.at[i], to))
+        return copies
+
+    def back_copies(self):
+        ln, copies = self.line, []
+        for k in range(1, ln.chips):
+            to, i = ln.at((ln.z + k) % ln.chips), ln.chips + ln.frames + k
+            ref = self.full.at[:, self.cols(ln.z)]
+            copies.append(ln.copy(ref, ref, self.sent.at[i], self.got.at[i], to))
+        return copies
 
     def over_pair(self, value):
-        self.src[0] = value.astype(BF16)
+        self.src[...] = value.astype(BF16)
         self.pair_copy().start()
 
     def over_line(self):
         self.pair_copy().wait()
-        pair = self.src[0].astype(F32) + self.dst_sib[...].astype(F32)
-        self.src[1] = pair.astype(BF16)
-        copies = self.line_copies()
-        for copy in copies:
+        pair = self.src[...].astype(F32) + self.dst_sib[...].astype(F32)
+        self.dst_sib[...] = pair.astype(BF16)
+        for copy in self.line_copies():
             copy.start()
-        self.dst_line[self.line.z] = self.src[1]
-
-    def over_frames(self, frames_value):
+
+    def over_frames(self):
+        ln = self.line
         for copy in self.line_copies():
             copy.wait()
-        total = self.dst_line[0].astype(F32)
-        for i in range(1, self.line.chips):
-            total = total + self.dst_line[i].astype(F32)
-        self.src[2] = (total + frames_value).astype(BF16)
+        total = self.dst_sib[:, self.cols(ln.z)].astype(F32)
+        for k in range(1, ln.chips):
+            total = total + self.dst_line[(ln.z + k) % ln.chips].astype(F32)
+        self.dst_line[ln.z] = total.astype(BF16)
         for copy in self.frame_copies():
             copy.start()
-        self.dst_frames[self.line.f] = self.src[2]
-
-    def result(self):
+        self.dst_frames[ln.f] = self.dst_line[ln.z]
+
+    def over_back(self):
         for copy in self.frame_copies():
             copy.wait()
         total = self.dst_frames[0].astype(F32)
         for i in range(1, self.line.frames):
             total = total + self.dst_frames[i].astype(F32)
-        return total
+        self.full[:, self.cols(self.line.z)] = total.astype(BF16)
+        for copy in self.back_copies():
+            copy.start()
+
+    def result(self):
+        for copy in self.back_copies():
+            copy.wait()
+        return self.full[...].astype(F32)
 
 
 class Timetable:
     def __init__(self, chips, streams):
+        last = chips - 1
         self.chips, self.streams = chips, streams
-        self.every = chips
-        while not self.place():
-            self.every += 1
-
-    def place(self):
-        last, every = self.chips - 1, self.every
-        self.arrive = [0]
-        for _ in range(1, last):
-            t = self.arrive[-1] + HOP
-            while t % every in [a % every for a in self.arrive]:
-                t += 1
-            self.arrive.append(t)
-        self.arrive.append(self.arrive[-1] + HOP)
-        self.compute = self.arrive[-1] + 2
-        self.hops = {}
-        for p in range(last):
-            taken = {a % every for a in self.arrive[: p + 1]}
-            for far in range(last, p, -1):
-                t = self.compute + 2
-                if p:
-                    t = max(t, self.hops[p - 1, far] + HOP)
-                while t % every in taken:
-                    t += 1
-                taken.add(t % every)
-                self.hops[p, far] = t
-        self.owner = max(self.hops[far - 1, far] for far in range(1, self.chips)) + HOP
-        self.turns = self.owner // every + 1
-        return self.owner + SLACK <= self.streams * every
+        steps = [(d * HOP_US, "arrive", d) for d in range(chips)]
+        self.compute = last * HOP_US + SIBLING_US
+        steps.append((self.compute, "compute", 0))
+        first = self.compute + COMPUTE_US + SIBLING_US
+        hops = {}
+        for place in range(last):
+            t = first
+            for far in range(last, place, -1):
+                if place:
+                    t = max(t, hops[place - 1, far] + HOP_US)
+                hops[place, far] = t
+                steps.append((t, "hop", (place, far)))
+                t += LINK_US
+        owner = max(hops[far - 1, far] for far in range(1, chips)) + HOP_US
+        steps.append((owner, "owner", 0))
+        self.turn = max((owner + OWNER_US) / streams, chips * LINK_US)
+        self.turns = int(owner / self.turn) + 1
+        self.every = 6
+        steps += [((i + 0.5) * self.turn / self.every, "beside", i) for i in range(self.every)]
+        self.order = []
+        for t, what, which in steps:
+            behind = int(t / self.turn)
+            self.order.append((t - behind * self.turn, -t, what, which, behind))
+        self.order.sort(key=lambda step: step[:2])
 
     def after(self, item):
-        return item + self.compute // self.every + 1
-
-    def steps(self, items):
-        return (items + self.turns - 1) * self.every
+        return item + int(self.compute / self.turn) + 1
 
 
 def pipeline(line, times, gather, sums, phases, enter, compute, owner, total, beside):
@@ -580,81 +583,60 @@
     items = phases * streams
 
     def body(m, carry):
-        for i in range(times.every):
-            for behind in reversed(range(times.turns)):
-                q = behind * times.every + i
-                n = m - behind
-                fits = (n >= 0) & (n < items)
-                gathers = fits & (n >= streams)
-                n = jnp.clip(n, 0, items - 1)
-                s = n % streams
-                held = jnp.maximum(n - streams, 0)
-                if q in times.arrive:
-                    distance = times.arrive.index(q)
-
-                    @pl.when(gathers)
-                    def _():
-                        if distance == 0:
-                            enter(n)
-                            gather.send(held)
-                        else:
-                            gather.arrive(distance, held)
-
-                if q == times.compute:
-
-                    @pl.when(gathers)
-                    def _():
-                        for zb in range(line.chips):
-                            gather.wait_across(held, zb)
-                            sums.drain(s, zb)
-
-                    @pl.when(fits)
-                    def _():
-                        compute(n)
-                        for zb in range(line.chips):
-                            sums.across(s, zb).start()
-
-                for (place, far), at in times.hops.items():
-                    if at == q:
-
-                        @pl.when(fits & (line.z == place))
-                        def _():
-                            sums.hop_up(s, far)
-
-                        @pl.when(fits & (line.z == last - place))
-                        def _():
-                            sums.hop_down(s, last - far)
-
-                if q == times.owner:
-
-                    @pl.when(fits)
-                    def _():
-                        sums.finish(s, total)
-                        owner(n)
-
-            beside(m, i)
+        for _, _, what, which, behind in times.order:
+            n = m - behind
+            fits = (n >= 0) & (n < items)
+            gathers = fits & (n >= streams)
+            n = jnp.clip(n, 0, items - 1)
+            s = n % streams
+            held = jnp.maximum(n - streams, 0)
+            if what == "beside":
+                beside(m, which)
+            elif what == "arrive":
+
+                @pl.when(gathers)
+                def _():
+                    if which == 0:
+                        enter(n)
+                        gather.send(held)
+                    else:
+                        gather.arrive(which, held)
+
+            elif what == "compute":
+
+                @pl.when(gathers)
+                def _():
+                    for zb in range(line.chips):
+                        gather.wait_across(held, zb)
+                        sums.drain(s, zb)
+
+                @pl.when(fits)
+                def _():
+                    compute(n)
+                    for zb in range(line.chips):
+                        sums.across(s, zb).start()
+
+            elif what == "hop":
+                place, far = which
+
+                @pl.when(fits & (line.z == place))
+                def _():
+                    sums.hop_up(s, far)
+
+                @pl.when(fits & (line.z == last - place))
+                def _():
+                    sums.hop_down(s, last - far)
+
+            else:
+
+                @pl.when(fits)
+                def _():
+                    sums.finish(s, total)
+                    owner(n)
+
         return carry
 
     lax.fori_loop(0, items + times.turns - 1, body, 0)
-
-
-def computed_sum(line, sums, compute, totals, beside):
-    steps, chips = line.steps, line.chips
-
-    def body(t, carry):
-        @pl.when(t < steps)
-        def _():
-            compute(t)
-            for zb in range(chips):
-                sums.across(t, zb).start()
-
-        sums.hops(t - 1)
-        beside(t)
-        return carry
-
-    lax.fori_loop(0, steps * chips + 1 + (chips - 1) * LAG, body, 0)
-    for s in range(steps):
-        sums.finish(s, totals.at[s])
 
 
 def frame_mask(segments, places, rows):
@@ -675,14 +657,9 @@
     return (place_q == place_k) & (frame_k <= frame_q) & (segment_q == segment_k)
 
 
-def qkv_grads(start, left, dqkv, qk_grad, v_grad):
-    all_tokens, width = left.shape[0], v_grad.shape[0]
-    for i in range(3):
-        grad = mm_tn(left, dqkv[i].reshape(all_tokens, dqkv.shape[-1])).astype(BF16)
-        if i < 2:
-            qk_grad[pl.ds(pl.multiple_of(i * width + start, 256), 256)] = grad
-        else:
-            v_grad[pl.ds(pl.multiple_of(start, 256), 256)] = grad
+def column_grads(start, left, right, out):
+    rows = pl.ds(pl.multiple_of(start, 256), 256)
+    out[rows] = mm_tn(left, right.reshape(left.shape[0], right.shape[-1])).astype(BF16)
 
 
 def row_sum(value):
@@ -707,7 +684,8 @@
 def block(names, *refs):
     r = Refs(names, refs)
     steps, patches, width = r.x.shape
-    streams, heads, rows, _ = r.g_all.shape
+    streams, rows, _ = r.y.shape
+    heads = 2 * r.g_all.shape[1]
     line, t_line = Line(steps), Line(streams)
     chips, frames = line.chips, line.frames
     s_rows = patches // heads
@@ -719,7 +697,7 @@
     times = Timetable(chips, streams)
     sums = ChainSum(t_line, (r.part, r.sib, r.rise, r.fall, r.out), r.sum_sems)
     gather = Gather(t_line, r.gathered, r.gather_sems)
-    last_part = getattr(r, "last_part", r.part)
+    last_part = getattr(r, "last_part", r.g_all)
     last_out = getattr(r, "last_out", r.out)
     last_sums = ChainSum(
         line, (last_part, r.last_sib, r.last_rise, r.last_fall, last_out), r.last_sems
@@ -733,17 +711,22 @@
     state_swap = Swap(line, lambda s, to: r.state_src.at[s, to], r.state_dst, r.state_sems)
     grad_swap = Swap(line, lambda s, to: r.grad_src.at[s, to], r.grad_dst, r.grad_sems)
     y_swap = Swap(line, lambda s, to: r.y_src.at[s, to], r.y_dst, r.y_sems)
-    every = Everyone(line, (r.every_src, r.every_sib, r.every_line, r.every_frames), r.every_sems)
+    every = Everyone(
+        line,
+        (r.every_src, r.every_sib, r.every_line, r.every_frames, r.every_full),
+        r.every_sems,
+    )
     reduced = frame_sums(
         line,
         [
             (r.down_grad, 0, False), (r.up_grad, 0, True),
-            (r.t_qk, 0, False), (r.t_v, 0, True), (r.t_out, 1, True),
-            (r.s_qk, 0, False), (r.s_v, 0, True), (r.s_out, 1, True),
+            (r.t_q, 0, False), (r.t_k, 0, True), (r.t_v, 0, False), (r.t_out, 1, True),
+            (r.s_q, 0, False), (r.s_k, 0, True), (r.s_v, 0, False), (r.s_out, 1, True),
         ],
         r.reduce,
     )
-    mlp_sums, t_sums, s_sums = reduced[:2], reduced[2:5], reduced[5:]
+    mlp_sums, t_sums, s_sums = reduced[:2], reduced[2:6], reduced[6:]
+    bias_swap = Swap(line, lambda _, to: r.bias_src, r.bias_dst, r.bias_sems)
     line.barrier(True, True)
 
     def g_out(i, carry):
@@ -761,7 +744,8 @@
 
     def g_in(i):
         moved = r.g_dst[0, :, i // 2, i % 2].reshape(tokens, width).astype(BF16)
-        r.g_all[:, i] = mm(r.to_parts[...], moved).astype(BF16).reshape(streams, rows, width)
+        moved = mm(r.to_parts[...], moved).astype(BF16)
+        r.g_all[:, i // 2, i % 2] = moved.reshape(streams, rows, width)
 
     table_row = lax.broadcasted_iota(jnp.int32, (entries, width), 0)
 
@@ -881,7 +865,7 @@
         r.gathered[n, line.z, line.c] = norm(state, 2)
 
     def owner_mlp(s, n):
-        grad = r.g_all[s, line.h].astype(F32)
+        grad = r.g_all[s, line.z, line.c].astype(F32)
         back, gain_grad, shift_grad = norm_back(r.state2[s], r.total[...], r.gain[2:3, :])
         dh = grad + back
         r.grad2[s] = dh
@@ -929,13 +913,42 @@
     def t_out_chunk(i):
         left = r.t_mixed[...].reshape(all_tokens, columns)
         right = r.gathered[2 * streams : 3 * streams].reshape(all_tokens, width)
-        t_sums[2].part[...] = mm_tn(left, right).astype(BF16)
+        t_sums[3].part[...] = mm_tn(left, right).astype(BF16)
 
     def t_qkv_chunk(i):
         start = i * 256
         cols = pl.ds(pl.multiple_of(start, 256), 256)
         left = r.gathered[0:streams, :, :, :, cols].reshape(all_tokens, 256)
-        qkv_grads(start, left, r.t_dproj, t_sums[0].part, t_sums[1].part)
+        for j in range(3):
+            column_grads(start, left, r.t_dproj[j], t_sums[j].part)
+
+    def s_cols_chunk(_):
+        def from_streams(i, carry):
+            rows_of = pl.ds(pl.multiple_of(i * s_rows, s_rows), s_rows)
+            moved = mm(r.from_streams[...], r.s_dmixed[:, i].reshape(tokens, columns)).astype(BF16)
+            r.s_cols[:, rows_of] = moved.reshape(steps, s_rows, columns)
+            return carry
+
+        lax.fori_loop(0, heads, from_streams, 0)
+
+    def s_back_chunk(s):
+        dq, dk, dv = attend_back(r.s_proj[0, s], r.s_proj[1, s], r.s_proj[2, s], None, r.s_cols[s])
+        r.s_dproj[0, s] = dq
+        r.s_dproj[1, s] = dk
+        r.s_dproj[2, s] = dv
+        da = mm_nt(dq, r.s_wqkv[0]) + mm_nt(dk, r.s_wqkv[1]) + mm_nt(dv, r.s_wqkv[2])
+        last_part[s] = da.astype(BF16).reshape(last_part.shape[1:])
+        for zb in range(chips):
+            last_sums.across(s, zb).start()
+
+    def s_out_chunk(_):
+        left = r.s_mixed[...].reshape(all_tokens, columns)
+        right = r.gathered[3 * streams : 4 * streams].reshape(all_tokens, width)
+        s_sums[3].part[...] = mm_tn(left, right).astype(BF16)
+
+    def bias_chunk(_):
+        r.bias_src[...] = jnp.broadcast_to(r.up_bias_grad[...], r.bias_src.shape)
+        bias_swap.start(0)
 
     def g_in_chunk(i):
         @pl.when(i == 0)
@@ -947,12 +960,17 @@
     n_down, n_up = hidden // 128, width // 256
     turn_of = times.after
     mlp_turn, back_turn = turn_of(3 * streams - 1), turn_of(4 * streams - 1)
+    last_turn = turn_of(5 * streams - 1)
     chunks = (
         (streams + 1, 0, heads, g_in_chunk),
         (mlp_turn, 0, n_down, down_chunk),
         (mlp_turn, n_down, n_up, up_chunk),
+        (mlp_turn, n_down + n_up, 1, bias_chunk),
         (back_turn, 0, 1, t_out_chunk),
         (back_turn, 1, width // 256, t_qkv_chunk),
+        (last_turn, 0, 1, s_cols_chunk),
+        (last_turn, 1, steps, s_back_chunk),
+        (last_turn, 1 + steps, 1, s_out_chunk),
     )
     slots = [i for i in range(times.every) if i % 2 == 1][:3]
     per_turn = 2 * len(slots)
@@ -960,21 +978,26 @@
     stages = reduced[0].stages()
     bits = len(reduced[0].bits)
 
-    def moments_of(begin, first):
-        t, out = begin, []
-        for k in range(stages):
-            out.append(t)
-            halvings = k if k < bits else max(2 * bits - 1 - k, 0)
-            t += 2 + max(first >> halvings, 1)
-        return out
-
     def begin_of(turn, number):
         return (turn + number // per_turn) * times.every + times.every - 1
 
+    def moments_of(begin, waits):
+        out = [begin]
+        for k in range(1, stages):
+            half = k if k <= bits else 2 * bits + 1 - k
+            out.append(out[-1] + waits[min(half, len(waits)) - 1])
+        return out
+
     moments = (
-        (mlp_sums, moments_of(begin_of(mlp_turn, n_down + n_up), 10)),
-        (t_sums, moments_of(begin_of(back_turn, 1 + width // 256), 5)),
+        (mlp_sums, moments_of(begin_of(mlp_turn, n_down + n_up), MLP_WAITS)),
+        (t_sums, moments_of(begin_of(back_turn, 1 + width // 256), T_WAITS)),
     )
+    late = [
+        (k, sums_of)
+        for sums_of, steps_of in moments
+        for k, moment in enumerate(steps_of)
+        if moment // times.every >= turns
+    ]
 
     def beside(m, i):
         if i in slots:
@@ -1014,22 +1037,7 @@
     r.y_src[0] = y.astype(r.y_src.dtype).reshape(r.y_src.shape[1:])
     y_swap.start(0)
 
-    def from_streams(i, carry):
-        rows_of = pl.ds(pl.multiple_of(i * s_rows, s_rows), s_rows)
-        moved = mm(r.from_streams[...], r.s_dmixed[:, i].reshape(tokens, columns)).astype(BF16)
-        r.s_cols[:, rows_of] = moved.reshape(steps, s_rows, columns)
-        return carry
-
-    lax.fori_loop(0, heads, from_streams, 0)
     r.sums0[...] = jnp.zeros_like(r.sums0)
-
-    def compute_spatial_back(s):
-        dq, dk, dv = attend_back(r.s_proj[0, s], r.s_proj[1, s], r.s_proj[2, s], None, r.s_cols[s])
-        r.s_dproj[0, s] = dq
-        r.s_dproj[1, s] = dk
-        r.s_dproj[2, s] = dv
-        da = mm_nt(dq, r.s_wqkv[0]) + mm_nt(dk, r.s_wqkv[1]) + mm_nt(dv, r.s_wqkv[2])
-        last_part[s] = da.astype(BF16).reshape(last_part.shape[1:])
 
     def small_part(s):
         state = r.x[s].astype(F32) + added(s)
@@ -1039,7 +1047,7 @@
         r.sums0[1:2] += shift_grad
         r.sums0[8 : 8 + entries] += jnp.where(table_row == r.ids[s], row_sum(back), 0.0)
 
-    room = r.every_src.shape[1]
+    room = r.every_src.shape[0]
     filled = 9 + entries
 
     def small_value(own_grad):
@@ -1054,51 +1062,53 @@
         ]
         return jnp.concatenate(rows_of, axis=0)
 
-    s_moments = moments_of(steps + 1, 4)
-
-    def beside_last(t):
-        @pl.when(t == steps)
-        def _():
-            left = r.s_mixed[...].reshape(all_tokens, columns)
-            right = r.gathered[3 * streams : 4 * streams].reshape(all_tokens, width)
-            s_sums[2].part[...] = mm_tn(left, right).astype(BF16)
-
-        @pl.when((t >= steps) & (t < steps + 2))
-        def _():
-            for i in range(width // 512):
-                start = ((t - steps) * (width // 512) + i) * 256
-                cols = pl.ds(pl.multiple_of(start, 256), 256)
-                left = r.normed0[:, :, cols].reshape(all_tokens, 256)
-                qkv_grads(start, left, r.s_dproj, s_sums[0].part, s_sums[1].part)
-
-        for k in range(stages - 1):
-
-            @pl.when(t == s_moments[k])
+    def body(t, carry):
+        last_sums.hops(t)
+        for j in range(3):
+
+            @pl.when(t == j)
+            def _():
+                for i in range(width // 256):
+                    left = r.normed0[:, :, i * 256 : (i + 1) * 256].reshape(all_tokens, 256)
+                    column_grads(i * 256, left, r.s_dproj[j], s_sums[j].part)
+                s_sums[j].stage(0)
+                if j == 0:
+                    s_sums[3].stage(0)
+                    for k, sums_of in late:
+                        for one in sums_of:
+                            one.stage(k)
+
+        @pl.when((t >= 3) & (t < 3 + steps))
+        def _():
+            small_part(t - 3)
+
+        for k in range(1, stages - 1):
+
+            @pl.when(t == LAST_STAGES[min(k, 3) - 1] + 4 * max(k - 3, 0))
             def _():
                 for one in s_sums:
                     one.stage(k)
 
-        @pl.when((t >= steps + 2) & (t < 2 * steps + 2))
-        def _():
-            small_part(t - steps - 2)
-
-        @pl.when(t == 2 * steps + 2)
+        @pl.when(t == 3 + steps)
         def _():
             grad = r.grad1[...].reshape(tokens, width)
             own_grad = moved_exactly(r.from_streams[...], grad)
             r.state0[...] = own_grad.reshape(r.state0.shape)
             every.over_pair(small_value(own_grad))
 
-        @pl.when(t == 2 * steps + 4)
-        def _():
-            every.over_line()
-
-        @pl.when(t == 2 * steps + 7)
-        def _():
-            row = lax.broadcasted_iota(jnp.int32, (room, width), 0)
-            every.over_frames(jnp.where(row == filled, r.up_bias_grad[...], 0.0))
-
-    computed_sum(line, last_sums, compute_spatial_back, r.last_total, beside_last)
+        for moment, step in zip(LAST_SMALL, (every.over_line, every.over_frames, every.over_back)):
+
+            @pl.when(t == moment)
+            def _():
+                step()
+
+        return carry
+
+    bound = steps * (chips - 1) + (chips - 2) * LAG
+    bound = max(bound, LAST_SMALL[-1] + 1, LAST_STAGES[2] + 4 * max(stages - 5, 0) + 1)
+    lax.fori_loop(0, bound, body, 0)
+    for s in range(steps):
+        last_sums.finish(s, r.last_total.at[s])
     own_grad = r.state0[...].reshape(tokens, width)
     for s in range(steps):
         state = r.x[s, own_rows].astype(F32) + added(s)
@@ -1107,27 +1117,25 @@
     y_swap.wait(0)
     r.y_res[...] = mm(r.from_peers[...], r.y_dst[0].reshape(tokens, width).astype(BF16)).astype(BF16)
     r.small_res[...] = every.result()
-    for sums_of, steps_of in moments:
-        for k, moment in enumerate(steps_of):
-            if moment // times.every >= turns:
-                for one in sums_of:
-                    one.stage(k)
-    for k, moment in enumerate(s_moments):
-        if k == stages - 1:
-            for one in s_sums:
-                one.stage(k)
+    bias_swap.wait(0)
+    up_bias = r.bias_dst[0, 0]
+    for i in range(1, frames):
+        up_bias = up_bias + r.bias_dst[0, i]
+    r.up_bias_res[...] = up_bias
+    for one in s_sums:
+        one.stage(stages - 1)
     drain_all(line, (last_sums,), steps)
     drain_all(t_line, (gather,), 4 * streams)
 
 
 def finish(
-    t_qk, t_v, t_out, s_qk, s_v, s_out, up, down, y, grad, small,
+    t_q, t_k, t_v, t_out, s_q, s_k, s_v, s_out, up, down, y, grad, small, up_bias,
     y_res, grad_res, table_res, gain_res, shift_res, s_qkv_res, s_out_res, t_qkv_res, t_out_res,
     bias_res, up_res, up_bias_res, down_res,
 ):
-    for qk, v, res in ((t_qk, t_v, t_qkv_res), (s_qk, s_v, s_qkv_res)):
-        res[0:2] = qk[...].astype(F32)
-        res[2] = v[...].astype(F32)
+    for parts, res in (((t_q, t_k, t_v), t_qkv_res), ((s_q, s_k, s_v), s_qkv_res)):
+        for i, part in enumerate(parts):
+            res[i] = part[...].astype(F32)
     t_out_res[...] = t_out[...].astype(F32)
     s_out_res[...] = s_out[...].astype(F32)
     up_res[...] = up[...].astype(F32)
@@ -1137,16 +1145,15 @@
 
     @pl.when(pl.program_id(0) == 0)
     def _():
-        entries = table_res.shape[0]
         gain_res[...] = small[0:3]
         shift_res[...] = small[3:6]
         bias_res[...] = small[6:9]
-        table_res[...] = small[9 : 9 + entries]
-        up_bias_res[...] = small[9 + entries : 10 + entries, : up_bias_res.shape[1]]
+        table_res[...] = small[9 : 9 + table_res.shape[0]]
+        up_bias_res[...] = up_bias[0:1, : up_bias_res.shape[1]]
 
 
 def results(values, entries, hidden):
-    grid = 8
+    grid = 4
 
     def blocks(shape, sliced=True):
         axis = len(shape) - 2
@@ -1163,9 +1170,9 @@
 
         return pl.BlockSpec(tuple(block), index)
 
-    t_qk, t_v, t_out, _, _, _, g_up, g_down, y, grad, small = values
+    t_q, _, _, t_out, _, _, _, _, g_up, g_down, y, grad, small, up_bias = values
     width = g_up.shape[0]
-    qkv = ((3,) + t_qk.shape[1:], F32, True)
+    qkv = ((3,) + t_q.shape, F32, True)
     out = (t_out.shape, F32, True)
     few = ((3, width), F32, False)
     outs = [
@@ -1178,7 +1185,7 @@
         name="finish",
         grid=(grid,),
         out_shape=[jax.ShapeDtypeStruct(shape, kind) for shape, kind, _ in outs],
-        in_specs=[blocks(v.shape, v is not small) for v in values],
+        in_specs=[blocks(v.shape, v is not small and v is not up_bias) for v in values],
         out_specs=[blocks(shape, sliced) for shape, _, sliced in outs],
     )(*values)
 
@@ -1246,20 +1253,23 @@
         down=down_weight,
         **orders(steps, frames, places, streams),
     )
-    qk, v, out = (2 * width, columns), (width, columns), (columns, width)
+    qkv, out = (width, columns), (columns, width)
     down, up = (hidden, width), (width, hidden)
     outs = dict(
-        t_qk=(qk, BF16),
-        t_v=(v, BF16),
+        t_q=(qkv, BF16),
+        t_k=(qkv, BF16),
+        t_v=(qkv, BF16),
         t_out=(out, BF16),
-        s_qk=(qk, BF16),
-        s_v=(v, BF16),
+        s_q=(qkv, BF16),
+        s_k=(qkv, BF16),
+        s_v=(qkv, BF16),
         s_out=(out, BF16),
         up_grad=(up, BF16),
         down_grad=(down, BF16),
         y_res=((tokens, width), BF16),
         grad_res=((tokens, width), F32),
         small_res=((room, width), F32),
+        up_bias_res=((8, width), F32),
     )
     s_all = (steps, chips, 2, rows, width)
     t_all = (streams, chips, 2, t_rows, width)
@@ -1285,7 +1295,7 @@
         dpre=(streams, count, hidden),
         normed0=(steps, patches, width),
         gathered=(4 * streams,) + t_all[1:],
-        g_all=(streams, heads, t_rows, width),
+        g_all=t_all,
         part=t_all,
         sib=t_one,
         rise=t_one,
@@ -1321,11 +1331,15 @@
     scratch |= {name: pltpu.VMEM(whole, kind_of(whole)) for name in ("y_src", "y_dst")}
     every_shape = (room, width)
     scratch |= dict(
-        every_src=pltpu.VMEM((3,) + every_shape, BF16),
+        every_src=pltpu.VMEM(every_shape, BF16),
         every_sib=pltpu.VMEM(every_shape, BF16),
-        every_line=pltpu.VMEM((chips,) + every_shape, BF16),
-        every_frames=pltpu.VMEM((frames,) + every_shape, BF16),
-        every_sems=[pltpu.SemaphoreType.DMA((chips + frames,))] * 2,
+        every_line=pltpu.VMEM((chips, room, width // chips), BF16),
+        every_frames=pltpu.VMEM((frames, room, width // chips), BF16),
+        every_full=pltpu.VMEM(every_shape, BF16),
+        every_sems=[pltpu.SemaphoreType.DMA((2 * chips + frames,))] * 2,
+        bias_src=pltpu.VMEM((8, width), F32),
+        bias_dst=pltpu.VMEM((1, frames, 8, width), F32),
+        bias_sems=[pltpu.SemaphoreType.DMA((1, frames))] * 2,
         sum_sems=[pltpu.SemaphoreType.DMA((streams, chips))] * 5,
         last_sems=[pltpu.SemaphoreType.DMA((steps, chips))] * 5,
         gather_sems=[pltpu.SemaphoreType.DMA((4 * streams, chips))] * 5,
@@ -1335,9 +1349,7 @@
         y_sems=[pltpu.SemaphoreType.DMA((1, frames))] * 2,
         reduce=[
             x
-            for shape, dim in (
-                (down, 0), (up, 0), (qk, 0), (v, 0), (out, 1), (qk, 0), (v, 0), (out, 1)
-            )
+            for shape, dim in ((down, 0), (up, 0)) + 2 * (((qkv, 0),) * 3 + ((out, 1),))
             for x in frame_sum_scratch(frames, shape, dim)
         ],
     )
@@ -1357,8 +1369,6 @@
         ),
     )(*args.values())
     found = dict(zip(outs, parts))
-    for name in ("t_qk", "s_qk"):
-        found[name] = found[name].reshape(2, width, columns)
     (
         block_output, input_grad, table_grad, gain_grad, shift_grad, s_qkv_grad, s_out_grad,
         t_qkv_grad, t_out_grad, bias_grad, up_grad, up_bias_grad, down_grad,

time: 262 us -> 246 us (0.939)
  Pallas kernels: 261 us -> 245 us
    pallas_call x1, Pallas kernels: 252 us -> 238 us  [on_device(): pl.pallas_call(lambda *refs: block(names, *refs), name='block', out_shape...]
where the time goes in v4:
time: 246 us
  Pallas kernels  245 us (100%)
    pallas_call x1, Pallas kernels, on_device(): pl.pallas_call(lambda *refs: block(names, *refs), name='block', out_shape...  238 us
    pallas_call x1, Pallas kernels, results(): pl.pallas_call(finish, name='finish', grid=(grid,), out_shape=[jax.ShapeD...  6.68 us

profile of v4, /device:TPU:0, one launch (start us, length us, event | category | flops | bytes accessed | tf_op | source)
XLA Modules:
  0.0 245.6 jit_solution(18178359273652884306)
XLA Ops:
  0.7 238.1 %block.1 = (bf16[1024,128]{1,0:T(8,128)(2,1)}, bf16[1024,128]{1,0:T(8,128)(2,1)}, bf16[1024,128]{1,0:T(8,128)(2,1)}, bf16[128,1024]{1,0:T(8,128)(2,1)}, bf16[102...) custom-call(s32[4]{0:T(128)} %refs_0_.1, ...), custom_call_target="tpu_custom_call" | custom-call | tf_op jit(solution)/shard_map/block/pallas_call | solution.py:1357
  238.8 6.7 %finish.1 = (bf16[128,1024]{1,0:T(8,128)(2,1)}, f32[128,1024]{1,0:T(8,128)}, f32[8,1024]{1,0:T(8,128)}, f32[3,1024]{1,0:T(4,128)}, f32[3,1024]{1,0:T(4,128)}, /*...) custom-call(bf16[1024,128]{1,0:T(8,128)(2,1)} %get-tuple-element.40., ...), custom_call_target="tpu_custom_call" | custom-call | tf_op jit(solution)/shard_map/finish/pallas_call | solution.py:1183

commit v5 on v4

--- a/solution.py
+++ b/solution.py
@@ -13,6 +13,9 @@
 F32 = jnp.float32
 BF16 = jnp.bfloat16
 MESH = pl.DeviceIdType.MESH
+MLP_RESULTS = ("down_grad", "up_grad")
+T_RESULTS = ("t_q", "t_k", "t_v", "t_out")
+S_RESULTS = ("s_q", "s_k", "s_v", "s_out")
 VMEM_LIMIT = 62 * 1024 * 1024
 GELU_C = float(np.sqrt(2.0 / np.pi))
 LAG = 2
@@ -20,7 +23,7 @@
 T_WAITS = (9, 6)
 LAST_STAGES = (8, 11, 14)
 LAST_SMALL = (9, 12, 15)
-HOP_US, SIBLING_US, COMPUTE_US, LINK_US, OWNER_US = 3.4, 0.6, 0.6, 1.45, 0.4
+HOP_US, SIBLING_US, COMPUTE_US, LINK_US, OWNER_US, SWAP_US = 3.4, 1.0, 1.6, 1.45, 0.6, 4.0
 
 
 def mm(a, b):
@@ -546,97 +549,124 @@
 
 
 class Timetable:
+    PHASES = 5
+
     def __init__(self, chips, streams):
+        self.chips, self.streams = chips, streams
         last = chips - 1
-        self.chips, self.streams = chips, streams
-        steps = [(d * HOP_US, "arrive", d) for d in range(chips)]
-        self.compute = last * HOP_US + SIBLING_US
-        steps.append((self.compute, "compute", 0))
-        first = self.compute + COMPUTE_US + SIBLING_US
+        arrivals = [(d * HOP_US, "arrive", d) for d in range(chips)]
+        gathered = last * HOP_US + SIBLING_US
+        first = self.sum_steps(0.0)
+        middle = self.sum_steps(gathered)
+        self.turn = max((middle[-1][0] + OWNER_US) / streams, chips * LINK_US)
+        period = self.turn * streams
+        second = max(HOP_US, SIBLING_US + COMPUTE_US + SIBLING_US)
+        y = self.sum_steps(second - COMPUTE_US - SIBLING_US)
+        leads = [0.0, first[-1][0] + OWNER_US + SWAP_US - period]
+        leads.append(leads[1] + max(middle[-1][0] + OWNER_US + SWAP_US - period, 0.0))
+        groups = (
+            (0, 0, leads[0], first),
+            (1, 3, leads[1], arrivals + middle),
+            (4, 4, leads[2], arrivals + [(gathered, "gathered", 0)] + y),
+        )
+        self.every = 6
+        self.order = []
+        for i in range(self.every):
+            at = (i + 0.5) * self.turn / self.every
+            self.order.append((at, 0.0, "beside", i, 0, 0, 0))
+        self.computed = {}
+        self.turns = 0
+        for low, high, lead, steps in groups:
+            for t, what, which in steps:
+                t += lead
+                behind = int(np.floor(t / self.turn))
+                at = t - behind * self.turn
+                self.order.append((at, -t, what, which, behind, low, high))
+                if what == ("gathered" if low == 4 else "compute"):
+                    self.computed |= {phase: behind for phase in range(low, high + 1)}
+                self.turns = max(self.turns, (high + 1) * streams + behind)
+        self.order.sort(key=lambda step: step[:2])
+
+    def sum_steps(self, compute):
+        last = self.chips - 1
+        steps = [(compute, "compute", 0)]
+        start = compute + COMPUTE_US + SIBLING_US
         hops = {}
         for place in range(last):
-            t = first
+            t = start
             for far in range(last, place, -1):
                 if place:
                     t = max(t, hops[place - 1, far] + HOP_US)
                 hops[place, far] = t
                 steps.append((t, "hop", (place, far)))
                 t += LINK_US
-        owner = max(hops[far - 1, far] for far in range(1, chips)) + HOP_US
-        steps.append((owner, "owner", 0))
-        self.turn = max((owner + OWNER_US) / streams, chips * LINK_US)
-        self.turns = int(owner / self.turn) + 1
-        self.every = 6
-        steps += [((i + 0.5) * self.turn / self.every, "beside", i) for i in range(self.every)]
-        self.order = []
-        for t, what, which in steps:
-            behind = int(t / self.turn)
-            self.order.append((t - behind * self.turn, -t, what, which, behind))
-        self.order.sort(key=lambda step: step[:2])
+        owner = max(hops[far - 1, far] for far in range(1, self.chips)) + HOP_US
+        return steps + [(owner, "owner", 0)]
 
     def after(self, item):
-        return item + int(self.compute / self.turn) + 1
-
-
-def pipeline(line, times, gather, sums, phases, enter, compute, owner, total, beside):
+        return item + self.computed[item // self.streams] + 1
+
+
+def pipeline(line, times, turns, gather, sums, enter, compute, gathered, owner, total, beside):
     last, streams = line.chips - 1, times.streams
-    items = phases * streams
 
     def body(m, carry):
-        for _, _, what, which, behind in times.order:
-            n = m - behind
-            fits = (n >= 0) & (n < items)
-            gathers = fits & (n >= streams)
-            n = jnp.clip(n, 0, items - 1)
-            s = n % streams
-            held = jnp.maximum(n - streams, 0)
+        for _, _, what, which, behind, low, high in times.order:
             if what == "beside":
                 beside(m, which)
-            elif what == "arrive":
-
-                @pl.when(gathers)
+                continue
+            n = m - behind
+            fits = (n >= low * streams) & (n < (high + 1) * streams)
+            n = jnp.clip(n, low * streams, (high + 1) * streams - 1)
+            s = n % streams
+            held = n - streams
+            if what == "hop":
+                place, far = which
+
+                @pl.when(fits & (line.z == place))
                 def _():
+                    sums.hop_up(s, far)
+
+                @pl.when(fits & (line.z == last - place))
+                def _():
+                    sums.hop_down(s, last - far)
+
+                continue
+
+            @pl.when(fits)
+            def _():
+                if what == "arrive":
                     if which == 0:
                         enter(n)
                         gather.send(held)
                     else:
                         gather.arrive(which, held)
-
-            elif what == "compute":
-
-                @pl.when(gathers)
-                def _():
+                elif what == "compute":
+                    if low == 4:
+                        gather.wait_across(held, line.z)
                     for zb in range(line.chips):
-                        gather.wait_across(held, zb)
-                        sums.drain(s, zb)
-
-                @pl.when(fits)
-                def _():
-                    compute(n)
+                        if 1 <= low <= 3:
+                            gather.wait_across(held, zb)
+                        if low:
+                            sums.drain(s, zb)
+                    compute(n, low, high)
                     for zb in range(line.chips):
                         sums.across(s, zb).start()
-
-            elif what == "hop":
-                place, far = which
-
-                @pl.when(fits & (line.z == place))
-                def _():
-                    sums.hop_up(s, far)
-
-                @pl.when(fits & (line.z == last - place))
-                def _():
-                    sums.hop_down(s, last - far)
-
-            else:
-
-                @pl.when(fits)
-                def _():
+                elif what == "gathered":
+                    for zb in range(line.chips):
+
+                        @pl.when(line.z != zb)
+                        def _():
+                            gather.wait_across(held, zb)
+
+                    gathered(n)
+                else:
                     sums.finish(s, total)
-                    owner(n)
+                    owner(n, low, high)
 
         return carry
 
-    lax.fori_loop(0, items + times.turns - 1, body, 0)
+    lax.fori_loop(0, turns, body, 0)
 
 
 def frame_mask(segments, places, rows):
@@ -681,8 +711,12 @@
             setattr(self, name, ref)
 
 
-def block(names, *refs):
-    r = Refs(names, refs)
+def block(fetched, results, names, *refs):
+    ends = len(fetched), len(fetched) + len(results)
+    r = Refs(names, refs[ends[1] :])
+    r.fetched = dict(zip(fetched, refs))
+    r.stored = dict(zip(results, refs[ends[0] :]))
+    r.ids, r.segments = r.fetched.pop("ids"), r.fetched.pop("segments")
     steps, patches, width = r.x.shape
     streams, rows, _ = r.y.shape
     heads = 2 * r.g_all.shape[1]
@@ -727,7 +761,23 @@
     )
     mlp_sums, t_sums, s_sums = reduced[:2], reduced[2:6], reduced[6:]
     bias_swap = Swap(line, lambda _, to: r.bias_src, r.bias_dst, r.bias_sems)
+    fetches = [
+        pltpu.make_async_copy(r.fetched[name], getattr(r, name), r.fetch_sems.at[i])
+        for i, name in enumerate(r.fetched)
+    ]
+    for fetch in fetches:
+        fetch.start()
     line.barrier(True, True)
+    for fetch in fetches:
+        fetch.wait()
+    stored = []
+
+    def store(name):
+        i = list(r.stored).index(name)
+        stored.append(
+            pltpu.make_async_copy(getattr(r, name), r.stored[name], r.store_sems.at[i])
+        )
+        stored[-1].start()
 
     def g_out(i, carry):
         rows_of = pl.ds(pl.multiple_of(i * s_rows, s_rows), s_rows)
@@ -847,10 +897,12 @@
         da = mm_nt(dq, r.t_wqkv[0]) + mm_nt(dk, r.t_wqkv[1]) + mm_nt(dv, r.t_wqkv[2])
         r.part[s] = da.astype(BF16).reshape(chips, 2, rows, width)
 
-    def compute_last(s, n):
+    def gathered_last(n):
         grad = r.gathered[held(n)].reshape(count, width)
         moved = mm_nt(grad, r.s_wout[...]).astype(BF16)
-        r.s_dmixed[s] = moved.reshape(heads, rows, columns)
+        r.s_dmixed[n % streams] = moved.reshape(heads, rows, columns)
+
+    def compute_last(s, n):
         y = mm(r.act[s], r.down[...])
         r.part[s] = y.astype(BF16).reshape(chips, 2, rows, width)
 
@@ -888,9 +940,9 @@
         r.y[s] = (r.state2[s] + r.total[...] + r.bias[2:3, :]).astype(BF16)
 
     def by_phase(bodies):
-        def run(n):
+        def run(n, low=0, high=4):
             for i, one in enumerate(bodies):
-                if one is not None:
+                if one is not None and low <= i <= high:
 
                     @pl.when(n // streams == i)
                     def _():
@@ -974,7 +1026,7 @@
     )
     slots = [i for i in range(times.every) if i % 2 == 1][:3]
     per_turn = 2 * len(slots)
-    turns = 5 * streams + times.turns - 1
+    turns = max(times.turns, last_turn + -(-(steps + 2) // per_turn))
     stages = reduced[0].stages()
     bits = len(reduced[0].bits)
 
@@ -1030,8 +1082,14 @@
         (compute_spatial, compute_temporal, compute_mlp, compute_back, compute_last)
     )
     owner = by_phase((owner_spatial, owner_temporal, owner_mlp, owner_back, owner_last))
-    pipeline(t_line, times, gather, sums, 5, enter, compute, owner, r.total, beside)
+    pipeline(
+        t_line, times, turns, gather, sums, enter, compute, gathered_last, owner, r.total, beside
+    )
     drain_all(t_line, (sums,), streams)
+    for sums_of, group in ((mlp_sums, MLP_RESULTS), (t_sums, T_RESULTS)):
+        if (stages - 1, sums_of) not in late:
+            for name in group:
+                store(name)
 
     y = mm(r.from_parts[...], r.y[...].reshape(tokens, width)).astype(BF16)
     r.y_src[0] = y.astype(r.y_src.dtype).reshape(r.y_src.shape[1:])
@@ -1122,72 +1180,93 @@
     for i in range(1, frames):
         up_bias = up_bias + r.bias_dst[0, i]
     r.up_bias_res[...] = up_bias
+    for name in ("grad_res", "y_res", "small_res", "up_bias_res"):
+        store(name)
     for one in s_sums:
         one.stage(stages - 1)
+    for sums_of, group in ((mlp_sums, MLP_RESULTS), (t_sums, T_RESULTS)):
+        if (stages - 1, sums_of) in late:
+            for name in group:
+                store(name)
+    for name in S_RESULTS:
+        store(name)
     drain_all(line, (last_sums,), steps)
     drain_all(t_line, (gather,), 4 * streams)
-
-
-def finish(
-    t_q, t_k, t_v, t_out, s_q, s_k, s_v, s_out, up, down, y, grad, small, up_bias,
-    y_res, grad_res, table_res, gain_res, shift_res, s_qkv_res, s_out_res, t_qkv_res, t_out_res,
-    bias_res, up_res, up_bias_res, down_res,
-):
-    for parts, res in (((t_q, t_k, t_v), t_qkv_res), ((s_q, s_k, s_v), s_qkv_res)):
-        for i, part in enumerate(parts):
-            res[i] = part[...].astype(F32)
-    t_out_res[...] = t_out[...].astype(F32)
-    s_out_res[...] = s_out[...].astype(F32)
-    up_res[...] = up[...].astype(F32)
-    down_res[...] = down[...].astype(F32)
-    y_res[...] = y[...]
-    grad_res[...] = grad[...]
-
-    @pl.when(pl.program_id(0) == 0)
-    def _():
-        gain_res[...] = small[0:3]
-        shift_res[...] = small[3:6]
-        bias_res[...] = small[6:9]
-        table_res[...] = small[9 : 9 + table_res.shape[0]]
-        up_bias_res[...] = up_bias[0:1, : up_bias_res.shape[1]]
-
-
-def results(values, entries, hidden):
-    grid = 4
-
-    def blocks(shape, sliced=True):
-        axis = len(shape) - 2
-        block = list(shape)
-        if sliced:
-            block[axis] //= grid
-        place = [0] * len(shape)
-
-        def index(i):
-            at = list(place)
-            if sliced:
-                at[axis] = i
-            return tuple(at)
-
-        return pl.BlockSpec(tuple(block), index)
-
-    t_q, _, _, t_out, _, _, _, _, g_up, g_down, y, grad, small, up_bias = values
-    width = g_up.shape[0]
-    qkv = ((3,) + t_q.shape, F32, True)
-    out = (t_out.shape, F32, True)
-    few = ((3, width), F32, False)
-    outs = [
-        (y.shape, BF16, True), (grad.shape, F32, True), ((entries, width), F32, False), few, few,
-        qkv, out, qkv, out, few,
-        (g_up.shape, F32, True), ((1, hidden), F32, False), (g_down.shape, F32, True),
-    ]
-    return pl.pallas_call(
-        finish,
+    for one in stored:
+        one.wait()
+
+
+def finish(names, parts, *refs):
+    sources = dict(zip(names, refs))
+    results = dict(zip(parts, refs[len(names) :]))
+    held = refs[len(names) + len(parts) :]
+    sems_in, sems_out = held[-2:]
+    local = dict(zip(names, held))
+    made = dict(zip(parts, held[len(names) :]))
+    loads = {
+        name: pltpu.make_async_copy(sources[name], local[name], sems_in.at[i])
+        for i, name in enumerate(names)
+    }
+    for load in loads.values():
+        load.start()
+    loaded, stores = set(), []
+    for i, (name, given) in enumerate(parts.items()):
+        for j, (source, low, high, columns) in enumerate(given):
+            if source not in loaded:
+                loads[source].wait()
+                loaded.add(source)
+            value = local[source][low:high, :columns].astype(made[name].dtype)
+            if len(given) > 1:
+                made[name][j] = value
+            else:
+                made[name][...] = value
+        stores.append(pltpu.make_async_copy(made[name], results[name], sems_out.at[i]))
+        stores[-1].start()
+    for store in stores:
+        store.wait()
+
+
+def results(found, entries):
+    width, hidden = found["up_grad"].shape
+
+    def whole(name):
+        rows, columns = found[name].shape
+        return [(name, 0, rows, columns)]
+
+    parts = {
+        "down": whole("down_grad"),
+        "up": whole("up_grad"),
+        "t_qkv": whole("t_q") + whole("t_k") + whole("t_v"),
+        "t_out": whole("t_out"),
+        "grad": whole("grad_res"),
+        "y": whole("y_res"),
+        "gain": [("small_res", 0, 3, width)],
+        "shift": [("small_res", 3, 6, width)],
+        "bias": [("small_res", 6, 9, width)],
+        "table": [("small_res", 9, 9 + entries, width)],
+        "up_bias": [("up_bias_res", 0, 1, hidden)],
+        "s_out": whole("s_out"),
+        "s_qkv": whole("s_q") + whole("s_k") + whole("s_v"),
+    }
+    shapes = []
+    for name, given in parts.items():
+        _, low, high, columns = given[0]
+        lead = (len(given),) if len(given) > 1 else ()
+        kind = BF16 if name == "y" else F32
+        shapes.append(jax.ShapeDtypeStruct(lead + (high - low, columns), kind))
+    names = tuple(found)
+    made = pl.pallas_call(
+        lambda *refs: finish(names, parts, *refs),
         name="finish",
-        grid=(grid,),
-        out_shape=[jax.ShapeDtypeStruct(shape, kind) for shape, kind, _ in outs],
-        in_specs=[blocks(v.shape, v is not small and v is not up_bias) for v in values],
-        out_specs=[blocks(shape, sliced) for shape, _, sliced in outs],
-    )(*values)
+        out_shape=shapes,
+        in_specs=[pl.BlockSpec(memory_space=pltpu.HBM)] * len(names),
+        out_specs=[pl.BlockSpec(memory_space=pltpu.HBM)] * len(shapes),
+        scratch_shapes=[pltpu.VMEM(v.shape, v.dtype) for v in found.values()]
+        + [pltpu.VMEM(v.shape, v.dtype) for v in shapes]
+        + [pltpu.SemaphoreType.DMA((len(names),)), pltpu.SemaphoreType.DMA((len(shapes),))],
+        compiler_params=pltpu.CompilerParams(vmem_limit_bytes=VMEM_LIMIT),
+    )(*found.values())
+    return dict(zip(parts, made))
 
 
 def orders(frames_local, frames, places, streams):
@@ -1353,41 +1432,42 @@
             for x in frame_sum_scratch(frames, shape, dim)
         ],
     )
-    names = tuple(args) + tuple(outs) + tuple(scratch)
+    held = {k: v for k, v in args.items() if k not in ("ids", "segments")}
+    scratch |= {name: pltpu.VMEM(v.shape, v.dtype) for name, v in held.items()}
+    scratch |= {name: pltpu.VMEM(shape, kind) for name, (shape, kind) in outs.items()}
+    scratch["fetch_sems"] = pltpu.SemaphoreType.DMA((len(held),))
+    scratch["store_sems"] = pltpu.SemaphoreType.DMA((len(outs),))
+    fetched, results_of, names = tuple(args), tuple(outs), tuple(scratch)
     parts = pl.pallas_call(
-        lambda *refs: block(names, *refs),
+        lambda *refs: block(fetched, results_of, names, *refs),
         name="block",
         out_shape=[jax.ShapeDtypeStruct(shape, kind) for shape, kind in outs.values()],
         in_specs=[
-            pl.BlockSpec(memory_space=pltpu.SMEM if name in ("ids", "segments") else pltpu.VMEM)
+            pl.BlockSpec(memory_space=pltpu.HBM if name in held else pltpu.SMEM)
             for name in args
         ],
-        out_specs=[pl.BlockSpec(memory_space=pltpu.VMEM)] * len(outs),
+        out_specs=[pl.BlockSpec(memory_space=pltpu.HBM)] * len(outs),
         scratch_shapes=list(scratch.values()),
         compiler_params=pltpu.CompilerParams(
             collective_id=0, has_side_effects=True, vmem_limit_bytes=VMEM_LIMIT
         ),
     )(*args.values())
-    found = dict(zip(outs, parts))
-    (
-        block_output, input_grad, table_grad, gain_grad, shift_grad, s_qkv_grad, s_out_grad,
-        t_qkv_grad, t_out_grad, bias_grad, up_grad, up_bias_grad, down_grad,
-    ) = results(list(found.values()), entries, hidden)
+    made = results(dict(zip(outs, parts)), entries)
     s_blocks = (steps, rows, width)
     return (
-        block_output.reshape(s_blocks),
-        input_grad.reshape(s_blocks),
-        table_grad,
-        gain_grad,
-        shift_grad,
-        s_qkv_grad.transpose(1, 0, 2),
-        s_out_grad,
-        t_qkv_grad.transpose(1, 0, 2),
-        t_out_grad,
-        bias_grad,
-        up_grad,
-        up_bias_grad.reshape(hidden),
-        down_grad,
+        made["y"].reshape(s_blocks),
+        made["grad"].reshape(s_blocks),
+        made["table"],
+        made["gain"],
+        made["shift"],
+        made["s_qkv"].transpose(1, 0, 2),
+        made["s_out"],
+        made["t_qkv"].transpose(1, 0, 2),
+        made["t_out"],
+        made["bias"],
+        made["up"],
+        made["up_bias"].reshape(hidden),
+        made["down"],
     )
 
 

time: 246 us -> 224 us (0.911)
  Pallas kernels: 245 us -> 223 us
    pallas_call x2, Pallas kernels: 245 us -> 223 us  [the longest x1 217 us: on_device(): pl.pallas_call(lambda *refs: block(fetched, results_of, names, *refs), na...]
where the time goes in v5:
time: 224 us
  Pallas kernels  223 us (100%)
    pallas_call x1, Pallas kernels, on_device(): pl.pallas_call(lambda *refs: block(fetched, results_of, names, *refs), na...  217 us
    pallas_call x1, Pallas kernels, results(): pl.pallas_call(lambda *refs: finish(names, parts, *refs), name='finish',...  6.14 us

profile of v5, /device:TPU:0, one launch (start us, length us, event | category | flops | bytes accessed | tf_op | source)
XLA Modules:
  0.0 224.1 jit_solution(3421054383306113278)
XLA Ops:
  0.7 217.2 %block.1 = (bf16[1024,128]{1,0:T(8,128)(2,1)}, bf16[1024,128]{1,0:T(8,128)(2,1)}, bf16[1024,128]{1,0:T(8,128)(2,1)}, bf16[128,1024]{1,0:T(8,128)(2,1)}, bf16[102...) custom-call(s32[4]{0:T(128)} %refs_0_.1, ...), custom_call_target="tpu_custom_call" | custom-call | tf_op jit(solution)/shard_map/block/pallas_call | solution.py:1441
  217.8 6.1 %finish.1 = (f32[512,1024]{1,0:T(8,128)}, f32[1024,512]{1,0:T(8,128)}, f32[3,1024,128]{2,1,0:T(8,128)}, f32[128,1024]{1,0:T(8,128)}, f32[128,1024]{1,0:T(8,128)}...) custom-call(bf16[1024,128]{1,0:T(8,128)(2,1)} %get-tuple-element.40., ...), custom_call_target="tpu_custom_call" | custom-call | tf_op jit(solution)/shard_map/finish/pallas_call | solution.py:1258

commit v6 on v5

--- a/solution.py
+++ b/solution.py
@@ -19,11 +19,12 @@
 VMEM_LIMIT = 62 * 1024 * 1024
 GELU_C = float(np.sqrt(2.0 / np.pi))
 LAG = 2
-MLP_WAITS = (13, 8)
-T_WAITS = (9, 6)
-LAST_STAGES = (8, 11, 14)
-LAST_SMALL = (9, 12, 15)
-HOP_US, SIBLING_US, COMPUTE_US, LINK_US, OWNER_US, SWAP_US = 3.4, 1.0, 1.6, 1.45, 0.6, 4.0
+SLOT_US, STEP_US, FRAME_US, MLP_US, ATTENTION_US, LAST_FRAME_US = 1.15, 1.45, 4.5, 5.8, 2.9, 3.6
+CHUNK_US, WHOLE_US = 1.45, 100.0
+ADJUST = {}
+LAST_GRADS = 3
+LAST_SMALL = (5, 6, 9, 12)
+HOP_US, SIBLING_US, COMPUTE_US, LINK_US, OWNER_US, SWAP_US = 3.4, 1.0, 2.0, 1.45, 1.0, 4.0
 
 
 def mm(a, b):
@@ -410,65 +411,101 @@
             self.spans.append((keep, give, size, peer))
             start = keep
 
-    def view(self, ref, start, size):
+    def view(self, ref, start, size, step):
         if self.dim == 0:
-            return ref.at[pl.ds(pl.multiple_of(start, size), size)]
-        return ref.at[:, pl.ds(pl.multiple_of(start, size), size)]
-
-    def out(self, i):
+            return ref.at[pl.ds(pl.multiple_of(start, step), size)]
+        return ref.at[:, pl.ds(pl.multiple_of(start, step), size)]
+
+    def out(self, i, chunk=0, chunks=1):
         _, give, size, peer = self.spans[i]
-        src = self.view(self.part, give, size)
-        return self.line.copy(src, self.recv_bufs[i], self.sent.at[i], self.got.at[i], peer)
-
-    def back(self, i):
+        step = size // chunks
+        src = self.view(self.part, give + chunk * step, step, step)
+        dst = self.view(self.recv_bufs[i], chunk * step, step, step)
+        return self.line.copy(src, dst, self.sent.at[i], self.got.at[i], peer)
+
+    def back(self, i, chunk=0, chunks=1):
         keep, _, size, peer = self.spans[i]
-        ref = self.view(self.full, keep, size)
+        step = size // chunks
+        ref = self.view(self.full, keep + chunk * step, step, step)
         return self.line.copy(ref, ref, self.sent_back.at[i], self.got_back.at[i], peer)
 
     def back_in(self, i):
         _, give, size, peer = self.spans[i]
-        ref = self.view(self.full, give, size)
+        ref = self.view(self.full, give, size, size)
         return self.line.copy(ref, ref, self.sent_back.at[i], self.got_back.at[i], peer)
 
-    def stages(self):
-        return 2 * len(self.bits) + 1
-
-    def stage(self, k):
+    def send(self, k, chunk=0, chunks=1):
         n = len(self.bits)
-        if 1 <= k <= n:
-            keep, _, size, _ = self.spans[k - 1]
-            self.out(k - 1).wait()
-            ref = self.view(self.part, keep, size)
-            to = self.view(self.full, keep, size) if k == n else ref
-            to[...] = (ref[...].astype(F32) + self.recv_bufs[k - 1][...].astype(F32)).astype(BF16)
-        elif k > n:
-            i = 2 * n - k
+        if k < n:
+            self.out(k, chunk, chunks).start()
+        else:
+            self.back(2 * n - 1 - k, chunk, chunks).start()
+
+    def end(self, k):
+        n = len(self.bits)
+        if k < n:
+            keep, _, size, _ = self.spans[k]
+            self.out(k).wait()
+            ref = self.view(self.part, keep, size, size)
+            to = self.view(self.full, keep, size, size) if k == n - 1 else ref
+            to[...] = (ref[...].astype(F32) + self.recv_bufs[k][...].astype(F32)).astype(BF16)
+        else:
+            i = 2 * n - 1 - k
             self.back(i).wait_send()
             self.back_in(i).wait_recv()
-        if k < n:
-            self.out(k).start()
-        elif k < 2 * n:
-            self.back(2 * n - 1 - k).start()
-
-
-def frame_sum_scratch(frames, shape, dim):
+
+
+def frame_sum_scratch(frames, shape, dim, pieces):
     bits = frames.bit_length() - 1
-    scratch = []
-    for i in range(bits):
-        part = list(shape)
-        part[dim] = shape[dim] >> (i + 1)
-        scratch.append(pltpu.VMEM(tuple(part), BF16))
-    return [pltpu.VMEM(shape, BF16)] + scratch + [pltpu.SemaphoreType.DMA((bits,))] * 4
+    scratch = [pltpu.VMEM(shape, BF16)]
+    for _ in range(pieces):
+        for i in range(bits):
+            part = list(shape)
+            part[dim] = (shape[dim] // pieces) >> (i + 1)
+            scratch.append(pltpu.VMEM(tuple(part), BF16))
+        scratch += [pltpu.SemaphoreType.DMA((bits,))] * 4
+    return scratch
 
 
 def frame_sums(line, arrays, scratch):
     bits = line.frames.bit_length() - 1
-    sums = []
-    for full, dim, reverse in arrays:
-        part, *mine = scratch[: bits + 5]
-        scratch = scratch[bits + 5 :]
-        sums.append(FrameSum(line, part, full, dim, reverse, mine[:bits], mine[bits:]))
-    return sums
+    out = []
+    for full, dim, reverse, pieces in arrays:
+        part, scratch = scratch[0], scratch[1:]
+        sums = []
+        for i in range(pieces):
+            mine, scratch = scratch[: bits + 4], scratch[bits + 4 :]
+            size = full.shape[dim] // pieces
+            at = (slice(None),) * dim + (pl.ds(i * size, size),)
+            views = (part.at[at], full.at[at]) if pieces > 1 else (part, full)
+            sums.append(FrameSum(line, *views, dim, reverse, mine[:bits], mine[bits:]))
+        out.append((part, sums))
+    return out
+
+
+def stage_times(sums, begins, first, bits, free, latency, chunk_us):
+    ready = list(begins)
+    plan = []
+    for k in range(2 * bits):
+        for i, group in enumerate(sums):
+            length = first / 2 ** (k if k < bits else 2 * bits - 1 - k)
+            chunks = 1 << max(int(np.log2(length / chunk_us) + 0.5), 0)
+            start = max(free, ready[i])
+            for j in range(chunks):
+                plan.append((start + j * length / chunks, len(plan), ("send", group, k, j, chunks)))
+            free = start + length
+            ready[i] = free + latency
+            plan.append((ready[i], len(plan), ("end", group, k, 0, 0)))
+    return plan, free
+
+
+def run_step(step):
+    what, group, k, chunk, chunks = step
+    for one in group:
+        if what == "send":
+            one.send(k, chunk, chunks)
+        else:
+            one.end(k)
 
 
 class Everyone:
@@ -578,7 +615,7 @@
         self.turns = 0
         for low, high, lead, steps in groups:
             for t, what, which in steps:
-                t += lead
+                t += lead + ADJUST.get((low, what, which), 0.0)
                 behind = int(np.floor(t / self.turn))
                 at = t - behind * self.turn
                 self.order.append((at, -t, what, which, behind, low, high))
@@ -602,6 +639,10 @@
                 t += LINK_US
         owner = max(hops[far - 1, far] for far in range(1, self.chips)) + HOP_US
         return steps + [(owner, "owner", 0)]
+
+    def y_owner(self, item):
+        t = [t for t in self.order if t[2] == "owner" and t[5] == 4][0]
+        return (item + t[4]) * self.every + int(t[0] / self.turn * self.every + 0.5)
 
     def after(self, item):
         return item + self.computed[item // self.streams] + 1
@@ -733,6 +774,7 @@
     gather = Gather(t_line, r.gathered, r.gather_sems)
     last_part = getattr(r, "last_part", r.g_all)
     last_out = getattr(r, "last_out", r.out)
+    last_total = getattr(r, "last_total", r.grad2)
     last_sums = ChainSum(
         line, (last_part, r.last_sib, r.last_rise, r.last_fall, last_out), r.last_sems
     )
@@ -750,16 +792,25 @@
         (r.every_src, r.every_sib, r.every_line, r.every_frames, r.every_full),
         r.every_sems,
     )
-    reduced = frame_sums(
+    (
+        (down_part, down_sums), (up_part, up_sums),
+        (t_q_part, t_q_sums), (t_k_part, t_k_sums), (t_v_part, t_v_sums), (t_out_part, t_out_sums),
+        (s_q_part, s_q_sums), (s_k_part, s_k_sums), (s_v_part, s_v_sums), (s_out_part, s_out_sums),
+    ) = frame_sums(
         line,
         [
-            (r.down_grad, 0, False), (r.up_grad, 0, True),
-            (r.t_q, 0, False), (r.t_k, 0, True), (r.t_v, 0, False), (r.t_out, 1, True),
-            (r.s_q, 0, False), (r.s_k, 0, True), (r.s_v, 0, False), (r.s_out, 1, True),
+            (r.down_grad, 0, False, 2), (r.up_grad, 0, True, 2),
+            (r.t_q, 0, False, 1), (r.t_k, 0, True, 1), (r.t_v, 0, False, 1), (r.t_out, 1, True, 1),
+            (r.s_q, 0, False, 1), (r.s_k, 0, True, 1), (r.s_v, 0, False, 1), (r.s_out, 1, True, 1),
         ],
         r.reduce,
     )
-    mlp_sums, t_sums, s_sums = reduced[:2], reduced[2:6], reduced[6:]
+    t_parts = t_q_part, t_k_part, t_v_part
+    s_parts = s_q_part, s_k_part, s_v_part
+    mlp_sums = list(zip(down_sums, up_sums))
+    t_sums = [t_q_sums + t_k_sums, t_v_sums + t_out_sums]
+    s_sums = [s_q_sums + s_k_sums, s_v_sums]
+    bits = len(down_sums[0].bits)
     bias_swap = Swap(line, lambda _, to: r.bias_src, r.bias_dst, r.bias_sems)
     fetches = [
         pltpu.make_async_copy(r.fetched[name], getattr(r, name), r.fetch_sems.at[i])
@@ -954,25 +1005,25 @@
         cols = pl.ds(pl.multiple_of(i * 128, 128), 128)
         left = r.act[:, :, cols].reshape(all_tokens, 128)
         right = r.g_all[...].reshape(all_tokens, width)
-        mlp_sums[0].part[cols] = mm_tn(left, right).astype(BF16)
+        down_part[cols] = mm_tn(left, right).astype(BF16)
 
     def up_chunk(i):
         cols = pl.ds(pl.multiple_of(i * 256, 256), 256)
         left = r.gathered[streams : 2 * streams, :, :, :, cols].reshape(all_tokens, 256)
         right = r.dpre[...].reshape(all_tokens, hidden)
-        mlp_sums[1].part[cols] = mm_tn(left, right).astype(BF16)
+        up_part[cols] = mm_tn(left, right).astype(BF16)
 
     def t_out_chunk(i):
         left = r.t_mixed[...].reshape(all_tokens, columns)
         right = r.gathered[2 * streams : 3 * streams].reshape(all_tokens, width)
-        t_sums[3].part[...] = mm_tn(left, right).astype(BF16)
+        t_out_part[...] = mm_tn(left, right).astype(BF16)
 
     def t_qkv_chunk(i):
         start = i * 256
         cols = pl.ds(pl.multiple_of(start, 256), 256)
         left = r.gathered[0:streams, :, :, :, cols].reshape(all_tokens, 256)
         for j in range(3):
-            column_grads(start, left, r.t_dproj[j], t_sums[j].part)
+            column_grads(start, left, r.t_dproj[j], t_parts[j])
 
     def s_cols_chunk(_):
         def from_streams(i, carry):
@@ -992,11 +1043,21 @@
         last_part[s] = da.astype(BF16).reshape(last_part.shape[1:])
         for zb in range(chips):
             last_sums.across(s, zb).start()
+        if early:
+
+            @pl.when(s == 1)
+            def _():
+                drain_all(t_line, (sums,), streams)
+
+            @pl.when(s > 0)
+            def _():
+                last_sums.hops(s - 1)
 
     def s_out_chunk(_):
         left = r.s_mixed[...].reshape(all_tokens, columns)
         right = r.gathered[3 * streams : 4 * streams].reshape(all_tokens, width)
-        s_sums[3].part[...] = mm_tn(left, right).astype(BF16)
+        s_out_part[...] = mm_tn(left, right).astype(BF16)
+        s_out_sums[0].send(0)
 
     def bias_chunk(_):
         r.bias_src[...] = jnp.broadcast_to(r.up_bias_grad[...], r.bias_src.shape)
@@ -1020,44 +1081,35 @@
         (mlp_turn, n_down + n_up, 1, bias_chunk),
         (back_turn, 0, 1, t_out_chunk),
         (back_turn, 1, width // 256, t_qkv_chunk),
-        (last_turn, 0, 1, s_cols_chunk),
-        (last_turn, 1, steps, s_back_chunk),
-        (last_turn, 1 + steps, 1, s_out_chunk),
+        (last_turn, 0, 1, s_out_chunk),
+        (last_turn, 1, 1, s_cols_chunk),
+        (last_turn, 2, steps, s_back_chunk),
     )
     slots = [i for i in range(times.every) if i % 2 == 1][:3]
-    per_turn = 2 * len(slots)
+    per_slot = 3
+    per_turn = per_slot * len(slots)
     turns = max(times.turns, last_turn + -(-(steps + 2) // per_turn))
-    stages = reduced[0].stages()
-    bits = len(reduced[0].bits)
+    early = times.y_owner(5 * streams - 1) < last_turn * times.every + slots[1]
 
     def begin_of(turn, number):
         return (turn + number // per_turn) * times.every + times.every - 1
 
-    def moments_of(begin, waits):
-        out = [begin]
-        for k in range(1, stages):
-            half = k if k <= bits else 2 * bits + 1 - k
-            out.append(out[-1] + waits[min(half, len(waits)) - 1])
-        return out
-
-    moments = (
-        (mlp_sums, moments_of(begin_of(mlp_turn, n_down + n_up), MLP_WAITS)),
-        (t_sums, moments_of(begin_of(back_turn, 1 + width // 256), T_WAITS)),
-    )
-    late = [
-        (k, sums_of)
-        for sums_of, steps_of in moments
-        for k, moment in enumerate(steps_of)
-        if moment // times.every >= turns
-    ]
+    begin = begin_of(mlp_turn, n_down + n_up) * SLOT_US
+    plan, free = stage_times(mlp_sums, [begin] * 2, MLP_US, bits, 0.0, FRAME_US, CHUNK_US)
+    begin = begin_of(back_turn, 1 + width // 256) * SLOT_US
+    plan += stage_times(t_sums, [begin] * 2, ATTENTION_US, bits, free, FRAME_US, WHOLE_US)[0]
+    plan = [(t, i, step) for i, (t, _, step) in enumerate(plan)]
+    plan.sort(key=lambda entry: entry[:2])
+    end = turns * times.every * SLOT_US
+    late = [entry for entry in plan if entry[0] >= end]
 
     def beside(m, i):
         if i in slots:
             for turn, first, number, chunk in chunks:
-                which = per_turn * (m - turn) + 2 * slots.index(i) - first
-                here = jnp.clip(number - which, 0, 2)
-
-                @pl.when((which > -2) & (which < number))
+                which = per_turn * (m - turn) + per_slot * slots.index(i) - first
+                here = jnp.clip(number - which, 0, per_slot)
+
+                @pl.when((which > -per_slot) & (which < number))
                 def _():
                     def one(j, carry):
                         @pl.when(which + j >= 0)
@@ -1068,14 +1120,13 @@
 
                     lax.fori_loop(0, here, one, 0)
 
-        for sums_of, steps_of in moments:
-            for k, moment in enumerate(steps_of):
-                if moment % times.every == i and moment // times.every < turns:
-
-                    @pl.when(m == moment // times.every)
-                    def _():
-                        for one in sums_of:
-                            one.stage(k)
+        for t, _, step in plan:
+            moment = int(t / SLOT_US)
+            if t < end and moment % times.every == i:
+
+                @pl.when(m == moment // times.every)
+                def _():
+                    run_step(step)
 
     enter = by_phase((None, enter_temporal, None, None, enter_spatial))
     compute = by_phase(
@@ -1085,11 +1136,8 @@
     pipeline(
         t_line, times, turns, gather, sums, enter, compute, gathered_last, owner, r.total, beside
     )
-    drain_all(t_line, (sums,), streams)
-    for sums_of, group in ((mlp_sums, MLP_RESULTS), (t_sums, T_RESULTS)):
-        if (stages - 1, sums_of) not in late:
-            for name in group:
-                store(name)
+    if not early:
+        drain_all(t_line, (sums,), streams)
 
     y = mm(r.from_parts[...], r.y[...].reshape(tokens, width)).astype(BF16)
     r.y_src[0] = y.astype(r.y_src.dtype).reshape(r.y_src.shape[1:])
@@ -1120,57 +1168,72 @@
         ]
         return jnp.concatenate(rows_of, axis=0)
 
+    first = steps - 1 if early else 0
+    begin = LAST_GRADS * STEP_US + 2.5
+    last_plan = [(max(int((t - end) / STEP_US), 0) + first + 1, i, step) for t, i, step in late]
+    begins = [begin] * len(s_sums) + [begin - 4.0]
+    s_plan, _ = stage_times(
+        s_sums + [s_out_sums], begins, ATTENTION_US, bits, 0.0, LAST_FRAME_US, WHOLE_US
+    )
+    last_plan += [
+        (int(np.ceil(t / STEP_US)), len(plan) + i, step)
+        for t, i, step in s_plan
+        if step[0] == "end" or step[2] > 0
+    ]
+    last_plan.sort(key=lambda entry: entry[:2])
+    bound = steps * (chips - 1) + (chips - 2) * LAG + 1
+    bound = max(bound, LAST_SMALL[-1] + 1)
+
     def body(t, carry):
         last_sums.hops(t)
-        for j in range(3):
-
-            @pl.when(t == j)
-            def _():
+
+        @pl.when(t == LAST_GRADS)
+        def _():
+            for j in range(3):
                 for i in range(width // 256):
                     left = r.normed0[:, :, i * 256 : (i + 1) * 256].reshape(all_tokens, 256)
-                    column_grads(i * 256, left, r.s_dproj[j], s_sums[j].part)
-                s_sums[j].stage(0)
-                if j == 0:
-                    s_sums[3].stage(0)
-                    for k, sums_of in late:
-                        for one in sums_of:
-                            one.stage(k)
-
-        @pl.when((t >= 3) & (t < 3 + steps))
-        def _():
-            small_part(t - 3)
-
-        for k in range(1, stages - 1):
-
-            @pl.when(t == LAST_STAGES[min(k, 3) - 1] + 4 * max(k - 3, 0))
-            def _():
-                for one in s_sums:
-                    one.stage(k)
-
-        @pl.when(t == 3 + steps)
+                    column_grads(i * 256, left, r.s_dproj[j], s_parts[j])
+            for one in s_q_sums + s_k_sums + s_v_sums:
+                one.send(0)
+
+        @pl.when((t > LAST_GRADS) & (t <= LAST_GRADS + steps // 2))
+        def _():
+            def one(i, carry):
+                small_part((t - LAST_GRADS - 1) * 2 + i)
+                return carry
+
+            lax.fori_loop(0, 2, one, 0)
+
+        @pl.when(t == LAST_SMALL[0])
         def _():
             grad = r.grad1[...].reshape(tokens, width)
             own_grad = moved_exactly(r.from_streams[...], grad)
             r.state0[...] = own_grad.reshape(r.state0.shape)
             every.over_pair(small_value(own_grad))
 
-        for moment, step in zip(LAST_SMALL, (every.over_line, every.over_frames, every.over_back)):
+        steps_of = (every.over_line, every.over_frames, every.over_back)
+        for moment, step in zip(LAST_SMALL[1:], steps_of):
 
             @pl.when(t == moment)
             def _():
                 step()
 
+        for moment, _, step in last_plan:
+            if moment < bound:
+
+                @pl.when(t == max(moment, first))
+                def _():
+                    run_step(step)
+
         return carry
 
-    bound = steps * (chips - 1) + (chips - 2) * LAG
-    bound = max(bound, LAST_SMALL[-1] + 1, LAST_STAGES[2] + 4 * max(stages - 5, 0) + 1)
-    lax.fori_loop(0, bound, body, 0)
+    lax.fori_loop(first, bound, body, 0)
     for s in range(steps):
-        last_sums.finish(s, r.last_total.at[s])
+        last_sums.finish(s, last_total.at[s])
     own_grad = r.state0[...].reshape(tokens, width)
     for s in range(steps):
         state = r.x[s, own_rows].astype(F32) + added(s)
-        back, _, _ = norm_back(state, r.last_total[s], r.gain[0:1, :])
+        back, _, _ = norm_back(state, last_total[s], r.gain[0:1, :])
         r.grad_res[pl.ds(s * s_rows, s_rows)] = own_grad[s * s_rows : (s + 1) * s_rows] + back
     y_swap.wait(0)
     r.y_res[...] = mm(r.from_peers[...], r.y_dst[0].reshape(tokens, width).astype(BF16)).astype(BF16)
@@ -1180,15 +1243,12 @@
     for i in range(1, frames):
         up_bias = up_bias + r.bias_dst[0, i]
     r.up_bias_res[...] = up_bias
-    for name in ("grad_res", "y_res", "small_res", "up_bias_res"):
+    for name in ("grad_res", "y_res", "small_res", "up_bias_res") + MLP_RESULTS:
         store(name)
-    for one in s_sums:
-        one.stage(stages - 1)
-    for sums_of, group in ((mlp_sums, MLP_RESULTS), (t_sums, T_RESULTS)):
-        if (stages - 1, sums_of) in late:
-            for name in group:
-                store(name)
-    for name in S_RESULTS:
+    for moment, _, step in last_plan:
+        if moment >= bound:
+            run_step(step)
+    for name in T_RESULTS + S_RESULTS:
         store(name)
     drain_all(line, (last_sums,), steps)
     drain_all(t_line, (gather,), 4 * streams)
@@ -1393,7 +1453,7 @@
         grad1=owned,
         grad2=owned,
         total=(t_rows, width),
-        last_total=(steps, rows, width),
+        **({} if (steps, rows) == (streams, t_rows) else dict(last_total=(steps, rows, width))),
         mask=(count, count),
         small=(8, width),
         sums0=(8 + entries, width),
@@ -1428,8 +1488,9 @@
         y_sems=[pltpu.SemaphoreType.DMA((1, frames))] * 2,
         reduce=[
             x
-            for shape, dim in ((down, 0), (up, 0)) + 2 * (((qkv, 0),) * 3 + ((out, 1),))
-            for x in frame_sum_scratch(frames, shape, dim)
+            for shape, dim, pieces in ((down, 0, 2), (up, 0, 2))
+            + 2 * (((qkv, 0, 1),) * 3 + ((out, 1, 1),))
+            for x in frame_sum_scratch(frames, shape, dim, pieces)
         ],
     )
     held = {k: v for k, v in args.items() if k not in ("ids", "segments")}

time: 224 us -> 218 us (0.973)
  Pallas kernels: 223 us -> 217 us
    pallas_call x1, Pallas kernels: 217 us -> 211 us  [on_device(): pl.pallas_call(lambda *refs: block(fetched, results_of, names, *refs), na...]
where the time goes in v6:
time: 218 us
  Pallas kernels  217 us (100%)
    pallas_call x1, Pallas kernels, on_device(): pl.pallas_call(lambda *refs: block(fetched, results_of, names, *refs), na...  211 us
    pallas_call x1, Pallas kernels, results(): pl.pallas_call(lambda *refs: finish(names, parts, *refs), name='finish',...  6.14 us

profile of v6, /device:TPU:0, one launch (start us, length us, event | category | flops | bytes accessed | tf_op | source)
XLA Modules:
  0.0 217.9 jit_solution(1571147650165145128)
XLA Ops:
  0.7 211.0 %block.1 = (bf16[1024,128]{1,0:T(8,128)(2,1)}, bf16[1024,128]{1,0:T(8,128)(2,1)}, bf16[1024,128]{1,0:T(8,128)(2,1)}, bf16[128,1024]{1,0:T(8,128)(2,1)}, bf16[102...) custom-call(s32[4]{0:T(128)} %refs_0_.1, ...), custom_call_target="tpu_custom_call" | custom-call | tf_op jit(solution)/shard_map/block/pallas_call | solution.py:1502
  211.6 6.1 %finish.1 = (f32[512,1024]{1,0:T(8,128)}, f32[1024,512]{1,0:T(8,128)}, f32[3,1024,128]{2,1,0:T(8,128)}, f32[128,1024]{1,0:T(8,128)}, f32[128,1024]{1,0:T(8,128)}...) custom-call(bf16[1024,128]{1,0:T(8,128)(2,1)} %get-tuple-element.40., ...), custom_call_target="tpu_custom_call" | custom-call | tf_op jit(solution)/shard_map/finish/pallas_call | solution.py:1318

commit v7 on v6

--- a/solution.py
+++ b/solution.py
@@ -21,7 +21,7 @@
 LAG = 2
 SLOT_US, STEP_US, FRAME_US, MLP_US, ATTENTION_US, LAST_FRAME_US = 1.15, 1.45, 4.5, 5.8, 2.9, 3.6
 CHUNK_US, WHOLE_US = 1.45, 100.0
-ADJUST = {}
+ADJUST = {(1, 'hop', (0, 3)): -1.2, (4, 'owner', 0): 0.3}
 LAST_GRADS = 3
 LAST_SMALL = (5, 6, 9, 12)
 HOP_US, SIBLING_US, COMPUTE_US, LINK_US, OWNER_US, SWAP_US = 3.4, 1.0, 2.0, 1.45, 1.0, 4.0
@@ -781,7 +781,7 @@
     shared = not hasattr(r, "g_src")
 
     def g_src_at(part, to):
-        return r.gathered.at[3 * streams + to] if shared else r.g_src.at[part, to]
+        return r.gathered.at[3 * streams + to, part] if shared else r.g_src.at[0, to, part]
 
     g_swap = Swap(line, g_src_at, r.g_dst, r.g_sems)
     state_swap = Swap(line, lambda s, to: r.state_src.at[s, to], r.state_dst, r.state_sems)
@@ -841,10 +841,11 @@
         return carry
 
     lax.fori_loop(0, heads, g_out, 0)
-    g_swap.start(0)
+    for part in range(chips - 1):
+        g_swap.start(part)
 
     def g_in(i):
-        moved = r.g_dst[0, :, i // 2, i % 2].reshape(tokens, width).astype(BF16)
+        moved = r.g_dst[i // 2, :, i % 2].reshape(tokens, width).astype(BF16)
         moved = mm(r.to_parts[...], moved).astype(BF16)
         r.g_all[:, i // 2, i % 2] = moved.reshape(streams, rows, width)
 
@@ -962,6 +963,10 @@
         r.state_src[s] = state.reshape(r.state_src.shape[1:])
         state_swap.start(s)
 
+        @pl.when(s == streams - 1)
+        def _():
+            g_swap.start(chips - 1)
+
     def owner_temporal(s, n):
         state = r.state1[s] + r.total[...] + r.bias[1:2, :]
         r.state2[s] = state
@@ -1064,18 +1069,21 @@
         bias_swap.start(0)
 
     def g_in_chunk(i):
-        @pl.when(i == 0)
-        def _():
-            g_swap.wait(0)
+        @pl.when(i % 2 == 0)
+        def _():
+            g_swap.wait(i // 2)
 
         g_in(i)
 
     n_down, n_up = hidden // 128, width // 256
     turn_of = times.after
+    slots = [i for i in range(times.every) if i % 2 == 1][:3]
+    per_slot = 3
+    per_turn = per_slot * len(slots)
     mlp_turn, back_turn = turn_of(3 * streams - 1), turn_of(4 * streams - 1)
     last_turn = turn_of(5 * streams - 1)
     chunks = (
-        (streams + 1, 0, heads, g_in_chunk),
+        (2 * streams - 1 - heads // per_turn, 0, heads, g_in_chunk),
         (mlp_turn, 0, n_down, down_chunk),
         (mlp_turn, n_down, n_up, up_chunk),
         (mlp_turn, n_down + n_up, 1, bias_chunk),
@@ -1085,9 +1093,6 @@
         (last_turn, 1, 1, s_cols_chunk),
         (last_turn, 2, steps, s_back_chunk),
     )
-    slots = [i for i in range(times.every) if i % 2 == 1][:3]
-    per_slot = 3
-    per_turn = per_slot * len(slots)
     turns = max(times.turns, last_turn + -(-(steps + 2) // per_turn))
     early = times.y_owner(5 * streams - 1) < last_turn * times.every + slots[1]
 
@@ -1417,6 +1422,7 @@
     swapped = (streams, frames, t_rows // frames, width)
     whole = (1, frames, tokens // frames, width)
     g_part = (1, frames, chips, 2, tokens // frames, width)
+    g_into = (chips, frames, 2, tokens // frames, width)
 
     def kind_of(shape):
         return BF16 if shape[-2] % 16 == 0 else F32
@@ -1465,8 +1471,9 @@
     )
     scratch = {name: pltpu.VMEM(shape, BF16) for name, shape in cols.items()}
     scratch |= {name: pltpu.VMEM(shape, F32) for name, shape in floats.items()}
-    moving = ("g_dst",) if g_part[1:] == t_all else ("g_src", "g_dst")
-    scratch |= {name: pltpu.VMEM(g_part, kind_of(g_part)) for name in moving}
+    scratch["g_dst"] = pltpu.VMEM(g_into, kind_of(g_into))
+    if g_part[1:] != t_all:
+        scratch["g_src"] = pltpu.VMEM(g_part, kind_of(g_part))
     scratch |= {name: pltpu.VMEM(whole, kind_of(whole)) for name in ("y_src", "y_dst")}
     every_shape = (room, width)
     scratch |= dict(
@@ -1484,7 +1491,7 @@
         gather_sems=[pltpu.SemaphoreType.DMA((4 * streams, chips))] * 5,
         state_sems=[pltpu.SemaphoreType.DMA((streams, frames))] * 2,
         grad_sems=[pltpu.SemaphoreType.DMA((streams, frames))] * 2,
-        g_sems=[pltpu.SemaphoreType.DMA((1, frames))] * 2,
+        g_sems=[pltpu.SemaphoreType.DMA((chips, frames))] * 2,
         y_sems=[pltpu.SemaphoreType.DMA((1, frames))] * 2,
         reduce=[
             x

time: 218 us -> 214 us (0.982)
  Pallas kernels: 217 us -> 213 us
    pallas_call x1, Pallas kernels: 211 us -> 207 us  [on_device(): pl.pallas_call(lambda *refs: block(fetched, results_of, names, *refs), na...]
where the time goes in v7:
time: 214 us
  Pallas kernels  213 us (100%)
    pallas_call x1, Pallas kernels, on_device(): pl.pallas_call(lambda *refs: block(fetched, results_of, names, *refs), na...  207 us
    pallas_call x1, Pallas kernels, results(): pl.pallas_call(lambda *refs: finish(names, parts, *refs), name='finish',...  6.14 us

profile of v7, /device:TPU:0, one launch (start us, length us, event | category | flops | bytes accessed | tf_op | source)
XLA Modules:
  0.0 214.3 jit_solution(15970919796576042537)
XLA Ops:
  0.7 207.3 %block.1 = (bf16[1024,128]{1,0:T(8,128)(2,1)}, bf16[1024,128]{1,0:T(8,128)(2,1)}, bf16[1024,128]{1,0:T(8,128)(2,1)}, bf16[128,1024]{1,0:T(8,128)(2,1)}, bf16[102...) custom-call(s32[4]{0:T(128)} %refs_0_.1, ...), custom_call_target="tpu_custom_call" | custom-call | tf_op jit(solution)/shard_map/block/pallas_call | solution.py:1509
  208.0 6.1 %finish.1 = (f32[512,1024]{1,0:T(8,128)}, f32[1024,512]{1,0:T(8,128)}, f32[3,1024,128]{2,1,0:T(8,128)}, f32[128,1024]{1,0:T(8,128)}, f32[128,1024]{1,0:T(8,128)}...) custom-call(bf16[1024,128]{1,0:T(8,128)(2,1)} %get-tuple-element.40., ...), custom_call_target="tpu_custom_call" | custom-call | tf_op jit(solution)/shard_map/finish/pallas_call | solution.py:1323

commit v8 on v7

--- a/solution.py
+++ b/solution.py
@@ -841,7 +841,7 @@
         return carry
 
     lax.fori_loop(0, heads, g_out, 0)
-    for part in range(chips - 1):
+    for part in range(chips - 2):
         g_swap.start(part)
 
     def g_in(i):
@@ -963,9 +963,11 @@
         r.state_src[s] = state.reshape(r.state_src.shape[1:])
         state_swap.start(s)
 
-        @pl.when(s == streams - 1)
-        def _():
-            g_swap.start(chips - 1)
+        for part, after in ((chips - 2, streams // 2 - 1), (chips - 1, streams - 1)):
+
+            @pl.when(s == after)
+            def _():
+                g_swap.start(part)
 
     def owner_temporal(s, n):
         state = r.state1[s] + r.total[...] + r.bias[1:2, :]
@@ -1299,10 +1301,10 @@
         return [(name, 0, rows, columns)]
 
     parts = {
+        "t_out": whole("t_out"),
+        "t_qkv": whole("t_q") + whole("t_k") + whole("t_v"),
         "down": whole("down_grad"),
         "up": whole("up_grad"),
-        "t_qkv": whole("t_q") + whole("t_k") + whole("t_v"),
-        "t_out": whole("t_out"),
         "grad": whole("grad_res"),
         "y": whole("y_res"),
         "gain": [("small_res", 0, 3, width)],
@@ -1319,6 +1321,8 @@
         lead = (len(given),) if len(given) > 1 else ()
         kind = BF16 if name == "y" else F32
         shapes.append(jax.ShapeDtypeStruct(lead + (high - low, columns), kind))
+    order = [name for given in parts.values() for name, _, _, _ in given]
+    found = {name: found[name] for name in dict.fromkeys(order)}
     names = tuple(found)
     made = pl.pallas_call(
         lambda *refs: finish(names, parts, *refs),

time: 214 us -> 213 us (level)
  no operation moved by 1% of the time
where the time goes in v8:
time: 213 us
  Pallas kernels  212 us (100%)
    pallas_call x1, Pallas kernels, on_device(): pl.pallas_call(lambda *refs: block(fetched, results_of, names, *refs), na...  207 us
    pallas_call x1, Pallas kernels, results(): pl.pallas_call(lambda *refs: finish(names, parts, *refs), name='finish',...  5.2 us

profile of v8, /device:TPU:0, one launch (start us, length us, event | category | flops | bytes accessed | tf_op | source)
XLA Modules:
  0.0 212.7 jit_solution(2062081274743876828)
XLA Ops:
  0.7 206.7 %block.1 = (bf16[1024,128]{1,0:T(8,128)(2,1)}, bf16[1024,128]{1,0:T(8,128)(2,1)}, bf16[1024,128]{1,0:T(8,128)(2,1)}, bf16[128,1024]{1,0:T(8,128)(2,1)}, bf16[102...) custom-call(s32[4]{0:T(128)} %refs_0_.1, ...), custom_call_target="tpu_custom_call" | custom-call | tf_op jit(solution)/shard_map/block/pallas_call | solution.py:1513
  207.4 5.2 %finish.1 = (f32[128,1024]{1,0:T(8,128)}, f32[3,1024,128]{2,1,0:T(8,128)}, f32[512,1024]{1,0:T(8,128)}, f32[1024,512]{1,0:T(8,128)}, f32[128,1024]{1,0:T(8,128)}...) custom-call(bf16[128,1024]{1,0:T(8,128)(2,1)} %get-tuple-element.40., ...), custom_call_target="tpu_custom_call" | custom-call | tf_op jit(solution)/shard_map/finish/pallas_call | solution.py:1327

commit v9 on v8

--- a/solution.py
+++ b/solution.py
@@ -19,7 +19,7 @@
 VMEM_LIMIT = 62 * 1024 * 1024
 GELU_C = float(np.sqrt(2.0 / np.pi))
 LAG = 2
-SLOT_US, STEP_US, FRAME_US, MLP_US, ATTENTION_US, LAST_FRAME_US = 1.15, 1.45, 4.5, 5.8, 2.9, 3.6
+SLOT_US, STEP_US, FRAME_US, MLP_US, ATTENTION_US, LAST_FRAME_US = 1.15, 1.45, 4.5, 6.4, 3.2, 3.6
 CHUNK_US, WHOLE_US = 1.45, 100.0
 ADJUST = {(1, 'hop', (0, 3)): -1.2, (4, 'owner', 0): 0.3}
 LAST_GRADS = 3

time: 213 us -> 213 us (level)
  no operation moved by 1% of the time
where the time goes in v9:
time: 213 us
  Pallas kernels  212 us (100%)
    pallas_call x1, Pallas kernels, on_device(): pl.pallas_call(lambda *refs: block(fetched, results_of, names, *refs), na...  207 us
    pallas_call x1, Pallas kernels, results(): pl.pallas_call(lambda *refs: finish(names, parts, *refs), name='finish',...  5.2 us

profile of v9, /device:TPU:0, one launch (start us, length us, event | category | flops | bytes accessed | tf_op | source)
XLA Modules:
  0.0 213.2 jit_solution(11930461542166476890)
XLA Ops:
  0.7 207.2 %block.1 = (bf16[1024,128]{1,0:T(8,128)(2,1)}, bf16[1024,128]{1,0:T(8,128)(2,1)}, bf16[1024,128]{1,0:T(8,128)(2,1)}, bf16[128,1024]{1,0:T(8,128)(2,1)}, bf16[102...) custom-call(s32[4]{0:T(128)} %refs_0_.1, ...), custom_call_target="tpu_custom_call" | custom-call | tf_op jit(solution)/shard_map/block/pallas_call | solution.py:1513
  207.8 5.2 %finish.1 = (f32[128,1024]{1,0:T(8,128)}, f32[3,1024,128]{2,1,0:T(8,128)}, f32[512,1024]{1,0:T(8,128)}, f32[1024,512]{1,0:T(8,128)}, f32[128,1024]{1,0:T(8,128)}...) custom-call(bf16[128,1024]{1,0:T(8,128)(2,1)} %get-tuple-element.40., ...), custom_call_target="tpu_custom_call" | custom-call | tf_op jit(solution)/shard_map/finish/pallas_call | solution.py:1327
